TPU v7x, 32 devices: a whole 2x2x4 slice. The times are simulated.
32 devices in a mesh: fsdp: 4 (over z), ctx: 4 (over y, x), tp: 2 (over core).
Axes of the slice: x: 2, y: 2, z: 4, core: 2. Of those that a mesh axis runs over, the one named last changes fastest.
Arguments:
- tokens: bfloat16 [8, 1152, 1536], P('fsdp', 'ctx')
- positions: int32 [8, 1152], P('fsdp', 'ctx'), may hold values from 0 to 3456, as said below
- valid: int32 [8, 1152], P('fsdp', 'ctx'), may hold values from 0 to 1, as said below
- piece_starts: int32 [8, 2], P('fsdp'), may hold values from 0 to 896, as said below
- d_out: bfloat16 [8, 1152, 1536], P('fsdp', 'ctx'), may hold values from -6 to 6
- attn_gain: bfloat16 [2, 1536], P(None, 'fsdp'), may hold values from 0.5 to 1.5
- w_query: bfloat16 [2, 1536, 1536], P(None, 'fsdp', 'tp'), may hold values from -0.15625 to 0.15625
- w_key: bfloat16 [2, 1536, 768], P(None, 'fsdp', 'tp'), may hold values from -0.15625 to 0.15625
- w_value: bfloat16 [2, 1536, 768], P(None, 'fsdp', 'tp'), may hold values from -0.15625 to 0.15625
- w_out: bfloat16 [2, 1536, 1536], P(None, 'tp', 'fsdp'), may hold values from -1.25 to 1.25
- mlp_gain: bfloat16 [2, 1536], P(None, 'fsdp'), may hold values from 0.5 to 1.5
- w_gate: bfloat16 [2, 1536, 4096], P(None, 'fsdp', 'tp'), may hold values from -0.15625 to 0.15625
- w_up: bfloat16 [2, 1536, 4096], P(None, 'fsdp', 'tp'), may hold values from -0.15625 to 0.15625
- w_down: bfloat16 [2, 4096, 1536], P(None, 'tp', 'fsdp'), may hold values from -0.09375 to 0.09375
Outputs:
- output: bfloat16 [8, 1152, 1536], P('fsdp', 'ctx')
- input_grad: float32 [8, 1152, 1536], P('fsdp', 'ctx')
- g_attn_gain: float32 [2, 1536], P(None, 'fsdp')
- g_w_query: float32 [2, 1536, 1536], P(None, 'fsdp', 'tp')
- g_w_key: float32 [2, 1536, 768], P(None, 'fsdp', 'tp')
- g_w_value: float32 [2, 1536, 768], P(None, 'fsdp', 'tp')
- g_w_out: float32 [2, 1536, 1536], P(None, 'tp', 'fsdp')
- g_mlp_gain: float32 [2, 1536], P(None, 'fsdp')
- g_w_gate: float32 [2, 1536, 4096], P(None, 'fsdp', 'tp')
- g_w_up: float32 [2, 1536, 4096], P(None, 'fsdp', 'tp')
- g_w_down: float32 [2, 4096, 1536], P(None, 'tp', 'fsdp')
- rms_stats: float32 [2, 3], replicated
Inputs may be any that keep to these rules, and one draw needn't show every extreme that they name: Each sequence's positions rise by 1 or 2 from token to token and start at most 2305. The first token of every sequence is valid. `piece_starts`: piece k of a sequence starts between k * (576) and (k + 1) * 576 - 256, so that pieces never intersect.
All inputs are finite; a program needn't handle non-finite values.
Results may differ from a plain program's by a relative error of at most 0.033.
Values may be sent and summed in bfloat16 or wider, within the bound.
A program may use at most 320 MiB of HBM per device.

v0:
```python
import jax
import jax.numpy as jnp
from jax import lax
from jax.sharding import PartitionSpec as P

HEADS = 16
KV_HEADS = 8
HEAD_DIM = 96
PIECE_LEN = 256


epsilon = 1e-05
rope_base = 100000.0
neg_big = -1e30


def rope_tables(positions, head_dim):
    half_dim = head_dim // 2
    freqs = rope_base ** (-(jnp.arange(half_dim).astype(jnp.float32) * 2.0 / head_dim))
    angles = positions.astype(jnp.float32)[..., None] * freqs
    return (jnp.cos(angles)[:, :, None, :], jnp.sin(angles)[:, :, None, :])


def rotate(values, cosine, sine_t):
    half_dim = values.shape[-1] // 2
    lead_part = values[..., :half_dim]
    tail_part = values[..., half_dim:]
    return jnp.concatenate(
        [lead_part * cosine - tail_part * sine_t, tail_part * cosine + lead_part * sine_t], axis=-1
    )


def normalize(stream, gain_vec):
    inv_rms = lax.rsqrt(jnp.mean(stream * stream, axis=-1, keepdims=True) + epsilon)
    return stream * inv_rms * gain_vec.astype(jnp.float32)


def norm_back(stream, gain_vec, grad_out):
    inv_rms = lax.rsqrt(jnp.mean(stream * stream, axis=-1, keepdims=True) + epsilon)
    scaled_grad = gain_vec.astype(jnp.float32) * grad_out
    grad_in = inv_rms * scaled_grad - stream * inv_rms**3 * jnp.mean(
        scaled_grad * stream, axis=-1, keepdims=True
    )
    grad_gain = jnp.sum(grad_out * stream * inv_rms, axis=0)
    return (grad_in, grad_gain)


def score_block(query_b, key_heads, allowed, score_scale):
    raw_scores = (
        jnp.einsum("sckgd,snkd->skgcn", query_b, key_heads, preferred_element_type=jnp.float32)
        * score_scale
    )
    return jnp.where(allowed[:, None, None], raw_scores, neg_big)


def local(
    tokens,
    positions,
    valid,
    piece_starts,
    d_out,
    attn_gain,
    w_query,
    w_key,
    w_value,
    w_out,
    mlp_gain,
    w_gate,
    w_up,
    w_down,
):
    seq_count, shard_len, model_width = tokens.shape
    tok_rows = seq_count * shard_len
    tp_count = lax.axis_size("tp")
    local_heads = HEADS // tp_count
    local_kv = KV_HEADS // tp_count
    group_size = HEADS // KV_HEADS
    score_scale = HEAD_DIM ** (-0.5)
    seq_length = shard_len * lax.axis_size("ctx")
    start_tok = lax.axis_index("ctx") * shard_len
    query_index = start_tok + jnp.arange(shard_len, dtype=jnp.int32)
    key_index = jnp.arange(seq_length, dtype=jnp.int32)
    cosine, sine_t = rope_tables(positions, HEAD_DIM)
    valid_flat = valid.astype(jnp.float32).reshape(tok_rows)
    in_query = (query_index[None, None, :] >= piece_starts[:, :, None]) & (
        query_index[None, None, :] < piece_starts[:, :, None] + PIECE_LEN
    )
    in_key = (key_index[None, None, :] >= piece_starts[:, :, None]) & (
        key_index[None, None, :] < piece_starts[:, :, None] + PIECE_LEN
    )
    same_piece = jnp.any(in_query[:, :, :, None] & in_key[:, :, None, :], axis=1)
    causal = key_index[None, :] <= query_index[:, None]
    diagonal = key_index[None, :] == query_index[:, None]
    layer_count = attn_gain.shape[0]
    stream = tokens.astype(jnp.float32).reshape(tok_rows, model_width)
    saved = []
    stat_rows = []
    for layer_no in range(layer_count):
        weights = (
            lax.all_gather(attn_gain[layer_no], "fsdp", axis=0, tiled=True),
            lax.all_gather(w_query[layer_no], "fsdp", axis=0, tiled=True),
            lax.all_gather(w_key[layer_no], "fsdp", axis=0, tiled=True),
            lax.all_gather(w_value[layer_no], "fsdp", axis=0, tiled=True),
            lax.all_gather(w_out[layer_no], "fsdp", axis=1, tiled=True),
            lax.all_gather(mlp_gain[layer_no], "fsdp", axis=0, tiled=True),
            lax.all_gather(w_gate[layer_no], "fsdp", axis=0, tiled=True),
            lax.all_gather(w_up[layer_no], "fsdp", axis=0, tiled=True),
            lax.all_gather(w_down[layer_no], "fsdp", axis=1, tiled=True),
        )
        gain_a, w_q, w_k, w_v, w_o, gain_m, w_g, w_u, w_d = weights
        normed_a = normalize(stream, gain_a).astype(jnp.bfloat16)
        query_heads = jnp.dot(normed_a, w_q, preferred_element_type=jnp.float32).reshape(
            seq_count, shard_len, local_heads, HEAD_DIM
        )
        query_b = (
            rotate(query_heads, cosine, sine_t)
            .astype(jnp.bfloat16)
            .reshape(seq_count, shard_len, local_kv, group_size, HEAD_DIM)
        )
        key_local = jnp.dot(normed_a, w_k, preferred_element_type=jnp.float32).reshape(
            seq_count, shard_len, local_kv, HEAD_DIM
        )
        key_local = (
            rotate(key_local, cosine, sine_t)
            .astype(jnp.bfloat16)
            .reshape(seq_count, shard_len, local_kv * HEAD_DIM)
        )
        value_local = (
            jnp.dot(normed_a, w_v, preferred_element_type=jnp.float32)
            .astype(jnp.bfloat16)
            .reshape(seq_count, shard_len, local_kv * HEAD_DIM)
        )
        key_all, value_all, valid_all = (
            lax.all_gather(key_local, "ctx", axis=1, tiled=True),
            lax.all_gather(value_local, "ctx", axis=1, tiled=True),
            lax.all_gather(valid.astype(jnp.bfloat16), "ctx", axis=1, tiled=True),
        )
        allowed = (causal[None] | same_piece) & ((valid_all[:, None, :] > 0.5) | diagonal[None])
        key_heads = key_all.reshape(seq_count, seq_length, local_kv, HEAD_DIM)
        value_heads = value_all.reshape(seq_count, seq_length, local_kv, HEAD_DIM)
        raw_scores = score_block(query_b, key_heads, allowed, score_scale)
        row_max = jnp.max(raw_scores, axis=-1, keepdims=True)
        log_total = row_max + jnp.log(
            jnp.sum(jnp.exp(raw_scores - row_max), axis=-1, keepdims=True)
        )
        softmax_b = jnp.exp(raw_scores - log_total).astype(jnp.bfloat16)
        mixed_heads = jnp.einsum(
            "skgcn,snkd->sckgd", softmax_b, value_heads, preferred_element_type=jnp.float32
        )
        mixed_b = mixed_heads.astype(jnp.bfloat16).reshape(tok_rows, local_heads * HEAD_DIM)
        attn_branch = lax.psum(
            jnp.dot(mixed_b, w_o, preferred_element_type=jnp.float32).astype(jnp.bfloat16), "tp"
        ).astype(jnp.float32)
        middle = stream + attn_branch
        normed_m = normalize(middle, gain_m).astype(jnp.bfloat16)
        gate_act = jnp.dot(normed_m, w_g, preferred_element_type=jnp.float32)
        up_act = jnp.dot(normed_m, w_u, preferred_element_type=jnp.float32)
        hidden = (jax.nn.silu(gate_act) * up_act).astype(jnp.bfloat16)
        mlp_branch = lax.psum(
            jnp.dot(hidden, w_d, preferred_element_type=jnp.float32).astype(jnp.bfloat16), "tp"
        ).astype(jnp.float32)
        stat_rows.append(
            jnp.stack(
                [
                    jnp.sum(valid_flat[:, None] * stream * stream),
                    jnp.sum(valid_flat[:, None] * attn_branch * attn_branch),
                    jnp.sum(valid_flat[:, None] * mlp_branch * mlp_branch),
                ]
            )
        )
        kept_weights = None
        saved.append(
            (
                stream,
                normed_a,
                query_b,
                key_heads,
                value_heads,
                allowed,
                log_total,
                mixed_b,
                middle,
                normed_m,
                gate_act,
                up_act,
                hidden,
                kept_weights,
            )
        )
        stream = middle + mlp_branch
    output = stream.astype(jnp.bfloat16).reshape(seq_count, shard_len, model_width)
    total_squares, total_count = lax.psum(
        (jnp.stack(stat_rows), jnp.sum(valid_flat)), ("fsdp", "ctx")
    )
    rms_stats = jnp.sqrt(total_squares / (total_count * model_width))
    grad_stream = d_out.astype(jnp.float32).reshape(tok_rows, model_width)
    results = [None] * layer_count
    for layer_no in reversed(range(layer_count)):
        (
            stream_in,
            normed_a,
            query_b,
            key_heads,
            value_heads,
            allowed,
            log_total,
            mixed_b,
            middle,
            normed_m,
            gate_act,
            up_act,
            hidden,
            kept_weights,
        ) = saved[layer_no]
        weights = (
            lax.all_gather(attn_gain[layer_no], "fsdp", axis=0, tiled=True),
            lax.all_gather(w_query[layer_no], "fsdp", axis=0, tiled=True),
            lax.all_gather(w_key[layer_no], "fsdp", axis=0, tiled=True),
            lax.all_gather(w_value[layer_no], "fsdp", axis=0, tiled=True),
            lax.all_gather(w_out[layer_no], "fsdp", axis=1, tiled=True),
            lax.all_gather(mlp_gain[layer_no], "fsdp", axis=0, tiled=True),
            lax.all_gather(w_gate[layer_no], "fsdp", axis=0, tiled=True),
            lax.all_gather(w_up[layer_no], "fsdp", axis=0, tiled=True),
            lax.all_gather(w_down[layer_no], "fsdp", axis=1, tiled=True),
        )
        gain_a, w_q, w_k, w_v, w_o, gain_m, w_g, w_u, w_d = weights
        grad_mlp = grad_stream.astype(jnp.bfloat16)
        grad_hidden = jnp.einsum("rd,fd->rf", grad_mlp, w_d, preferred_element_type=jnp.float32)
        g_down = jnp.einsum("rf,rd->fd", hidden, grad_mlp, preferred_element_type=jnp.float32)
        sigmoid_g = jax.nn.sigmoid(gate_act)
        grad_gate = (
            grad_hidden * up_act * sigmoid_g * (1.0 + gate_act * (1.0 - sigmoid_g))
        ).astype(jnp.bfloat16)
        grad_up = (grad_hidden * gate_act * sigmoid_g).astype(jnp.bfloat16)
        grad_normed_m = lax.psum(
            (
                jnp.einsum("rf,df->rd", grad_gate, w_g, preferred_element_type=jnp.float32)
                + jnp.einsum("rf,df->rd", grad_up, w_u, preferred_element_type=jnp.float32)
            ).astype(jnp.bfloat16),
            "tp",
        ).astype(jnp.float32)
        g_gate = jnp.einsum("rd,rf->df", normed_m, grad_gate, preferred_element_type=jnp.float32)
        g_up = jnp.einsum("rd,rf->df", normed_m, grad_up, preferred_element_type=jnp.float32)
        grad_from_norm, g_gain_m = norm_back(middle, gain_m, grad_normed_m)
        grad_middle = grad_stream + grad_from_norm
        grad_attn = grad_middle.astype(jnp.bfloat16)
        grad_heads = jnp.einsum(
            "rd,hd->rh", grad_attn, w_o, preferred_element_type=jnp.float32
        ).astype(jnp.bfloat16)
        g_out = jnp.einsum("rh,rd->hd", mixed_b, grad_attn, preferred_element_type=jnp.float32)
        grad_heads = grad_heads.reshape(seq_count, shard_len, local_kv, group_size, HEAD_DIM)
        raw_scores = score_block(query_b, key_heads, allowed, score_scale)
        softmax_p = jnp.exp(raw_scores - log_total)
        grad_probs = jnp.einsum(
            "sckgd,snkd->skgcn", grad_heads, value_heads, preferred_element_type=jnp.float32
        )
        row_dots = jnp.sum(softmax_p * grad_probs, axis=-1, keepdims=True)
        grad_scores = (softmax_p * (grad_probs - row_dots)).astype(jnp.bfloat16)
        grad_query = (
            jnp.einsum(
                "skgcn,snkd->sckgd", grad_scores, key_heads, preferred_element_type=jnp.float32
            )
            * score_scale
        )
        grad_key_all = (
            jnp.einsum(
                "skgcn,sckgd->snkd", grad_scores, query_b, preferred_element_type=jnp.float32
            )
            * score_scale
        )
        grad_value_all = jnp.einsum(
            "skgcn,sckgd->snkd",
            softmax_p.astype(jnp.bfloat16),
            grad_heads,
            preferred_element_type=jnp.float32,
        )
        grad_key, grad_value = (
            lax.psum_scatter(
                grad_key_all.reshape(seq_count, seq_length, local_kv * HEAD_DIM).astype(
                    jnp.bfloat16
                ),
                "ctx",
                scatter_dimension=1,
                tiled=True,
            ).astype(jnp.float32),
            lax.psum_scatter(
                grad_value_all.reshape(seq_count, seq_length, local_kv * HEAD_DIM).astype(
                    jnp.bfloat16
                ),
                "ctx",
                scatter_dimension=1,
                tiled=True,
            ).astype(jnp.float32),
        )
        grad_query_b = rotate(
            grad_query.reshape(seq_count, shard_len, local_heads, HEAD_DIM), cosine, -sine_t
        )
        grad_query_b = grad_query_b.astype(jnp.bfloat16).reshape(tok_rows, local_heads * HEAD_DIM)
        grad_key_b = rotate(
            grad_key.reshape(seq_count, shard_len, local_kv, HEAD_DIM), cosine, -sine_t
        )
        grad_key_b = grad_key_b.astype(jnp.bfloat16).reshape(tok_rows, local_kv * HEAD_DIM)
        grad_value_b = grad_value.astype(jnp.bfloat16).reshape(tok_rows, local_kv * HEAD_DIM)
        grad_normed_a = lax.psum(
            (
                jnp.einsum("rh,dh->rd", grad_query_b, w_q, preferred_element_type=jnp.float32)
                + jnp.einsum("rh,dh->rd", grad_key_b, w_k, preferred_element_type=jnp.float32)
                + jnp.einsum("rh,dh->rd", grad_value_b, w_v, preferred_element_type=jnp.float32)
            ).astype(jnp.bfloat16),
            "tp",
        ).astype(jnp.float32)
        g_query = jnp.einsum(
            "rd,rh->dh", normed_a, grad_query_b, preferred_element_type=jnp.float32
        )
        g_key = jnp.einsum("rd,rh->dh", normed_a, grad_key_b, preferred_element_type=jnp.float32)
        g_value = jnp.einsum(
            "rd,rh->dh", normed_a, grad_value_b, preferred_element_type=jnp.float32
        )
        grad_from_attn_norm, g_gain_a = norm_back(stream_in, gain_a, grad_normed_a)
        grad_stream = grad_middle + grad_from_attn_norm
        grad_terms = (g_gain_a, g_query, g_key, g_value, g_out, g_gain_m, g_gate, g_up, g_down)
        shares = (
            lax.psum_scatter(grad_terms[0], ("fsdp", "ctx"), scatter_dimension=0, tiled=True),
            lax.psum_scatter(grad_terms[1], ("fsdp", "ctx"), scatter_dimension=0, tiled=True),
            lax.psum_scatter(grad_terms[2], ("fsdp", "ctx"), scatter_dimension=0, tiled=True),
            lax.psum_scatter(grad_terms[3], ("fsdp", "ctx"), scatter_dimension=0, tiled=True),
            lax.psum_scatter(grad_terms[4], ("fsdp", "ctx"), scatter_dimension=1, tiled=True),
            lax.psum_scatter(grad_terms[5], ("fsdp", "ctx"), scatter_dimension=0, tiled=True),
            lax.psum_scatter(grad_terms[6], ("fsdp", "ctx"), scatter_dimension=0, tiled=True),
            lax.psum_scatter(grad_terms[7], ("fsdp", "ctx"), scatter_dimension=0, tiled=True),
            lax.psum_scatter(grad_terms[8], ("fsdp", "ctx"), scatter_dimension=1, tiled=True),
        )
        results[layer_no] = (
            lax.all_gather(shares[0].astype(jnp.bfloat16), "ctx", axis=0, tiled=True).astype(
                jnp.float32
            ),
            lax.all_gather(shares[1].astype(jnp.bfloat16), "ctx", axis=0, tiled=True).astype(
                jnp.float32
            ),
            lax.all_gather(shares[2].astype(jnp.bfloat16), "ctx", axis=0, tiled=True).astype(
                jnp.float32
            ),
            lax.all_gather(shares[3].astype(jnp.bfloat16), "ctx", axis=0, tiled=True).astype(
                jnp.float32
            ),
            lax.all_gather(shares[4].astype(jnp.bfloat16), "ctx", axis=1, tiled=True).astype(
                jnp.float32
            ),
            lax.all_gather(shares[5].astype(jnp.bfloat16), "ctx", axis=0, tiled=True).astype(
                jnp.float32
            ),
            lax.all_gather(shares[6].astype(jnp.bfloat16), "ctx", axis=0, tiled=True).astype(
                jnp.float32
            ),
            lax.all_gather(shares[7].astype(jnp.bfloat16), "ctx", axis=0, tiled=True).astype(
                jnp.float32
            ),
            lax.all_gather(shares[8].astype(jnp.bfloat16), "ctx", axis=1, tiled=True).astype(
                jnp.float32
            ),
        )
    stacked = [
        jnp.stack([results[layer_no][member] for layer_no in range(layer_count)])
        for member in range(9)
    ]
    input_grad = grad_stream.reshape(seq_count, shard_len, model_width)
    return (
        output,
        input_grad,
        stacked[0],
        stacked[1],
        stacked[2],
        stacked[3],
        stacked[4],
        stacked[5],
        stacked[6],
        stacked[7],
        stacked[8],
        rms_stats,
    )


def solution(mesh):
    in_specs = (
        P("fsdp", "ctx", None),
        P("fsdp", "ctx"),
        P("fsdp", "ctx"),
        P("fsdp", None),
        P("fsdp", "ctx", None),
        P(None, "fsdp"),
        P(None, "fsdp", "tp"),
        P(None, "fsdp", "tp"),
        P(None, "fsdp", "tp"),
        P(None, "tp", "fsdp"),
        P(None, "fsdp"),
        P(None, "fsdp", "tp"),
        P(None, "fsdp", "tp"),
        P(None, "tp", "fsdp"),
    )
    out_specs = (
        P("fsdp", "ctx", None),
        P("fsdp", "ctx", None),
        P(None, "fsdp"),
        P(None, "fsdp", "tp"),
        P(None, "fsdp", "tp"),
        P(None, "fsdp", "tp"),
        P(None, "tp", "fsdp"),
        P(None, "fsdp"),
        P(None, "fsdp", "tp"),
        P(None, "fsdp", "tp"),
        P(None, "tp", "fsdp"),
        P(),
    )
    return jax.shard_map(local, mesh=mesh, in_specs=in_specs, out_specs=out_specs, check_vma=False)
```

profile of v0, /device:TPU:0, one launch (start us, length us, event | category | flops | bytes accessed | tf_op | source)
XLA Modules:
  0.0 4274.7 jit_solution(18125892624954639735)
XLA Ops:
  92.1 34.8 all-gather.68.cloned.1.call-done
  163.4 32.1 all-gather.46.cloned.1.call-done
  279.0 112.1 %all-gather.72.cloned.1.call-done = bf16[1,1536,2048]{2,1,0:T(8,128)(2,1)} async-done(((bf16[1,384,2048]{2,1,0:T(8,128)(2,1)}), bf16[1,1536,2048]{2,1,0:T(8,128)(2,1)}) %all-gather.72.cloned.1.call-update) | async-done | bytes 6291472 | tf_op jit(solution)/shard_map/all_gather | solution.py:106
  400.4 106.5 %all-gather.74.cloned.1.call-done = bf16[1,1536,2048]{2,1,0:T(8,128)(2,1)} async-done(((bf16[1,384,2048]{2,1,0:T(8,128)(2,1)}), bf16[1,1536,2048]{2,1,0:T(8,128)(2,1)}) %all-gather.74.cloned.1.call-update) | async-done | bytes 6291472 | tf_op jit(solution)/shard_map/all_gather | solution.py:107
  518.5 104.1 %all-gather.76.cloned.1.call-done = bf16[1,2048,1536]{2,1,0:T(8,128)(2,1)} async-done(((bf16[1,2048,384]{2,1,0:T(8,128)(2,1)}), bf16[1,2048,1536]{2,1,0:T(8,128)(2,1)}) %all-gather.76.cloned.1.call-update) | async-done | bytes 6291472 | tf_op jit(solution)/shard_map/all_gather | solution.py:108
  654.5 28.9 all-gather.78.cloned.1.call-done
  686.5 28.0 all-gather.80.cloned.1.call-done
  724.4 41.1 all-gather.82.cloned.1.call-done
  801.4 31.6 all-gather.50.cloned.1.call-done
  902.6 97.8 %all-gather.90.cloned.1.call-done = bf16[1,2048,1536]{2,1,0:T(8,128)(2,1)} async-done(((bf16[1,2048,384]{2,1,0:T(8,128)(2,1)}), bf16[1,2048,1536]{2,1,0:T(8,128)(2,1)}) %all-gather.90.cloned.1.call-update) | async-done | bytes 6291472 | tf_op jit(solution)/shard_map/all_gather | solution.py:108
  1027.2 113.2 %all-gather.88.cloned.1.call-done = bf16[1,1536,2048]{2,1,0:T(8,128)(2,1)} async-done(((bf16[1,384,2048]{2,1,0:T(8,128)(2,1)}), bf16[1,1536,2048]{2,1,0:T(8,128)(2,1)}) %all-gather.88.cloned.1.call-update) | async-done | bytes 6291472 | tf_op jit(solution)/shard_map/all_gather | solution.py:107
  1149.6 106.0 %all-gather.86.cloned.1.call-done = bf16[1,1536,2048]{2,1,0:T(8,128)(2,1)} async-done(((bf16[1,384,2048]{2,1,0:T(8,128)(2,1)}), bf16[1,1536,2048]{2,1,0:T(8,128)(2,1)}) %all-gather.86.cloned.1.call-update) | async-done | bytes 6291472 | tf_op jit(solution)/shard_map/all_gather | solution.py:106
  1378.0 34.9 all-reduce.35.cloned.1.call-done
  1418.9 29.3 reduce-scatter.17.cloned.1.call-done
  1731.3 157.8 %reduce-scatter.47.cloned.1.call-done = f32[2048,96]{0,1:T(8,128)} async-done(((f32[2048,1536]{0,1:T(8,128)}), f32[2048,96]{0,1:T(8,128)}) %reduce-scatter.47.cloned.1.call-update) | async-done | bytes 786448 | tf_op jit(solution)/shard_map/reduce_scatter | solution.py:331
  1891.1 208.1 %reduce-scatter.45.cloned.1.call-done = f32[2048,96]{0,1:T(8,128)} async-done(((f32[2048,1536]{0,1:T(8,128)}), f32[2048,96]{0,1:T(8,128)}) %reduce-scatter.45.cloned.1.call-update) | async-done | bytes 786448 | tf_op jit(solution)/shard_map/reduce_scatter | solution.py:331
  2101.2 207.3 %reduce-scatter.39.cloned.1.call-done = f32[96,2048]{1,0:T(8,128)} async-done(((f32[1536,2048]{1,0:T(8,128)}), f32[96,2048]{1,0:T(8,128)}) %reduce-scatter.39.cloned.1.call-update) | async-done | bytes 786448 | tf_op jit(solution)/shard_map/reduce_scatter | solution.py:329
  2310.6 208.3 %reduce-scatter.37.cloned.1.call-done = f32[96,2048]{1,0:T(8,128)} async-done(((f32[1536,2048]{1,0:T(8,128)}), f32[96,2048]{1,0:T(8,128)}) %reduce-scatter.37.cloned.1.call-update) | async-done | bytes 786448 | tf_op jit(solution)/shard_map/reduce_scatter | solution.py:329
  2524.1 127.4 %reduce-scatter.27.cloned.1.call-done = f32[96,384]{1,0:T(8,128)} async-done(((f32[1536,384]{1,0:T(8,128)}), f32[96,384]{1,0:T(8,128)}) %reduce-scatter.27.cloned.1.call-update) | async-done | bytes 147472 | tf_op jit(solution)/shard_map/reduce_scatter | solution.py:325
  2662.5 122.3 %reduce-scatter.31.cloned.1.call-done = f32[96,384]{1,0:T(8,128)} async-done(((f32[1536,384]{1,0:T(8,128)}), f32[96,384]{1,0:T(8,128)}) %reduce-scatter.31.cloned.1.call-update) | async-done | bytes 147472 | tf_op jit(solution)/shard_map/reduce_scatter | solution.py:326
  2795.8 131.0 %reduce-scatter.35.cloned.1.call-done = f32[768,96]{0,1:T(8,128)} async-done(((f32[768,1536]{0,1:T(8,128)}), f32[768,96]{0,1:T(8,128)}) %reduce-scatter.35.cloned.1.call-update) | async-done | bytes 294928 | tf_op jit(solution)/shard_map/reduce_scatter | solution.py:327
  2928.5 140.7 %reduce-scatter.23.cloned.1.call-done = f32[96,768]{1,0:T(8,128)} async-done(((f32[1536,768]{1,0:T(8,128)}), f32[96,768]{1,0:T(8,128)}) %reduce-scatter.23.cloned.1.call-update) | async-done | bytes 294928 | tf_op jit(solution)/shard_map/reduce_scatter | solution.py:324
  3070.8 207.0 %reduce-scatter.43.cloned.1.call-done = f32[96,2048]{1,0:T(8,128)} async-done(((f32[1536,2048]{1,0:T(8,128)}), f32[96,2048]{1,0:T(8,128)}) %reduce-scatter.43.cloned.1.call-update) | async-done | bytes 786448 | tf_op jit(solution)/shard_map/reduce_scatter | solution.py:330
  3304.0 107.5 %reduce-scatter.25.cloned.1.call-done = f32[96,384]{1,0:T(8,128)} async-done(((f32[1536,384]{1,0:T(8,128)}), f32[96,384]{1,0:T(8,128)}) %reduce-scatter.25.cloned.1.call-update) | async-done | bytes 147472 | tf_op jit(solution)/shard_map/reduce_scatter | solution.py:325
  3449.2 80.6 %all-reduce.10 = (bf16[1536]{0:T(1024)(128)(2,1)}, bf16[1536]{0:T(1024)(128)(2,1)}, bf16[1536]{0:T(1024)(128)(2,1)}, bf16[1536]{0:T(1024)(128)(2,1)}, f32[2,3]{1,0:T(2,128)}, /*index=5*/f32[]{:T(128)}) all-reduce(f32[1536]{0:T(1024)} %get-tuple-element.76, ...), channel_id=25, replica_groups=mesh['fsdp'=4,'ctx'=4,'tp'=2] {'fsdp','ctx'}, use_global_device_ids=true, to_apply=%region_30.31.clone | all-reduce | flops 6151 | bytes 36920
  3560.2 89.8 %reduce-scatter.41.cloned.1.call-done = f32[96,2048]{1,0:T(8,128)} async-done(((f32[1536,2048]{1,0:T(8,128)}), f32[96,2048]{1,0:T(8,128)}) %reduce-scatter.41.cloned.1.call-update) | async-done | bytes 786448 | tf_op jit(solution)/shard_map/reduce_scatter | solution.py:330
  3658.1 124.7 %reduce-scatter.29.cloned.1.call-done = f32[96,384]{1,0:T(8,128)} async-done(((f32[1536,384]{1,0:T(8,128)}), f32[96,384]{1,0:T(8,128)}) %reduce-scatter.29.cloned.1.call-update) | async-done | bytes 147472 | tf_op jit(solution)/shard_map/reduce_scatter | solution.py:326
  3795.2 129.9 %reduce-scatter.33.cloned.1.call-done = f32[768,96]{0,1:T(8,128)} async-done(((f32[768,1536]{0,1:T(8,128)}), f32[768,96]{0,1:T(8,128)}) %reduce-scatter.33.cloned.1.call-update) | async-done | bytes 294928 | tf_op jit(solution)/shard_map/reduce_scatter | solution.py:327
  3939.0 127.4 %reduce-scatter.21.cloned.1.call-done = f32[96,768]{1,0:T(8,128)} async-done(((f32[1536,768]{1,0:T(8,128)}), f32[96,768]{1,0:T(8,128)}) %reduce-scatter.21.cloned.1.call-update) | async-done | bytes 294928 | tf_op jit(solution)/shard_map/reduce_scatter | solution.py:324
  4098.5 32.8 all-gather.60.cloned.1.call-done
  4164.2 32.8 all-gather.52.cloned.1.call-done
  4229.9 32.8 all-gather.56.cloned.1.call-done
  (583 shorter events, 1086.6 us)
Async XLA Ops:
  79.5 168.4 %all-gather.70.cloned.1.call-start = ((), (), s32[]{:S(2)}) async-start(), calls=%async_computation.51 | async-start | bytes 2949120 | tf_op jit(solution)/shard_map/all_gather | solution.py:104
  80.7 192.4 %all-reduce.23.cloned.1.call-start = ((), (), s32[]{:S(2)}) async-start(), calls=%async_computation.18 | async-start | bytes 3538944 | tf_op jit(solution)/shard_map/psum | solution.py:151
  254.7 252.2 %all-gather.74.cloned.1.call-start = ((), (), s32[]{:S(2)}) async-start(), calls=%async_computation.53 | async-start | bytes 7864320 | tf_op jit(solution)/shard_map/all_gather | solution.py:107
  258.9 363.7 %all-gather.76.cloned.1.call-start = ((), (), s32[]{:S(2)}) async-start(), calls=%async_computation.54 | async-start | bytes 7864320 | tf_op jit(solution)/shard_map/all_gather | solution.py:108
  261.0 389.3 %all-reduce.25.cloned.1.call-start = ((), (), s32[]{:S(2)}) async-start(), calls=%async_computation.19 | async-start | bytes 3538944 | tf_op jit(solution)/shard_map/psum | solution.py:159
  633.1 165.6 %all-gather.48.cloned.1.call-start = ((), (), s32[]{:S(2)}) async-start(), calls=%async_computation.20 | async-start | bytes 2211840 | tf_op jit(solution)/shard_map/all_gather | solution.py:135
  723.8 276.6 %all-gather.90.cloned.1.call-start = ((), (), s32[]{:S(2)}) async-start(), calls=%async_computation.61 | async-start | bytes 7864320 | tf_op jit(solution)/shard_map/all_gather | solution.py:108
  724.4 297.9 %all-reduce.27.cloned.1.call-start = ((), (), s32[]{:S(2)}) async-start(), calls=%async_computation.22 | async-start | bytes 3538944 | tf_op jit(solution)/shard_map/psum | solution.py:151
  889.2 251.1 %all-gather.88.cloned.1.call-start = ((), (), s32[]{:S(2)}) async-start(), calls=%async_computation.60 | async-start | bytes 7864320 | tf_op jit(solution)/shard_map/all_gather | solution.py:107
  889.8 365.8 %all-gather.86.cloned.1.call-start = ((), (), s32[]{:S(2)}) async-start(), calls=%async_computation.59 | async-start | bytes 7864320 | tf_op jit(solution)/shard_map/all_gather | solution.py:106
  890.6 407.2 %all-reduce.29.cloned.1.call-start = ((), (), s32[]{:S(2)}) async-start(), calls=%async_computation.23 | async-start | bytes 3538944 | tf_op jit(solution)/shard_map/psum | solution.py:235
  1590.0 299.2 %reduce-scatter.47.cloned.1.call-start = ((), (), s32[]{:S(2)}) async-start(), calls=%async_computation.46 | async-start | bytes 13369344 | tf_op jit(solution)/shard_map/reduce_scatter | solution.py:331
  1599.8 499.5 %reduce-scatter.45.cloned.1.call-start = ((), (), s32[]{:S(2)}) async-start(), calls=%async_computation.44 | async-start | bytes 13369344 | tf_op jit(solution)/shard_map/reduce_scatter | solution.py:331
  1611.9 696.7 %reduce-scatter.39.cloned.1.call-start = ((), (), s32[]{:S(2)}) async-start(), calls=%async_computation.38 | async-start | bytes 13369344 | tf_op jit(solution)/shard_map/reduce_scatter | solution.py:329
  1623.0 895.9 %reduce-scatter.37.cloned.1.call-start = ((), (), s32[]{:S(2)}) async-start(), calls=%async_computation.36 | async-start | bytes 13369344 | tf_op jit(solution)/shard_map/reduce_scatter | solution.py:329
  1634.1 1017.4 %reduce-scatter.27.cloned.1.call-start = ((), (), s32[]{:S(2)}) async-start(), calls=%async_computation.31 | async-start | bytes 2506752 | tf_op jit(solution)/shard_map/reduce_scatter | solution.py:325
  1638.5 1146.3 %reduce-scatter.31.cloned.1.call-start = ((), (), s32[]{:S(2)}) async-start(), calls=%async_computation.33 | async-start | bytes 2506752 | tf_op jit(solution)/shard_map/reduce_scatter | solution.py:326
  1643.0 1283.8 %reduce-scatter.35.cloned.1.call-start = ((), (), s32[]{:S(2)}) async-start(), calls=%async_computation.35 | async-start | bytes 5013504 | tf_op jit(solution)/shard_map/reduce_scatter | solution.py:327
  1648.7 1420.5 %reduce-scatter.23.cloned.1.call-start = ((), (), s32[]{:S(2)}) async-start(), calls=%async_computation.29 | async-start | bytes 5013504 | tf_op jit(solution)/shard_map/reduce_scatter | solution.py:324
  1654.6 1623.1 %reduce-scatter.43.cloned.1.call-start = ((), (), s32[]{:S(2)}) async-start(), calls=%async_computation.42 | async-start | bytes 13369344 | tf_op jit(solution)/shard_map/reduce_scatter | solution.py:330
  1665.8 1745.7 %reduce-scatter.25.cloned.1.call-start = ((), (), s32[]{:S(2)}) async-start(), calls=%async_computation.30 | async-start | bytes 2506752 | tf_op jit(solution)/shard_map/reduce_scatter | solution.py:325
  1673.3 1763.5 %all-reduce.39.cloned.1.call-start = ((), (), s32[]{:S(2)}) async-start(), calls=%async_computation.64 | async-start | bytes 7077888 | tf_op jit(solution)/shard_map/psum | solution.py:159
  1703.8 1946.3 %reduce-scatter.41.cloned.1.call-start = ((), (), s32[]{:S(2)}) async-start(), calls=%async_computation.40 | async-start | bytes 13369344 | tf_op jit(solution)/shard_map/reduce_scatter | solution.py:330
  1715.0 2067.8 %reduce-scatter.29.cloned.1.call-start = ((), (), s32[]{:S(2)}) async-start(), calls=%async_computation.32 | async-start | bytes 2506752 | tf_op jit(solution)/shard_map/reduce_scatter | solution.py:326
  1719.5 2205.6 %reduce-scatter.33.cloned.1.call-start = ((), (), s32[]{:S(2)}) async-start(), calls=%async_computation.34 | async-start | bytes 5013504 | tf_op jit(solution)/shard_map/reduce_scatter | solution.py:327
  1725.3 2341.1 %reduce-scatter.21.cloned.1.call-start = ((), (), s32[]{:S(2)}) async-start(), calls=%async_computation.28 | async-start | bytes 5013504 | tf_op jit(solution)/shard_map/reduce_scatter | solution.py:324
  1731.3 2367.2 %all-gather.62.cloned.1.call-start = ((), (), s32[]{:S(2)}) async-start(), calls=%async_computation.47 | async-start | bytes 1966080 | tf_op jit(solution)/shard_map/all_gather | solution.py:358
  1891.1 2240.2 %all-gather.60.cloned.1.call-start = ((), (), s32[]{:S(2)}) async-start(), calls=%async_computation.45 | async-start | bytes 1966080 | tf_op jit(solution)/shard_map/all_gather | solution.py:358
  2101.2 2063.0 %all-gather.54.cloned.1.call-start = ((), (), s32[]{:S(2)}) async-start(), calls=%async_computation.39 | async-start | bytes 1966080 | tf_op jit(solution)/shard_map/all_gather | solution.py:352
  2310.5 1886.5 %all-gather.52.cloned.1.call-start = ((), (), s32[]{:S(2)}) async-start(), calls=%async_computation.37 | async-start | bytes 1966080 | tf_op jit(solution)/shard_map/all_gather | solution.py:352
  2520.8 1709.0 %all-gather.58.cloned.1.call-start = ((), (), s32[]{:S(2)}) async-start(), calls=%async_computation.43 | async-start | bytes 1966080 | tf_op jit(solution)/shard_map/all_gather | solution.py:355
  3279.7 983.0 %all-gather.56.cloned.1.call-start = ((), (), s32[]{:S(2)}) async-start(), calls=%async_computation.41 | async-start | bytes 1966080 | tf_op jit(solution)/shard_map/all_gather | solution.py:355
  (132 other events, 7056.9 us)
Sparse Core Ops, SparseCore 0:
  10.2 33.2 all-gather.63
  77.3 49.5 all-gather.67
  162.9 32.5 all-gather.45
  197.5 50.2 all-gather.69
  274.5 116.5 all-gather.71
  393.3 113.5 all-gather.73
  509.0 113.5 all-gather.75
  651.7 31.6 all-gather.77
  715.9 49.5 all-gather.81
  800.4 32.5 all-gather.49
  834.5 50.2 all-gather.83
  886.2 114.0 all-gather.89
  1023.8 116.5 all-gather.87
  1142.0 113.5 all-gather.85
  1347.5 65.3 all-reduce.34
  1415.8 32.4 reduce-scatter.16
  1578.5 65.3 all-reduce.36
  1646.9 32.4 reduce-scatter.18
  1685.1 204.0 reduce-scatter.46
  1895.6 203.6 reduce-scatter.44
  2104.9 203.6 reduce-scatter.38
  2315.2 203.6 reduce-scatter.36
  2524.2 127.2 reduce-scatter.26
  2657.2 127.5 reduce-scatter.30
  2790.5 136.2 reduce-scatter.34
  2933.2 135.8 reduce-scatter.22
  3074.7 203.0 reduce-scatter.42
  3283.5 127.9 reduce-scatter.24
  3443.4 206.5 reduce-scatter.40
  3655.5 127.1 reduce-scatter.28
  3788.8 136.3 reduce-scatter.32
  3930.7 135.6 reduce-scatter.20
  (17 shorter events, 447.6 us)
where the time goes:
time: 4280 us; the launch traced here: 4270 us
  waiting for transfers between devices  3350 us (78%)
  matrix products  362 us (8%)
  blocking collectives  234 us (5%)
  local copies, waits for them, and re-layouts  153 us (4%)
  other arithmetic  153 us (4%)
    reduce_scatter x2, waiting for transfers between devices, local(): lax.psum_scatter(grad_terms[6], ('fsdp', 'ctx'), scatter_dimension=0, til...  416 us
    reduce_scatter x2, waiting for transfers between devices, local(): lax.psum_scatter(grad_terms[8], ('fsdp', 'ctx'), scatter_dimension=1, til...  366 us
    reduce_scatter x2, waiting for transfers between devices, local(): lax.psum_scatter(grad_terms[7], ('fsdp', 'ctx'), scatter_dimension=0, til...  297 us
    reduce_scatter x2, waiting for transfers between devices, local(): lax.psum_scatter(grad_terms[1], ('fsdp', 'ctx'), scatter_dimension=0, til...  268 us
    reduce_scatter x2, waiting for transfers between devices, local(): lax.psum_scatter(grad_terms[4], ('fsdp', 'ctx'), scatter_dimension=1, til...  261 us
    reduce_scatter x2, waiting for transfers between devices, local(): lax.psum_scatter(grad_terms[3], ('fsdp', 'ctx'), scatter_dimension=0, til...  247 us
    reduce_scatter x2, waiting for transfers between devices, local(): lax.psum_scatter(grad_terms[2], ('fsdp', 'ctx'), scatter_dimension=0, til...  235 us
    all_gather x2, waiting for transfers between devices, local(): lax.all_gather(w_up[layer_no], 'fsdp', axis=0, tiled=True)  220 us
  transfers between devices with their start and end apart: 49, of which 46 were waited for; matrix products, arithmetic and copies ran while one was open for 11% of the time, Pallas kernels for 0%

commit v1 on v0

--- a/solution.py
+++ b/solution.py
@@ -1,7 +1,13 @@
+import functools
+
 import jax
 import jax.numpy as jnp
 from jax import lax
+from jax.experimental import pallas as pl
+from jax.experimental.pallas import tpu as pltpu
 from jax.sharding import PartitionSpec as P
+
+MESH = pl.DeviceIdType.MESH
 
 HEADS = 16
 KV_HEADS = 8
@@ -53,7 +59,7 @@
     return jnp.where(allowed[:, None, None], raw_scores, neg_big)
 
 
-def local(
+def general(
     tokens,
     positions,
     valid,
@@ -380,6 +386,478 @@
     )
 
 
+def partners():
+    me = lax.axis_index("ctx")
+    return me, me ^ 1, me ^ 2, me ^ 3
+
+
+def greet(peers):
+    barrier = pltpu.get_barrier_semaphore()
+    for peer in peers:
+        pl.semaphore_signal(barrier, inc=1, device_id={"ctx": peer}, device_id_type=MESH)
+    pl.semaphore_wait(barrier, len(peers))
+
+
+def send(src, dst, sems, slot, peer):
+    copy = pltpu.make_async_remote_copy(
+        src_ref=src,
+        dst_ref=dst,
+        send_sem=sems[0].at[slot],
+        recv_sem=sems[1].at[slot],
+        device_id={"ctx": peer},
+        device_id_type=MESH,
+    )
+    copy.start()
+    return copy
+
+
+def gather_rows(full, sems, place):
+    me, side_x, side_y, _ = place
+    half = full.shape[1] // 2
+    top, low = pl.ds(0, half), pl.ds(half, half)
+    first = [
+        send(full.at[me, top], full.at[me, top], sems, 0, side_x),
+        send(full.at[me, low], full.at[me, low], sems, 1, side_y),
+    ]
+    rest = [
+        send(full.at[me, top], full.at[me, top], sems, 2, side_y),
+        send(full.at[me, low], full.at[me, low], sems, 3, side_x),
+    ]
+    first[0].wait_recv()
+    rest.append(send(full.at[side_x, top], full.at[side_x, top], sems, 4, side_y))
+    first[1].wait_recv()
+    rest.append(send(full.at[side_y, low], full.at[side_y, low], sems, 5, side_x))
+    for copy in rest:
+        copy.wait()
+    for copy in first:
+        copy.wait_send()
+
+
+def scatter_rows(part, from_x, from_y, passed, last, sems, place):
+    me, side_x, side_y, across = place
+    half = part.shape[1] // 2
+    top, low = pl.ds(0, half), pl.ds(half, half)
+    early = [
+        send(part.at[across, top], from_x.at[1], sems, 0, side_x),
+        send(part.at[across, low], from_y.at[1], sems, 1, side_y),
+    ]
+    rest = [
+        send(part.at[side_x, top], from_x.at[0], sems, 2, side_x),
+        send(part.at[side_y, low], from_y.at[0], sems, 3, side_y),
+    ]
+    step = 16
+
+    def add_to(slot, owner, start, came):
+        @pl.loop(0, half // step)
+        def _(i):
+            rows = pl.ds(pl.multiple_of(i * step, step), step)
+            mine = part[owner, pl.ds(pl.multiple_of(start + i * step, step), step), :]
+            total = mine.astype(jnp.float32) + came[1, rows, :].astype(jnp.float32)
+            passed[slot, rows, :] = total.astype(passed.dtype)
+
+    early[0].wait_recv()
+    add_to(0, side_y, 0, from_x)
+    rest.append(send(passed.at[0], last.at[0], sems, 4, side_y))
+    early[1].wait_recv()
+    add_to(1, side_x, half, from_y)
+    rest.append(send(passed.at[1], last.at[1], sems, 5, side_x))
+    for copy in rest:
+        copy.wait()
+    for copy in early:
+        copy.wait_send()
+
+
+def own_sum(part, from_x, from_y, last, me, side, rows, start, step):
+    came = from_x if side == 0 else from_y
+    total = part[me, pl.ds(pl.multiple_of(start, step), step), :].astype(jnp.float32)
+    total += came[0, rows, :].astype(jnp.float32)
+    return total + last[side, rows, :].astype(jnp.float32)
+
+
+def gather_kernel(x_ref, full_ref, local_sem, send_sems, recv_sems):
+    place = partners()
+    greet(place[1:3])
+    copy = pltpu.make_async_copy(x_ref, full_ref.at[place[0]], local_sem)
+    copy.start()
+    copy.wait()
+    gather_rows(full_ref, (send_sems, recv_sems), place)
+
+
+def forward_kernel(
+    part, stream, gain, valid, middle, full, branch_sq,
+    from_x, from_y, passed, last, send_a, recv_a, send_b, recv_b,
+):
+    place = partners()
+    me = place[0]
+    greet(place[1:3])
+    scatter_rows(part, from_x, from_y, passed, last, (send_a, recv_a), place)
+    half = part.shape[1] // 2
+    step = 16
+    for side in range(2):
+        @pl.loop(0, half // step)
+        def _(i):
+            rows = pl.ds(pl.multiple_of(i * step, step), step)
+            start = side * half + i * step
+            whole_rows = pl.ds(pl.multiple_of(start, step), step)
+            branch = own_sum(part, from_x, from_y, last, me, side, rows, start, step)
+            total = stream[whole_rows, :] + branch
+            middle[whole_rows, :] = total
+            inv_rms = lax.rsqrt(jnp.mean(total * total, axis=-1, keepdims=True) + epsilon)
+            full[me, whole_rows, :] = (total * inv_rms * gain[...]).astype(full.dtype)
+            branch_sq[whole_rows, :] = valid[whole_rows, :] * jnp.sum(
+                branch * branch, axis=-1, keepdims=True
+            )
+    gather_rows(full, (send_b, recv_b), place)
+
+
+def backward_kernel(
+    part, stream, gain, grad, grad_new, full, gain_rows,
+    from_x, from_y, passed, last, send_a, recv_a, send_b, recv_b,
+):
+    place = partners()
+    me = place[0]
+    greet(place[1:3])
+    scatter_rows(part, from_x, from_y, passed, last, (send_a, recv_a), place)
+    half = part.shape[1] // 2
+    step = 16
+    gain_rows[...] = jnp.zeros_like(gain_rows)
+    for side in range(2):
+        @pl.loop(0, half // step)
+        def _(i):
+            rows = pl.ds(pl.multiple_of(i * step, step), step)
+            start = side * half + i * step
+            whole_rows = pl.ds(pl.multiple_of(start, step), step)
+            came = own_sum(part, from_x, from_y, last, me, side, rows, start, step)
+            x = stream[whole_rows, :]
+            inv_rms = lax.rsqrt(jnp.mean(x * x, axis=-1, keepdims=True) + epsilon)
+            scaled = gain[...] * came
+            along = jnp.mean(scaled * x, axis=-1, keepdims=True)
+            total = grad[whole_rows, :] + inv_rms * scaled - x * (inv_rms * inv_rms * inv_rms * along)
+            grad_new[whole_rows, :] = total
+            full[me, whole_rows, :] = total.astype(full.dtype)
+            gain_rows[...] += came * x * inv_rms
+    gather_rows(full, (send_b, recv_b), place)
+
+
+def scatter_kernel(
+    part, out, from_x, from_y, passed, last, send_a, recv_a,
+):
+    place = partners()
+    me = place[0]
+    greet(place[1:3])
+    scatter_rows(part, from_x, from_y, passed, last, (send_a, recv_a), place)
+    half = part.shape[1] // 2
+    step = 16
+    for side in range(2):
+        @pl.loop(0, half // step)
+        def _(i):
+            rows = pl.ds(pl.multiple_of(i * step, step), step)
+            start = side * half + i * step
+            out[pl.ds(pl.multiple_of(start, step), step), :] = own_sum(
+                part, from_x, from_y, last, me, side, rows, start, step
+            )
+
+
+def rs_scratch(rows, width):
+    half = rows // 2
+    return [
+        pltpu.VMEM((2, half, width), jnp.bfloat16),
+        pltpu.VMEM((2, half, width), jnp.bfloat16),
+        pltpu.VMEM((2, half, width), jnp.bfloat16),
+        pltpu.VMEM((2, half, width), jnp.bfloat16),
+    ]
+
+
+def dma_sems(count):
+    return [pltpu.SemaphoreType.DMA((count,)), pltpu.SemaphoreType.DMA((count,))]
+
+
+def linked_call(kernel, number, out_shape, scratch, micros, *args):
+    vmem = pl.BlockSpec(memory_space=pltpu.VMEM)
+    return pl.pallas_call(
+        kernel,
+        out_shape=out_shape,
+        in_specs=[vmem] * len(args),
+        out_specs=jax.tree.map(lambda _: vmem, out_shape),
+        scratch_shapes=scratch,
+        compiler_params=pltpu.CompilerParams(
+            collective_id=number, has_side_effects=True, vmem_limit_bytes=48 << 20
+        ),
+        cost_estimate=pl.CostEstimate(
+            flops=0, bytes_accessed=int(micros * 3.6e6), transcendentals=0
+        ),
+    )(*args)
+
+
+def gather_ctx(x):
+    rows, width = x.shape
+    return linked_call(
+        gather_kernel, 1, jax.ShapeDtypeStruct((4, rows, width), x.dtype),
+        [pltpu.SemaphoreType.DMA] + dma_sems(6), 31, x,
+    )
+
+
+def forward_step(part, stream, gain, valid):
+    rows, width = stream.shape
+    return linked_call(
+        forward_kernel, 2,
+        (
+            jax.ShapeDtypeStruct((rows, width), jnp.float32),
+            jax.ShapeDtypeStruct((4, rows, width), jnp.bfloat16),
+            jax.ShapeDtypeStruct((rows, 1), jnp.float32),
+        ),
+        rs_scratch(rows, width) + dma_sems(6) + dma_sems(6), 65,
+        part, stream, gain, valid,
+    )
+
+
+def backward_step(part, stream, gain, grad):
+    rows, width = stream.shape
+    return linked_call(
+        backward_kernel, 3,
+        (
+            jax.ShapeDtypeStruct((rows, width), jnp.float32),
+            jax.ShapeDtypeStruct((4, rows, width), jnp.bfloat16),
+            jax.ShapeDtypeStruct((16, width), jnp.float32),
+        ),
+        rs_scratch(rows, width) + dma_sems(6) + dma_sems(6), 65,
+        part, stream, gain, grad,
+    )
+
+
+def scatter_ctx(part):
+    _, rows, width = part.shape
+    return linked_call(
+        scatter_kernel, 4, jax.ShapeDtypeStruct((rows, width), jnp.float32),
+        rs_scratch(rows, width) + dma_sems(6), 31, part,
+    )
+
+
+def dot32(a, b, dims):
+    return lax.dot_general(a, b, (dims, ((), ())), preferred_element_type=jnp.float32)
+
+
+def planned(
+    tokens, positions, valid, piece_starts, d_out,
+    attn_gain, w_query, w_key, w_value, w_out, mlp_gain, w_gate, w_up, w_down,
+):
+    seq_count, rows, width = tokens.shape
+    layers = attn_gain.shape[0]
+    ctx_count = lax.axis_size("ctx")
+    tp_count = lax.axis_size("tp")
+    me = lax.axis_index("ctx")
+    side = lax.axis_index("tp")
+    length = rows * ctx_count
+    heads_q = HEADS // tp_count // ctx_count
+    heads_k = KV_HEADS // tp_count // ctx_count
+    group = HEADS // KV_HEADS
+    cols_q = heads_q * HEAD_DIM
+    cols_k = heads_k * HEAD_DIM
+    units = w_gate.shape[2] // ctx_count
+    score_scale = HEAD_DIM ** (-0.5)
+
+    def own(a):
+        return lax.dynamic_index_in_dim(a, side, 0, keepdims=False)
+
+    def cut(w, axis, count):
+        return lax.dynamic_slice_in_dim(w, me * count, count, axis)
+
+    def whole(w):
+        return lax.all_gather(w, ("tp", "fsdp"), axis=0, tiled=True).reshape(
+            tp_count, width, w.shape[1]
+        )
+
+    attn_w, mlp_w = [], []
+    for layer in range(layers):
+        attn_w.append(whole(jnp.concatenate([
+            cut(w_query[layer], 1, cols_q),
+            cut(w_key[layer], 1, cols_k),
+            cut(w_value[layer], 1, cols_k),
+            cut(w_out[layer], 0, cols_q).T,
+        ], axis=1)))
+        mlp_w.append(whole(jnp.concatenate([
+            cut(w_gate[layer], 1, units),
+            cut(w_up[layer], 1, units),
+            cut(w_down[layer], 0, units).T,
+        ], axis=1)))
+    gains = lax.all_gather(
+        jnp.concatenate([attn_gain, mlp_gain], 0), "fsdp", axis=1, tiled=True
+    ).astype(jnp.float32)
+    gain_a = [gains[layer][None] for layer in range(layers)]
+    gain_m = [gains[layers + layer][None] for layer in range(layers)]
+
+    seq_pos, seq_valid = own(positions), own(valid)
+    starts = own(piece_starts)
+    both = lax.all_gather(jnp.stack([seq_pos, seq_valid]), "ctx", axis=1, tiled=True)
+    pos_all, valid_all = both[0], both[1]
+    half_dim = HEAD_DIM // 2
+    freqs = rope_base ** (-(jnp.arange(half_dim).astype(jnp.float32) * 2.0 / HEAD_DIM))
+    angles = pos_all.astype(jnp.float32)[:, None] * freqs
+    cosine, sine_t = jnp.cos(angles)[None], jnp.sin(angles)[None]
+    index = jnp.arange(length, dtype=jnp.int32)
+    inside = (index[None, :] >= starts[:, None]) & (index[None, :] < starts[:, None] + PIECE_LEN)
+    same_piece = jnp.any(inside[:, :, None] & inside[:, None, :], axis=0)
+    causal = index[None, :] <= index[:, None]
+    diagonal = index[None, :] == index[:, None]
+    allowed = (causal | same_piece) & ((valid_all[None, :] > 0) | diagonal)
+
+    valid_f = seq_valid.astype(jnp.float32)[:, None]
+    stream = own(tokens).astype(jnp.float32)
+    grad = own(d_out).astype(jnp.float32)
+    down_grad = gather_ctx(own(d_out)).reshape(length, width)
+    normed = gather_ctx(normalize(stream, gain_a[0]).astype(jnp.bfloat16))
+
+    def heads_of(flat, count):
+        return flat.reshape(length, count, HEAD_DIM).swapaxes(0, 1)
+
+    def flat_of(heads):
+        return heads.swapaxes(0, 1).reshape(length, -1)
+
+    def attn_scores(query, key):
+        raw = jnp.einsum(
+            "kgqd,knd->kgqn", query, key, preferred_element_type=jnp.float32
+        ) * score_scale
+        return jnp.where(allowed, raw, neg_big)
+
+    kv_total = heads_k * tp_count
+    stat_rows = []
+    saved = []
+    branch_out = None
+    for layer in range(layers):
+        normed_a = normed.reshape(length, width)
+        parts = [dot32(normed_a, attn_w[layer][t][:, : cols_q + 2 * cols_k], ((1,), (0,))) for t in range(tp_count)]
+        query = jnp.concatenate([heads_of(p[:, :cols_q], heads_q) for p in parts])
+        key = jnp.concatenate([heads_of(p[:, cols_q : cols_q + cols_k], heads_k) for p in parts])
+        value = jnp.concatenate([heads_of(p[:, cols_q + cols_k :], heads_k) for p in parts])
+        query = rotate(query, cosine, sine_t).astype(jnp.bfloat16).reshape(kv_total, group, length, HEAD_DIM)
+        key = rotate(key, cosine, sine_t).astype(jnp.bfloat16)
+        value = value.astype(jnp.bfloat16)
+        raw = attn_scores(query, key)
+        row_max = jnp.max(raw, axis=-1, keepdims=True)
+        log_total = row_max + jnp.log(jnp.sum(jnp.exp(raw - row_max), axis=-1, keepdims=True))
+        probs = jnp.exp(raw - log_total).astype(jnp.bfloat16)
+        mixed = jnp.einsum("kgqn,knd->kgqd", probs, value, preferred_element_type=jnp.float32)
+        mixed = mixed.astype(jnp.bfloat16).reshape(tp_count, heads_q, length, HEAD_DIM)
+        mixed = [flat_of(mixed[t]) for t in range(tp_count)]
+        part = sum(
+            dot32(mixed[t], attn_w[layer][t][:, cols_q + 2 * cols_k :], ((1,), (1,))) for t in range(tp_count)
+        )
+        middle, normed_m, attn_sq = forward_step(
+            part.astype(jnp.bfloat16).reshape(4, rows, width), stream, gain_m[layer], valid_f
+        )
+        normed_m = normed_m.reshape(length, width)
+        gates = [dot32(normed_m, mlp_w[layer][t][:, :units], ((1,), (0,))) for t in range(tp_count)]
+        ups = [dot32(normed_m, mlp_w[layer][t][:, units : 2 * units], ((1,), (0,))) for t in range(tp_count)]
+        hidden = [(jax.nn.silu(g) * u).astype(jnp.bfloat16) for g, u in zip(gates, ups)]
+        part = sum(dot32(hidden[t], mlp_w[layer][t][:, 2 * units :], ((1,), (1,))) for t in range(tp_count))
+        part = part.astype(jnp.bfloat16).reshape(4, rows, width)
+        saved.append((stream, normed_a, query, key, value, log_total, mixed, middle, normed_m, gates, ups, hidden))
+        stat_rows.append(jnp.sum(valid_f * stream * stream))
+        stat_rows.append(jnp.sum(attn_sq))
+        if layer + 1 < layers:
+            stream, normed, mlp_sq = forward_step(part, middle, gain_a[layer + 1], valid_f)
+            stat_rows.append(jnp.sum(mlp_sq))
+        else:
+            branch_out = scatter_ctx(part)
+            stat_rows.append(jnp.sum(valid_f * branch_out * branch_out))
+            stream = middle + branch_out
+    output = lax.all_gather(stream.astype(jnp.bfloat16), "tp", axis=0)
+    sums = lax.psum(
+        jnp.concatenate([jnp.stack(stat_rows), jnp.sum(valid_f)[None]]), ("fsdp", "ctx", "tp")
+    )
+    rms_stats = jnp.sqrt(sums[:-1] / (sums[-1] * width)).reshape(layers, 3)
+
+    def reduced(g):
+        return lax.psum_scatter(
+            g.astype(jnp.bfloat16).reshape(tp_count * width, -1), ("tp", "fsdp"), scatter_dimension=0, tiled=True
+        )
+
+    results = [None] * layers
+    input_grad = None
+    for layer in reversed(range(layers)):
+        stream_in, normed_a, query, key, value, log_total, mixed, middle, normed_m, gates, ups, hidden = saved[layer]
+        grad_gate, grad_up, part = [], [], 0.0
+        for t in range(tp_count):
+            wt = mlp_w[layer][t]
+            grad_hidden = dot32(down_grad, wt[:, 2 * units :], ((1,), (0,)))
+            sig = jax.nn.sigmoid(gates[t])
+            grad_gate.append((grad_hidden * ups[t] * sig * (1.0 + gates[t] * (1.0 - sig))).astype(jnp.bfloat16))
+            grad_up.append((grad_hidden * gates[t] * sig).astype(jnp.bfloat16))
+            part += dot32(grad_gate[t], wt[:, :units], ((1,), (1,)))
+            part += dot32(grad_up[t], wt[:, units : 2 * units], ((1,), (1,)))
+        g_down = jnp.stack([dot32(down_grad, hidden[t], ((0,), (0,))).astype(jnp.bfloat16) for t in range(tp_count)])
+        g_gate = jnp.stack([dot32(normed_m, grad_gate[t], ((0,), (0,))).astype(jnp.bfloat16) for t in range(tp_count)])
+        g_up = jnp.stack([dot32(normed_m, grad_up[t], ((0,), (0,))).astype(jnp.bfloat16) for t in range(tp_count)])
+        share_mlp = jnp.concatenate([reduced(g_gate), reduced(g_up), reduced(g_down)], axis=1)
+        grad_mid, attn_grad, gm_rows = backward_step(
+            part.astype(jnp.bfloat16).reshape(4, rows, width), middle, gain_m[layer], grad
+        )
+        attn_grad = attn_grad.reshape(length, width)
+        grad_heads = [dot32(attn_grad, attn_w[layer][t][:, cols_q + 2 * cols_k :], ((1,), (0,))).astype(jnp.bfloat16) for t in range(tp_count)]
+        g_out = [dot32(attn_grad, mixed[t], ((0,), (0,))).astype(jnp.bfloat16) for t in range(tp_count)]
+        gh = jnp.concatenate([heads_of(g, heads_q) for g in grad_heads]).reshape(kv_total, group, length, HEAD_DIM)
+        probs = jnp.exp(attn_scores(query, key) - log_total)
+        grad_probs = jnp.einsum("kgqd,knd->kgqn", gh, value, preferred_element_type=jnp.float32)
+        row_dots = jnp.sum(probs * grad_probs, axis=-1, keepdims=True)
+        grad_scores = (probs * (grad_probs - row_dots)).astype(jnp.bfloat16)
+        gq = jnp.einsum("kgqn,knd->kgqd", grad_scores, key, preferred_element_type=jnp.float32) * score_scale
+        gk = jnp.einsum("kgqn,kgqd->knd", grad_scores, query, preferred_element_type=jnp.float32) * score_scale
+        gv = jnp.einsum("kgqn,kgqd->knd", probs.astype(jnp.bfloat16), gh, preferred_element_type=jnp.float32)
+        gq = rotate(gq.reshape(kv_total * group, length, HEAD_DIM), cosine, -sine_t).astype(jnp.bfloat16)
+        gk = rotate(gk, cosine, -sine_t).astype(jnp.bfloat16)
+        gv = gv.astype(jnp.bfloat16)
+        part = 0.0
+        g_attn = []
+        for t in range(tp_count):
+            gqkv = jnp.concatenate([
+                flat_of(gq[t * heads_q : (t + 1) * heads_q]),
+                flat_of(gk[t * heads_k : (t + 1) * heads_k]),
+                flat_of(gv[t * heads_k : (t + 1) * heads_k]),
+            ], axis=1)
+            part += dot32(gqkv, attn_w[layer][t][:, : cols_q + 2 * cols_k], ((1,), (1,)))
+            g_attn.append(dot32(normed_a, gqkv, ((0,), (0,))).astype(jnp.bfloat16))
+        grad, down_grad, ga_rows = backward_step(
+            part.astype(jnp.bfloat16).reshape(4, rows, width), stream_in, gain_a[layer], grad_mid
+        )
+        down_grad = down_grad.reshape(length, width)
+        gain_grads = jnp.stack([jnp.sum(ga_rows, 0), jnp.sum(gm_rows, 0)], axis=1).astype(jnp.bfloat16)
+        g_attn = jnp.stack([jnp.concatenate([g_attn[t], g_out[t], gain_grads if t == 0 else jnp.zeros_like(gain_grads)], axis=1) for t in range(tp_count)])
+        share_attn = reduced(g_attn)
+        results[layer] = (share_attn, share_mlp)
+    input_grad = lax.all_gather(grad, "tp", axis=0)
+
+    outs = [[] for _ in range(9)]
+    for layer in range(layers):
+        share_attn, share_mlp = results[layer]
+        ga = lax.all_gather(share_attn, "ctx", axis=0).astype(jnp.float32)
+        gm = lax.all_gather(share_mlp, "ctx", axis=0).astype(jnp.float32)
+
+        def columns(a):
+            return a.swapaxes(0, 1).reshape(a.shape[1], -1)
+
+        def turned(a):
+            return a.swapaxes(1, 2).reshape(-1, a.shape[1])
+
+        base = cols_q + 2 * cols_k
+        gain_sum = lax.psum(jnp.sum(ga[:, :, base + cols_q :], 0), "tp")
+        outs[0].append(gain_sum[:, 0])
+        outs[1].append(columns(ga[:, :, :cols_q]))
+        outs[2].append(columns(ga[:, :, cols_q : cols_q + cols_k]))
+        outs[3].append(columns(ga[:, :, cols_q + cols_k : base]))
+        outs[4].append(turned(ga[:, :, base : base + cols_q]))
+        outs[5].append(gain_sum[:, 1])
+        outs[6].append(columns(gm[:, :, :units]))
+        outs[7].append(columns(gm[:, :, units : 2 * units]))
+        outs[8].append(turned(gm[:, :, 2 * units :]))
+    stacked = [jnp.stack(o) for o in outs]
+    return (output, input_grad, *stacked, rms_stats)
+
+
+def fits(mesh):
+    tp_count, ctx_count = mesh.shape["tp"], mesh.shape["ctx"]
+    return ctx_count == 4 and tp_count == 2
+
+
 def solution(mesh):
     in_specs = (
         P("fsdp", "ctx", None),
@@ -411,4 +889,4 @@
         P(None, "tp", "fsdp"),
         P(),
     )
-    return jax.shard_map(local, mesh=mesh, in_specs=in_specs, out_specs=out_specs, check_vma=False)
+    return jax.shard_map(planned if fits(mesh) else general, mesh=mesh, in_specs=in_specs, out_specs=out_specs, check_vma=False)

time: 4280 us -> 1680 us (0.39)
  waiting for transfers between devices: 3350 us -> 512 us
  Pallas kernels: 0 us -> 464 us
  blocking collectives: 234 us -> 65.8 us
  matrix products: 362 us -> 299 us
    reduce_scatter x16 -> x6, waiting for transfers between devices: 2120 us -> 418 us  [reduced(): lax.psum_scatter(g.astype(jnp.bfloat16).reshape(tp_count * width, -1), ('...]
    all_gather x24 -> x10, waiting for transfers between devices: 1100 us -> 93.7 us  [the longest x2 52.7 us: planned(): gm = lax.all_gather(share_mlp, 'ctx', axis=0).astype(jnp.float32)]
    pallas_call x0 -> x10, Pallas kernels: none -> 464 us  [linked_call(): pl.pallas_call(kernel, out_shape=out_shape, in_specs=[vmem] * len(args),...]
    all_gather x13 -> x2, blocking collectives: 145 us -> 23.5 us  [the longest x1 13.9 us: planned(): lax.all_gather(jnp.concatenate([attn_gain, mlp_gain], 0), 'fsdp', axis=1,...]
    psum x7 -> x0, waiting for transfers between devices: 92.7 us -> none  [the longest x2 41 us: local(): lax.psum((jnp.einsum('rf,df->rd', grad_gate, w_g, preferred_element_type=...]
    unnamed x2 -> x0, blocking collectives: 89 us -> none
    dot_general x54 -> x72, matrix products: 362 us -> 299 us  [the longest x60 187 us: dot32(): lax.dot_general(a, b, (dims, ((), ())), preferred_element_type=jnp.float32)]
  transfers between devices with their start and end apart: 49 -> 18, of which waited for: 46 -> 10; matrix products, arithmetic and copies ran while one was open for 11% -> 19% of each run, Pallas kernels for 0% -> 18%
where the time goes in v1:
time: 1680 us; the launch traced here: 1670 us
  waiting for transfers between devices  512 us (30%)
  Pallas kernels  464 us (28%)
  matrix products  299 us (18%)
  local copies, waits for them, and re-layouts  176 us (10%)
  other arithmetic  133 us (8%)
  blocking collectives  65.8 us (4%)
  between operations  17.7 us (1%)
    pallas_call x10, Pallas kernels, linked_call(): pl.pallas_call(kernel, out_shape=out_shape, in_specs=[vmem] * len(args),...  464 us
    reduce_scatter x6, waiting for transfers between devices, reduced(): lax.psum_scatter(g.astype(jnp.bfloat16).reshape(tp_count * width, -1), ('...  418 us
    dot_general x60, matrix products, dot32(): lax.dot_general(a, b, (dims, ((), ())), preferred_element_type=jnp.float32)  187 us
    unnamed x352, local copies, waits for them, and re-layouts  83.4 us
    all_gather x2, waiting for transfers between devices, planned(): gm = lax.all_gather(share_mlp, 'ctx', axis=0).astype(jnp.float32)  52.7 us
    all_gather x2, waiting for transfers between devices, planned(): ga = lax.all_gather(share_attn, 'ctx', axis=0).astype(jnp.float32)  41 us
    psum x1, blocking collectives, planned(): lax.psum(jnp.concatenate([jnp.stack(stat_rows), jnp.sum(valid_f)[None]]),...  39.6 us
    convert_element_type x2, other arithmetic, planned(): grad_scores = (probs * (grad_probs - row_dots)).astype(jnp.bfloat16)  37.8 us
  transfers between devices with their start and end apart: 18, of which 10 were waited for; matrix products, arithmetic and copies ran while one was open for 19% of the time, Pallas kernels for 18%

profile of v1, /device:TPU:0, one launch (start us, length us, event | category | flops | bytes accessed | tf_op | source)
XLA Modules:
  0.0 1670.5 jit_solution(5561658040394301554)
XLA Ops:
  36.1 9.6 all-gather.6
  47.0 13.9 all_gather.55
  78.7 27.5 %shard_map.229 = bf16[4,288,1536]{2,1,0:T(8,128)(2,1)S(1)} custom-call(bf16[288,1536]{1,0:T(8,128)(2,1)S(1)} %multiply_convert_fusion.14.x_ref), custom_call_target="tpu_custom_call" | custom-call | bytes 111600000 | tf_op jit(solution)/shard_map/pallas_call | solution.py:577
  108.0 26.6 %shard_map.234 = bf16[4,288,1536]{2,1,0:T(8,128)(2,1)S(1)} custom-call(bf16[288,1536]{1,0:T(8,128)(2,1)S(1)} %get-tuple-element.109.x_ref), custom_call_target="tpu_custom_call" | custom-call | bytes 111600000 | tf_op jit(solution)/shard_map/pallas_call | solution.py:577
  155.8 9.5 exponential_reduce_fusion.1
  166.2 10.7 convolution_convert_fusion.13
  181.0 58.3 %shard_map.230 = (f32[288,1536]{1,0:T(8,128)S(1)}, bf16[4,288,1536]{2,1,0:T(8,128)(2,1)}, f32[288,1]{1,0:T(8,128)S(1)}) custom-call(bf16[4,288,1536]{2,1,0:T(8,128)(2,1)} %bitcast.427, f32[288,1536]{1,0:T(8,128)S(1)} %bitcast_convert_fusion.stream, f32[1,1536]{1,0:T(1,128)S(1)} %get-tuple-element.188.gain, f32[288,1]{1,0:T(8,128)S(1)} %copy-done.12), custom_call_target="tpu_custom_call" | custom-call | bytes 234000000 | tf_op jit(solution)/shard_map/pallas_call | solution.py:577
  262.3 57.4 %shard_map.231 = (f32[288,1536]{1,0:T(8,128)S(1)}, bf16[4,288,1536]{2,1,0:T(8,128)(2,1)}, f32[288,1]{1,0:T(8,128)S(1)}) custom-call(bf16[4,288,1536]{2,1,0:T(8,128)(2,1)} %bitcast.465, f32[288,1536]{1,0:T(8,128)S(1)} %get-tuple-element.33.stream, f32[1,1536]{1,0:T(1,128)S(1)} %get-tuple-element.187.gain, f32[288,1]{1,0:T(8,128)S(1)} %copy-done.13), custom_call_target="tpu_custom_call" | custom-call | bytes 234000000 | tf_op jit(solution)/shard_map/pallas_call | solution.py:577
  329.2 9.1 fusion.168
  348.2 10.5 convolution_convert_fusion.12
  362.9 56.3 %shard_map.232 = (f32[288,1536]{1,0:T(8,128)S(1)}, bf16[4,288,1536]{2,1,0:T(8,128)(2,1)}, f32[288,1]{1,0:T(8,128)S(1)}) custom-call(bf16[4,288,1536]{2,1,0:T(8,128)(2,1)} %bitcast.426, f32[288,1536]{1,0:T(8,128)S(1)} %get-tuple-element.35.stream, f32[1,1536]{1,0:T(1,128)S(1)} %copy-done.28, f32[288,1]{1,0:T(8,128)S(1)} %copy-done.14), custom_call_target="tpu_custom_call" | custom-call | bytes 234000000 | tf_op jit(solution)/shard_map/pallas_call | solution.py:577
  451.4 55.6 %shard_map.235 = (f32[288,1536]{1,0:T(8,128)S(1)}, bf16[4,288,1536]{2,1,0:T(8,128)(2,1)}, f32[16,1536]{1,0:T(8,128)S(1)}) custom-call(bf16[4,288,1536]{2,1,0:T(8,128)(2,1)} %bitcast.459, f32[288,1536]{1,0:T(8,128)S(1)} %get-tuple-element.36.stream, f32[1,1536]{1,0:T(1,128)S(1)} %copy-done.29, f32[288,1536]{1,0:T(8,128)S(1)} %copy-done.4), custom_call_target="tpu_custom_call" | custom-call | bytes 234000000 | tf_op jit(solution)/shard_map/pallas_call | solution.py:577
  526.7 13.1 multiply_reduce_fusion.1
  539.8 18.9 %multiply_convert_fusion.1 = bf16[2,2,1152,1152]{2,3,1,0:T(8,128)(2,1)} fusion(f32[2,2,1152,1152]{2,3,1,0:T(8,128)} %get-tuple-element.207, f32[2,2,1152,1152]{2,3,1,0:T(8,128)} %get-tuple-element.205, f32[2,2,1152]{2,1,0:T(2,128)S(1)} %get-tuple-element.206, f32[2,2,1152]{2,1,0:T(2,128)S(1)} %copy-done.120), kind=kLoop, calls=%fused_computation.6 | loop fusion | flops 21233664 | bytes 53121024 | tf_op jit(solution)/shard_map/convert_element_type | solution.py:802
  585.7 54.9 %shard_map.236 = (f32[288,1536]{1,0:T(8,128)S(1)}, bf16[4,288,1536]{2,1,0:T(8,128)(2,1)}, f32[16,1536]{1,0:T(8,128)S(1)}) custom-call(bf16[4,288,1536]{2,1,0:T(8,128)(2,1)} %bitcast.417, f32[288,1536]{1,0:T(8,128)S(1)} %get-tuple-element.35.stream, f32[1,1536]{1,0:T(1,128)S(1)} %get-tuple-element.187.gain, f32[288,1536]{1,0:T(8,128)S(1)} %get-tuple-element.39.grad), custom_call_target="tpu_custom_call" | custom-call | bytes 234000000 | tf_op jit(solution)/shard_map/pallas_call | solution.py:577
  664.6 54.2 %shard_map.237 = (f32[288,1536]{1,0:T(8,128)S(1)}, bf16[4,288,1536]{2,1,0:T(8,128)(2,1)}, f32[16,1536]{1,0:T(8,128)S(1)}) custom-call(bf16[4,288,1536]{2,1,0:T(8,128)(2,1)} %bitcast.458, f32[288,1536]{1,0:T(8,128)S(1)} %copy-done.3, f32[1,1536]{1,0:T(1,128)S(1)} %get-tuple-element.188.gain, f32[288,1536]{1,0:T(8,128)S(1)} %get-tuple-element.41.grad), custom_call_target="tpu_custom_call" | custom-call | bytes 234000000 | tf_op jit(solution)/shard_map/pallas_call | solution.py:577
  728.3 9.7 fusion.44
  738.0 13.1 multiply_reduce_fusion
  751.1 18.9 %multiply_convert_fusion = bf16[2,2,1152,1152]{2,3,1,0:T(8,128)(2,1)} fusion(f32[2,2,1152,1152]{2,3,1,0:T(8,128)} %get-tuple-element.209, f32[2,2,1152,1152]{2,3,1,0:T(8,128)} %get-tuple-element.199, f32[2,2,1152]{2,1,0:T(2,128)S(1)} %get-tuple-element.208, f32[2,2,1152]{2,1,0:T(2,128)S(1)} %copy-done.118), kind=kLoop, calls=%fused_computation.4 | loop fusion | flops 21233664 | bytes 53121024 | tf_op jit(solution)/shard_map/convert_element_type | solution.py:802
  817.2 53.0 %shard_map.238 = (f32[288,1536]{1,0:T(8,128)S(1)}, bf16[4,288,1536]{2,1,0:T(8,128)(2,1)}, f32[16,1536]{1,0:T(8,128)S(1)}) custom-call(bf16[4,288,1536]{2,1,0:T(8,128)(2,1)} %bitcast.416, f32[288,1536]{1,0:T(8,128)S(1)} %copy-done.1, f32[1,1536]{1,0:T(1,128)S(1)} %copy-done.30, f32[288,1536]{1,0:T(8,128)S(1)} %copy-done.16), custom_call_target="tpu_custom_call" | custom-call | bytes 234000000 | tf_op jit(solution)/shard_map/pallas_call | solution.py:577
  950.6 20.5 %shard_map.233 = f32[288,1536]{1,0:T(8,128)S(1)} custom-call(bf16[4,288,1536]{2,1,0:T(8,128)(2,1)S(1)} %bitcast.411), custom_call_target="tpu_custom_call" | custom-call | bytes 111600000 | tf_op jit(solution)/shard_map/pallas_call | solution.py:577
  978.0 68.5 %reduce-scatter.23.cloned.1.call-done = bf16[384,512]{1,0:T(8,128)(2,1)} async-done(((bf16[3072,512]{1,0:T(8,128)(2,1)}), bf16[384,512]{1,0:T(8,128)(2,1)}) %reduce-scatter.23.cloned.1.call-update) | async-done | bytes 393232 | tf_op jit(solution)/shard_map/reduce_scatter | solution.py:771
  1046.4 70.9 %reduce-scatter.21.cloned.1.call-done = bf16[384,512]{1,0:T(8,128)(2,1)} async-done(((bf16[3072,512]{1,0:T(8,128)(2,1)}), bf16[384,512]{1,0:T(8,128)(2,1)}) %reduce-scatter.21.cloned.1.call-update) | async-done | bytes 393232 | tf_op jit(solution)/shard_map/reduce_scatter | solution.py:771
  1117.3 70.3 %reduce-scatter.19.cloned.1.call-done = bf16[384,512]{1,0:T(8,128)(2,1)} async-done(((bf16[3072,512]{1,0:T(8,128)(2,1)}), bf16[384,512]{1,0:T(8,128)(2,1)}) %reduce-scatter.19.cloned.1.call-update) | async-done | bytes 393232 | tf_op jit(solution)/shard_map/reduce_scatter | solution.py:771
  1190.0 67.8 %reduce-scatter.17.cloned.1.call-done = bf16[384,512]{1,0:T(8,128)(2,1)} async-done(((bf16[3072,512]{1,0:T(8,128)(2,1)}), bf16[384,512]{1,0:T(8,128)(2,1)}) %reduce-scatter.17.cloned.1.call-update) | async-done | bytes 393232 | tf_op jit(solution)/shard_map/reduce_scatter | solution.py:771
  1257.8 70.3 %reduce-scatter.15.cloned.1.call-done = bf16[384,512]{1,0:T(8,128)(2,1)} async-done(((bf16[3072,512]{1,0:T(8,128)(2,1)}), bf16[384,512]{1,0:T(8,128)(2,1)}) %reduce-scatter.15.cloned.1.call-update) | async-done | bytes 393232 | tf_op jit(solution)/shard_map/reduce_scatter | solution.py:771
  1328.1 70.2 %reduce-scatter.13.cloned.1.call-done = bf16[384,512]{1,0:T(8,128)(2,1)} async-done(((bf16[3072,512]{1,0:T(8,128)(2,1)}), bf16[384,512]{1,0:T(8,128)(2,1)}) %reduce-scatter.13.cloned.1.call-update) | async-done | bytes 393232 | tf_op jit(solution)/shard_map/reduce_scatter | solution.py:771
  1407.1 39.6 %psum.23 = f32[7]{0:T(128)S(1)} all-reduce(f32[7]{0:T(128)S(1)} %concatenate.153), channel_id=1, replica_groups=mesh['fsdp'=4,'ctx'=4,'tp'=2] {'fsdp','ctx','tp'}, use_global_device_ids=true, to_apply=%region_31.32 | all-reduce | flops 7 | bytes 56 | tf_op jit(solution)/shard_map/psum | solution.py:765
  1448.6 13.7 all-gather.32.cloned.1.call-done
  1470.1 27.2 %all-gather.30.cloned.1.call-done = bf16[1536,578]{0,1:T(8,128)(2,1)} async-done(((bf16[384,578]{0,1:T(8,128)(2,1)}), bf16[1536,578]{0,1:T(8,128)(2,1)}) %all-gather.30.cloned.1.call-update) | async-done | bytes 1775632 | tf_op jit(solution)/shard_map/all_gather | solution.py:832
  1532.6 24.1 %all-gather.36.cloned.1.call-done = bf16[1536,1536]{1,0:T(8,128)(2,1)} async-done(((bf16[384,1536]{1,0:T(8,128)(2,1)}), bf16[1536,1536]{1,0:T(8,128)(2,1)}) %all-gather.36.cloned.1.call-update) | async-done | bytes 4718608 | tf_op jit(solution)/shard_map/all_gather | solution.py:833
  1586.9 28.6 %all-gather.34.cloned.1.call-done = bf16[1536,1536]{1,0:T(8,128)(2,1)} async-done(((bf16[384,1536]{1,0:T(8,128)(2,1)}), bf16[1536,1536]{1,0:T(8,128)(2,1)}) %all-gather.34.cloned.1.call-update) | async-done | bytes 4718608 | tf_op jit(solution)/shard_map/all_gather | solution.py:833
  (609 shorter events, 500.3 us)
Async XLA Ops:
  7.2 131.4 %all-gather.18.cloned.1.call-start = ((), (), s32[]{:S(2)}) async-start(), calls=%async_computation.8 | async-start | bytes 3981312 | tf_op jit(solution)/shard_map/all_gather | solution.py:666
  18.1 221.8 %all-gather.20.cloned.1.call-start = ((), (), s32[]{:S(2)}) async-start(), calls=%async_computation.9 | async-start | bytes 10616832 | tf_op jit(solution)/shard_map/all_gather | solution.py:666
  25.5 294.9 %all-gather.22.cloned.1.call-start = ((), (), s32[]{:S(2)}) async-start(), calls=%async_computation.10 | async-start | bytes 3981312 | tf_op jit(solution)/shard_map/all_gather | solution.py:666
  28.8 391.1 %all-gather.24.cloned.1.call-start = ((), (), s32[]{:S(2)}) async-start(), calls=%async_computation.11 | async-start | bytes 10616832 | tf_op jit(solution)/shard_map/all_gather | solution.py:666
  30.9 30.6 %copy-start.136 = (s32[2,2]{1,0:T(2,128)S(1)}, s32[2,2]{1,0:T(2,128)}, u32[]{:S(2)}) copy-start(s32[2,2]{1,0:T(2,128)} %param.17) | copy-start | bytes 52
  30.9 31.1 %copy-start.56 = (bf16[2,288,1536]{2,1,0:T(8,128)(2,1)S(1)}, bf16[2,288,1536]{2,1,0:T(8,128)(2,1)}, u32[]{:S(2)}) copy-start(bf16[2,288,1536]{2,1,0:T(8,128)(2,1)} %param.14) | copy-start | bytes 5308420
  34.2 939.6 %reduce-scatter.27.cloned.1.call-start = ((), (), s32[]{:S(2)}) async-start(), calls=%async_computation.25 | async-start | bytes 4423680
  62.3 118.8 %copy-start = (f32[288,1536]{1,0:T(8,128)}, f32[288,1536]{1,0:T(8,128)S(1)}, u32[]{:S(2)}) copy-start(f32[288,1536]{1,0:T(8,128)S(1)} %bitcast_convert_fusion.stream) | copy-start | bytes 5308420
  108.0 29.1 %copy-start.126 = (f32[1152]{0:T(1024)S(1)}, f32[1152]{0:T(1024)}, u32[]{:S(2)}) copy-start(f32[1152]{0:T(1024)} %fusion.133) | copy-start | bytes 13828
  108.0 29.1 %copy-start.135 = (f32[48]{0:T(128)S(1)}, f32[48]{0:T(128)}, u32[]{:S(2)}) copy-start(f32[48]{0:T(128)} %negate_power_fusion) | copy-start | bytes 580
  240.0 22.4 %copy-start.2 = (f32[288,1536]{1,0:T(8,128)}, f32[288,1536]{1,0:T(8,128)S(1)}, u32[]{:S(2)}) copy-start(f32[288,1536]{1,0:T(8,128)S(1)} %get-tuple-element.33.stream) | copy-start | bytes 5308420
  451.4 55.7 %copy-start.46 = (bf16[1,2,1152,96]{2,3,1,0:T(8,128)(2,1)S(1)}, bf16[1,2,1152,96]{2,3,1,0:T(8,128)(2,1)}, u32[]{:S(2)}) copy-start(bf16[1,2,1152,96]{2,3,1,0:T(8,128)(2,1)} %copy-done.45) | copy-start | bytes 1327108
  585.7 61.8 %slice-start.2 = ((s8[9437184]{0:T(1024)(128)(4,1)}), s8[1048576]{0:T(1024)(128)(4,1)S(1)}, s32[]{:S(2)}) async-start(s8[9437184]{0:T(1024)(128)(4,1)} %bitcast.489), calls=%async_computation.28 | async-start | bytes 2097152
  664.6 54.2 %copy-start.53 = (bf16[1,2,1152,96]{2,3,1,0:T(8,128)(2,1)S(1)}, bf16[1,2,1152,96]{2,3,1,0:T(8,128)(2,1)}, u32[]{:S(2)}) copy-start(bf16[1,2,1152,96]{2,3,1,0:T(8,128)(2,1)} %copy-done.52) | copy-start | bytes 1327108
  751.1 18.9 %copy-start.91 = (bf16[4,1152,48]{1,2,0:T(8,128)(2,1)S(1)}, bf16[4,1152,48]{1,2,0:T(8,128)(2,1)}, u32[]{:S(2)}) copy-start(bf16[4,1152,48]{1,2,0:T(8,128)(2,1)} %copy-done.90) | copy-start | bytes 1327108
  806.7 169.2 %reduce-scatter.25.cloned.1.call-start = ((), (), s32[]{:S(2)}) async-start(), calls=%async_computation.24 | async-start | bytes 4423680
  887.7 158.7 %reduce-scatter.23.cloned.1.call-start = ((), (), s32[]{:S(2)}) async-start(), calls=%async_computation.17 | async-start | bytes 3538944 | tf_op jit(solution)/shard_map/reduce_scatter | solution.py:771
  896.8 220.6 %reduce-scatter.21.cloned.1.call-start = ((), (), s32[]{:S(2)}) async-start(), calls=%async_computation.16 | async-start | bytes 3538944 | tf_op jit(solution)/shard_map/reduce_scatter | solution.py:771
  906.1 281.5 %reduce-scatter.19.cloned.1.call-start = ((), (), s32[]{:S(2)}) async-start(), calls=%async_computation.15 | async-start | bytes 3538944 | tf_op jit(solution)/shard_map/reduce_scatter | solution.py:771
  915.4 342.4 %reduce-scatter.17.cloned.1.call-start = ((), (), s32[]{:S(2)}) async-start(), calls=%async_computation.14 | async-start | bytes 3538944 | tf_op jit(solution)/shard_map/reduce_scatter | solution.py:771
  924.5 403.6 %reduce-scatter.15.cloned.1.call-start = ((), (), s32[]{:S(2)}) async-start(), calls=%async_computation.13 | async-start | bytes 3538944 | tf_op jit(solution)/shard_map/reduce_scatter | solution.py:771
  933.7 464.6 %reduce-scatter.13.cloned.1.call-start = ((), (), s32[]{:S(2)}) async-start(), calls=%async_computation.12 | async-start | bytes 3538944 | tf_op jit(solution)/shard_map/reduce_scatter | solution.py:771
  943.1 505.5 %all-gather.26.cloned.1.call-start = ((), (), s32[]{:S(2)}) async-start(), calls=%async_computation.18 | async-start | bytes 2654208 | tf_op jit(solution)/shard_map/all_gather | solution.py:764
  950.5 20.5 %copy-start.128 = (f32[288]{0:T(512)S(1)}, f32[288]{0:T(512)}, u32[]{:S(2)}) copy-start(f32[288]{0:T(512)} %get-tuple-element.105) | copy-start | bytes 3460
  973.2 475.5 %all-gather.28.cloned.1.call-start = ((), (), s32[]{:S(2)}) async-start(), calls=%async_computation.19 | async-start | bytes 5308416 | tf_op jit(solution)/shard_map/all_gather | solution.py:827
  973.8 488.6 %all-gather.32.cloned.1.call-start = ((), (), s32[]{:S(2)}) async-start(), calls=%async_computation.21 | async-start | bytes 2242560 | tf_op jit(solution)/shard_map/all_gather | solution.py:832
  975.8 521.5 %all-gather.30.cloned.1.call-start = ((), (), s32[]{:S(2)}) async-start(), calls=%async_computation.20 | async-start | bytes 2242560 | tf_op jit(solution)/shard_map/all_gather | solution.py:832
  977.9 578.8 %all-gather.36.cloned.1.call-start = ((), (), s32[]{:S(2)}) async-start(), calls=%async_computation.23 | async-start | bytes 5898240 | tf_op jit(solution)/shard_map/all_gather | solution.py:833
  1190.0 210.7 %copy-start.19 = (f32[288,1]{1,0:T(8,128)S(1)}, f32[288,1]{1,0:T(8,128)}, u32[]{:S(2)}) copy-start(f32[288,1]{1,0:T(8,128)} %copy-done.18) | copy-start | bytes 3460
  1190.0 211.3 %copy-start.21 = (f32[288,1]{1,0:T(8,128)S(1)}, f32[288,1]{1,0:T(8,128)}, u32[]{:S(2)}) copy-start(f32[288,1]{1,0:T(8,128)} %copy-done.20) | copy-start | bytes 3460
  1190.0 212.0 %copy-start.23 = (f32[288,1]{1,0:T(8,128)S(1)}, f32[288,1]{1,0:T(8,128)}, u32[]{:S(2)}) copy-start(f32[288,1]{1,0:T(8,128)} %copy-done.22) | copy-start | bytes 3460
  1190.0 425.5 %all-gather.34.cloned.1.call-start = ((), (), s32[]{:S(2)}) async-start(), calls=%async_computation.22 | async-start | bytes 5898240 | tf_op jit(solution)/shard_map/all_gather | solution.py:833
  (153 other events, 770.6 us)
Sparse Core Ops, SparseCore 0:
  18.3 44.4 all-gather.17
  64.9 89.5 all-gather.19
  156.2 40.1 all-gather.21
  198.4 89.5 all-gather.23
  806.9 82.7 reduce-scatter.26
  892.4 82.8 reduce-scatter.24
  978.1 68.2 reduce-scatter.22
  1049.3 67.9 reduce-scatter.20
  1119.6 67.9 reduce-scatter.18
  1189.8 67.9 reduce-scatter.16
  1260.1 67.9 reduce-scatter.14
  1330.3 67.9 reduce-scatter.12
  1400.4 9.3 all-gather.25
  1411.8 13.8 all-gather.27
  1428.0 34.3 all-gather.31
  1464.6 32.6 all-gather.29
  1499.6 57.0 all-gather.35
  1558.4 57.0 all-gather.33

commit v2 on v1

--- a/solution.py
+++ b/solution.py
@@ -391,59 +391,67 @@
     return me, me ^ 1, me ^ 2, me ^ 3
 
 
-def greet(peers):
+def greet(*places):
     barrier = pltpu.get_barrier_semaphore()
-    for peer in peers:
-        pl.semaphore_signal(barrier, inc=1, device_id={"ctx": peer}, device_id_type=MESH)
-    pl.semaphore_wait(barrier, len(peers))
-
-
-def send(src, dst, sems, slot, peer):
+    for place in places:
+        pl.semaphore_signal(barrier, inc=1, device_id=place, device_id_type=MESH)
+    pl.semaphore_wait(barrier, len(places))
+
+
+def send(src, dst, sems, slot, place):
     copy = pltpu.make_async_remote_copy(
         src_ref=src,
         dst_ref=dst,
         send_sem=sems[0].at[slot],
         recv_sem=sems[1].at[slot],
-        device_id={"ctx": peer},
+        device_id=place,
         device_id_type=MESH,
     )
     copy.start()
     return copy
 
 
-def gather_rows(full, sems, place):
+def nothing():
+    pass
+
+
+def gather_rows(full, sems, place, work=(nothing, nothing)):
     me, side_x, side_y, _ = place
+    to_x, to_y = {"ctx": side_x}, {"ctx": side_y}
     half = full.shape[1] // 2
     top, low = pl.ds(0, half), pl.ds(half, half)
     first = [
-        send(full.at[me, top], full.at[me, top], sems, 0, side_x),
-        send(full.at[me, low], full.at[me, low], sems, 1, side_y),
+        send(full.at[me, top], full.at[me, top], sems, 0, to_x),
+        send(full.at[me, low], full.at[me, low], sems, 1, to_y),
     ]
     rest = [
-        send(full.at[me, top], full.at[me, top], sems, 2, side_y),
-        send(full.at[me, low], full.at[me, low], sems, 3, side_x),
+        send(full.at[me, top], full.at[me, top], sems, 2, to_y),
+        send(full.at[me, low], full.at[me, low], sems, 3, to_x),
     ]
+    work[0]()
     first[0].wait_recv()
-    rest.append(send(full.at[side_x, top], full.at[side_x, top], sems, 4, side_y))
+    rest.append(send(full.at[side_x, top], full.at[side_x, top], sems, 4, to_y))
     first[1].wait_recv()
-    rest.append(send(full.at[side_y, low], full.at[side_y, low], sems, 5, side_x))
+    rest.append(send(full.at[side_y, low], full.at[side_y, low], sems, 5, to_x))
+    work[1]()
     for copy in rest:
         copy.wait()
     for copy in first:
         copy.wait_send()
 
 
-def scatter_rows(part, from_x, from_y, passed, last, sems, place):
+def scatter_rows(part, from_x, from_y, passed, last, sems, place, work=(nothing, nothing)):
     me, side_x, side_y, across = place
+    to_x, to_y = {"ctx": side_x}, {"ctx": side_y}
     half = part.shape[1] // 2
     top, low = pl.ds(0, half), pl.ds(half, half)
     early = [
-        send(part.at[across, top], from_x.at[1], sems, 0, side_x),
-        send(part.at[across, low], from_y.at[1], sems, 1, side_y),
+        send(part.at[across, top], from_x.at[1], sems, 0, to_x),
+        send(part.at[across, low], from_y.at[1], sems, 1, to_y),
     ]
     rest = [
-        send(part.at[side_x, top], from_x.at[0], sems, 2, side_x),
-        send(part.at[side_y, low], from_y.at[0], sems, 3, side_y),
+        send(part.at[side_x, top], from_x.at[0], sems, 2, to_x),
+        send(part.at[side_y, low], from_y.at[0], sems, 3, to_y),
     ]
     step = 16
 
@@ -455,12 +463,14 @@
             total = mine.astype(jnp.float32) + came[1, rows, :].astype(jnp.float32)
             passed[slot, rows, :] = total.astype(passed.dtype)
 
+    work[0]()
     early[0].wait_recv()
     add_to(0, side_y, 0, from_x)
-    rest.append(send(passed.at[0], last.at[0], sems, 4, side_y))
+    rest.append(send(passed.at[0], last.at[0], sems, 4, to_y))
     early[1].wait_recv()
     add_to(1, side_x, half, from_y)
-    rest.append(send(passed.at[1], last.at[1], sems, 5, side_x))
+    rest.append(send(passed.at[1], last.at[1], sems, 5, to_x))
+    work[1]()
     for copy in rest:
         copy.wait()
     for copy in early:
@@ -476,7 +486,7 @@
 
 def gather_kernel(x_ref, full_ref, local_sem, send_sems, recv_sems):
     place = partners()
-    greet(place[1:3])
+    greet({"ctx": place[1]}, {"ctx": place[2]})
     copy = pltpu.make_async_copy(x_ref, full_ref.at[place[0]], local_sem)
     copy.start()
     copy.wait()
@@ -489,7 +499,7 @@
 ):
     place = partners()
     me = place[0]
-    greet(place[1:3])
+    greet({"ctx": place[1]}, {"ctx": place[2]})
     scatter_rows(part, from_x, from_y, passed, last, (send_a, recv_a), place)
     half = part.shape[1] // 2
     step = 16
@@ -510,52 +520,211 @@
     gather_rows(full, (send_b, recv_b), place)
 
 
-def backward_kernel(
-    part, stream, gain, grad, grad_new, full, gain_rows,
-    from_x, from_y, passed, last, send_a, recv_a, send_b, recv_b,
+def backward_kernel(plan, *refs):
+    refs = list(refs)
+
+    def take(count):
+        taken = refs[:count]
+        del refs[:count]
+        return taken
+
+    count = len(plan.sizes)
+    part, stream, gain, grad = take(4)
+    other_rows = take(1)[0] if plan.attn else None
+    left_in = take(2)
+    right_in = [take(n) for n in plan.pieces]
+    grad_new = take(1)[0]
+    full = None if plan.last else take(1)[0]
+    gain_rows = take(1)[0]
+    summed = take(1)[0]
+    from_x, from_y, passed, last = take(4)
+    left = take(2)
+    right, sent, came = take(count), take(count), take(count)
+    gain_sent, gain_came = take(2) if plan.attn else (None, None)
+    send_a, recv_a, send_b, recv_b, send_c, recv_c, local_sems = refs
+
+    place = partners()
+    me = place[0]
+    side = lax.axis_index("tp")
+    sibling = {"tp": 1 - side}
+    greet({"ctx": place[1]}, {"ctx": place[2]}, sibling)
+    loads = []
+    for p in range(2):
+        loads.append([pltpu.make_async_copy(left_in[p], left[p], local_sems.at[p])])
+    for p in range(count):
+        if plan.pieces[p] == 1:
+            loads.append([pltpu.make_async_copy(right_in[p][0], right[p], local_sems.at[2 + 2 * p])])
+            continue
+        loads.append([
+            pltpu.make_async_copy(right_in[p][t], right[p].at[t], local_sems.at[2 + 2 * p + t]) for t in range(2)
+        ])
+    for group in loads:
+        for load in group:
+            load.start()
+    starts = [sum(plan.sizes[:p]) for p in range(count)]
+    block = 256
+    width = stream.shape[1]
+    copies = []
+
+    def product(p, t, dst, start):
+        @pl.loop(0, width // block)
+        def _(i):
+            cols = pl.ds(pl.multiple_of(i * block, block), block)
+            dst[cols, start : start + plan.sizes[p]] = dot32(
+                left[plan.lefts[p]][:, cols], right[p][t], ((0,), (0,))
+            ).astype(jnp.bfloat16)
+
+    def theirs(p):
+        product(p, 1 - side, sent[p], 0)
+        copies.append(send(sent[p], came[p], (send_c, recv_c), p, sibling))
+
+    def ours(p):
+        product(p, side, summed, starts[p])
+
+    def add_up():
+        for p in range(count):
+            copies[p].wait_recv()
+            step = 64
+
+            @pl.loop(0, width // step)
+            def _(i):
+                rows = pl.ds(pl.multiple_of(i * step, step), step)
+                cols = slice(starts[p], starts[p] + plan.sizes[p])
+                total = summed[rows, cols].astype(jnp.float32) + came[p][rows, :].astype(jnp.float32)
+                summed[rows, cols] = total.astype(jnp.bfloat16)
+
+    def work(slot):
+        def run():
+            if slot == 0:
+                for group in loads:
+                    for load in group:
+                        load.wait()
+            for whose, p in plan.slots[slot]:
+                (theirs if whose else ours)(p)
+        return run
+
+    scatter_rows(part, from_x, from_y, passed, last, (send_a, recv_a), place, (work(0), work(1)))
+    half = part.shape[1] // 2
+    step = 16
+    gain_rows[...] = jnp.zeros_like(gain_rows)
+    for part_no in range(2):
+        @pl.loop(0, half // step)
+        def _(i):
+            rows = pl.ds(pl.multiple_of(i * step, step), step)
+            start = part_no * half + i * step
+            whole_rows = pl.ds(pl.multiple_of(start, step), step)
+            got = own_sum(part, from_x, from_y, last, me, part_no, rows, start, step)
+            x = stream[whole_rows, :]
+            inv_rms = lax.rsqrt(jnp.mean(x * x, axis=-1, keepdims=True) + epsilon)
+            scaled = gain[...] * got
+            along = jnp.mean(scaled * x, axis=-1, keepdims=True)
+            total = grad[whole_rows, :] + inv_rms * scaled - x * (inv_rms * inv_rms * inv_rms * along)
+            if plan.last:
+                grad_new[side, whole_rows, :] = total
+            else:
+                grad_new[whole_rows, :] = total
+                full[me, whole_rows, :] = total.astype(full.dtype)
+            gain_rows[...] += got * x * inv_rms
+    if plan.last:
+        copies.append(send(grad_new.at[side], grad_new.at[side], (send_c, recv_c), count + 1, sibling))
+    if plan.attn:
+        gain_sent[...] = jnp.zeros_like(gain_sent)
+        gain_sent[0:1, :] = jnp.sum(gain_rows[...], axis=0, keepdims=True)
+        gain_sent[1:2, :] = jnp.sum(other_rows[...], axis=0, keepdims=True)
+        copies.append(send(gain_sent, gain_came, (send_c, recv_c), count, sibling))
+    if plan.last:
+        work(2)()
+        work(3)()
+        add_up()
+    else:
+        def finish():
+            work(3)()
+            add_up()
+
+        gather_rows(full, (send_b, recv_b), place, (work(2), finish))
+    for copy in copies[count:]:
+        copy.wait_recv()
+    if plan.attn:
+        both = gain_sent[...] + gain_came[...]
+        spread = jnp.concatenate([both, jnp.zeros((120, width), jnp.float32)], axis=0).T
+        total = sum(plan.sizes)
+        summed[:, total : total + 64] = spread[:, :64].astype(jnp.bfloat16)
+    for copy in copies:
+        copy.wait_send()
+
+
+class Stage:
+    def __init__(self, sizes, pieces, lefts, slots, attn, last):
+        self.sizes, self.pieces, self.lefts, self.slots = sizes, pieces, lefts, slots
+        self.attn, self.last = attn, last
+
+
+def start_kernel(gains, places, all_gains, all_places, local_sems, send_a, recv_a, send_b, recv_b):
+    groups = (
+        ("fsdp", gains, all_gains, (send_a, recv_a)),
+        ("ctx", places, all_places, (send_b, recv_b)),
+    )
+    peers = []
+    for axis, _, _, _ in groups:
+        count = lax.axis_size(axis)
+        peers.append([lax.rem(lax.axis_index(axis) + step, count) for step in range(1, count)])
+    greet(*[{groups[n][0]: peer} for n in range(2) for peer in peers[n]])
+    copies = []
+    for n, (axis, src, dst, sems) in enumerate(groups):
+        me = lax.axis_index(axis)
+        for step, peer in enumerate(peers[n]):
+            copies.append(send(src, dst.at[me], sems, step, {axis: peer}))
+        mine = pltpu.make_async_copy(src, dst.at[me], local_sems.at[n])
+        mine.start()
+        mine.wait()
+    for copy in copies:
+        copy.wait()
+
+
+def end_kernel(
+    part, middle, valid, stats, out, all_stats,
+    from_x, from_y, passed, last, sums, stat_sent, stat_came, z_came, send_a, recv_a, send_c, recv_c, send_d, recv_d,
 ):
     place = partners()
     me = place[0]
-    greet(place[1:3])
+    side = lax.axis_index("tp")
+    depth = lax.axis_size("fsdp")
+    level = lax.axis_index("fsdp")
+    sibling = {"tp": 1 - side}
+    others = [{"fsdp": lax.rem(level + step, depth)} for step in range(1, depth)]
+    greet({"ctx": place[1]}, {"ctx": place[2]}, sibling, *others)
     scatter_rows(part, from_x, from_y, passed, last, (send_a, recv_a), place)
     half = part.shape[1] // 2
     step = 16
-    gain_rows[...] = jnp.zeros_like(gain_rows)
-    for side in range(2):
+    sums[...] = jnp.zeros_like(sums)
+    for part_no in range(2):
         @pl.loop(0, half // step)
         def _(i):
             rows = pl.ds(pl.multiple_of(i * step, step), step)
-            start = side * half + i * step
+            start = part_no * half + i * step
             whole_rows = pl.ds(pl.multiple_of(start, step), step)
-            came = own_sum(part, from_x, from_y, last, me, side, rows, start, step)
-            x = stream[whole_rows, :]
-            inv_rms = lax.rsqrt(jnp.mean(x * x, axis=-1, keepdims=True) + epsilon)
-            scaled = gain[...] * came
-            along = jnp.mean(scaled * x, axis=-1, keepdims=True)
-            total = grad[whole_rows, :] + inv_rms * scaled - x * (inv_rms * inv_rms * inv_rms * along)
-            grad_new[whole_rows, :] = total
-            full[me, whole_rows, :] = total.astype(full.dtype)
-            gain_rows[...] += came * x * inv_rms
-    gather_rows(full, (send_b, recv_b), place)
-
-
-def scatter_kernel(
-    part, out, from_x, from_y, passed, last, send_a, recv_a,
-):
-    place = partners()
-    me = place[0]
-    greet(place[1:3])
-    scatter_rows(part, from_x, from_y, passed, last, (send_a, recv_a), place)
-    half = part.shape[1] // 2
-    step = 16
-    for side in range(2):
-        @pl.loop(0, half // step)
-        def _(i):
-            rows = pl.ds(pl.multiple_of(i * step, step), step)
-            start = side * half + i * step
-            out[pl.ds(pl.multiple_of(start, step), step), :] = own_sum(
-                part, from_x, from_y, last, me, side, rows, start, step
-            )
+            branch = own_sum(part, from_x, from_y, last, me, part_no, rows, start, step)
+            out[side, whole_rows, :] = (middle[whole_rows, :] + branch).astype(out.dtype)
+            sums[...] += valid[whole_rows, :] * jnp.sum(branch * branch, axis=-1, keepdims=True)
+    handed = send(out.at[side], out.at[side], (send_c, recv_c), 0, sibling)
+    total = jnp.sum(sums[...], axis=0, keepdims=True)
+    lane = lax.broadcasted_iota(jnp.int32, (8, 128), 1)
+    held = stats[...] + jnp.where(lane == 5, total, 0.0)
+    for n, peer in enumerate((sibling, {"ctx": place[1]}, {"ctx": place[2]})):
+        stat_sent[n] = held
+        send(stat_sent.at[n], stat_came.at[n], (send_d, recv_d), n, peer).wait()
+        held = held + stat_came[n]
+    z_came[level] = held
+    copies = [
+        send(z_came.at[level], z_came.at[level], (send_d, recv_d), 3 + n, peer) for n, peer in enumerate(others)
+    ]
+    for copy in copies:
+        copy.wait()
+    held = z_came[0]
+    for n in range(1, depth):
+        held = held + z_came[n]
+    all_stats[...] = held
+    handed.wait()
 
 
 def rs_scratch(rows, width):
@@ -572,28 +741,29 @@
     return [pltpu.SemaphoreType.DMA((count,)), pltpu.SemaphoreType.DMA((count,))]
 
 
-def linked_call(kernel, number, out_shape, scratch, micros, *args):
+def linked_call(kernel, number, out_shape, scratch, micros, args, far=()):
     vmem = pl.BlockSpec(memory_space=pltpu.VMEM)
+    hbm = pl.BlockSpec(memory_space=pl.ANY)
     return pl.pallas_call(
         kernel,
         out_shape=out_shape,
-        in_specs=[vmem] * len(args),
+        in_specs=[vmem] * len(args) + [hbm] * len(far),
         out_specs=jax.tree.map(lambda _: vmem, out_shape),
         scratch_shapes=scratch,
         compiler_params=pltpu.CompilerParams(
-            collective_id=number, has_side_effects=True, vmem_limit_bytes=48 << 20
+            collective_id=number, has_side_effects=True, vmem_limit_bytes=60 << 20
         ),
         cost_estimate=pl.CostEstimate(
             flops=0, bytes_accessed=int(micros * 3.6e6), transcendentals=0
         ),
-    )(*args)
+    )(*args, *far)
 
 
 def gather_ctx(x):
     rows, width = x.shape
     return linked_call(
         gather_kernel, 1, jax.ShapeDtypeStruct((4, rows, width), x.dtype),
-        [pltpu.SemaphoreType.DMA] + dma_sems(6), 31, x,
+        [pltpu.SemaphoreType.DMA] + dma_sems(6), 31, [x],
     )
 
 
@@ -607,34 +777,238 @@
             jax.ShapeDtypeStruct((rows, 1), jnp.float32),
         ),
         rs_scratch(rows, width) + dma_sems(6) + dma_sems(6), 65,
-        part, stream, gain, valid,
-    )
-
-
-def backward_step(part, stream, gain, grad):
+        [part, stream, gain, valid],
+    )
+
+
+def backward_step(number, part, stream, gain, grad, lefts, rights, pairs, slots, other_rows=None, last=False):
     rows, width = stream.shape
+    length = lefts[0].shape[0]
+    sizes = [r[0].shape[-1] for r in rights]
+    pieces = [len(r) for r in rights]
+    attn = other_rows is not None
+    total = sum(sizes) + (64 if attn else 0)
+    bf16, f32 = jnp.bfloat16, jnp.float32
+    outs = [jax.ShapeDtypeStruct(((2,) if last else ()) + (rows, width), f32)]
+    if not last:
+        outs.append(jax.ShapeDtypeStruct((4, rows, width), bf16))
+    outs += [jax.ShapeDtypeStruct((16, width), f32), jax.ShapeDtypeStruct((width, total), bf16)]
+    scratch = rs_scratch(rows, width)
+    scratch += [pltpu.VMEM((length, width), bf16)] * 2
+    scratch += [pltpu.VMEM((2, length, n), bf16) for n in sizes]
+    scratch += [pltpu.VMEM((width, n), bf16) for n in sizes] * 2
+    if attn:
+        scratch += [pltpu.VMEM((8, width), f32)] * 2
+    scratch += dma_sems(6) + dma_sems(6) + dma_sems(len(sizes) + 2)
+    scratch += [pltpu.SemaphoreType.DMA((2 + 2 * len(sizes),))]
     return linked_call(
-        backward_kernel, 3,
+        functools.partial(backward_kernel, Stage(sizes, pieces, pairs, slots, attn, last)),
+        number, outs, scratch, 35 if last else 65,
+        [part, stream, gain, grad] + ([other_rows] if attn else []),
+        list(lefts) + [half for r in rights for half in r],
+    )
+
+
+def end_step(part, middle, valid, stats):
+    rows, width = middle.shape
+    depth = lax.axis_size("fsdp")
+    f32 = jnp.float32
+    return linked_call(
+        end_kernel, 4,
+        (jax.ShapeDtypeStruct((2, rows, width), jnp.bfloat16), jax.ShapeDtypeStruct((8, 128), f32)),
+        rs_scratch(rows, width)
+        + [pltpu.VMEM((16, 1), f32), pltpu.VMEM((3, 8, 128), f32), pltpu.VMEM((3, 8, 128), f32)]
+        + [pltpu.VMEM((depth, 8, 128), f32)]
+        + dma_sems(6) + dma_sems(1) + dma_sems(3 + depth),
+        31, [part, middle, valid, stats],
+    )
+
+
+def start_step(gains, places):
+    depth, across = lax.axis_size("fsdp"), lax.axis_size("ctx")
+    return linked_call(
+        start_kernel, 8,
         (
-            jax.ShapeDtypeStruct((rows, width), jnp.float32),
-            jax.ShapeDtypeStruct((4, rows, width), jnp.bfloat16),
-            jax.ShapeDtypeStruct((16, width), jnp.float32),
+            jax.ShapeDtypeStruct((depth, *gains.shape), gains.dtype),
+            jax.ShapeDtypeStruct((across, *places.shape), places.dtype),
         ),
-        rs_scratch(rows, width) + dma_sems(6) + dma_sems(6), 65,
-        part, stream, gain, grad,
-    )
-
-
-def scatter_ctx(part):
-    _, rows, width = part.shape
-    return linked_call(
-        scatter_kernel, 4, jax.ShapeDtypeStruct((rows, width), jnp.float32),
-        rs_scratch(rows, width) + dma_sems(6), 31, part,
+        [pltpu.SemaphoreType.DMA((2,))] + dma_sems(depth) + dma_sems(across),
+        5, [gains, places],
     )
 
 
 def dot32(a, b, dims):
     return lax.dot_general(a, b, (dims, ((), ())), preferred_element_type=jnp.float32)
+
+
+QUERIES = 128
+ROWS = 384
+LOG2E = 1.4426950408889634
+
+
+def turn(x, cos_row, sin_row):
+    half_dim = HEAD_DIM // 2
+    swapped = jnp.concatenate([x[:, half_dim:], x[:, :half_dim]], axis=1)
+    return x * cos_row + swapped * sin_row
+
+
+def block_groups(length):
+    count = length // QUERIES
+    per = 3 if count % 3 == 0 else 1
+    groups = []
+    for first in range(0, count, per):
+        seen = min(length, (first + per) * QUERIES + PIECE_LEN)
+        groups.append((first, per, seen))
+    return groups
+
+
+def attend_kernel(normed, weights, cos_ref, sin_ref, bias, part, query, key, value, lse, mixed):
+    length = normed.shape[0]
+    pairs = weights.shape[0]
+    cols_q = 2 * HEAD_DIM
+    base = 4 * HEAD_DIM
+    blocks = ROWS // QUERIES
+
+    @pl.loop(0, length // ROWS)
+    def _(i):
+        rows = pl.ds(pl.multiple_of(i * ROWS, ROWS), ROWS)
+        cos_b, sin_b = cos_ref[rows, :], sin_ref[rows, :]
+        for t in range(pairs):
+            flat = dot32(normed[rows, :], weights[t, :, :base], ((1,), (0,)))
+            for g in range(2):
+                head = turn(flat[:, g * HEAD_DIM : (g + 1) * HEAD_DIM], cos_b, sin_b).astype(jnp.bfloat16)
+                for n in range(blocks):
+                    query[t, i * blocks + n, g * QUERIES : (g + 1) * QUERIES, :] = head[n * QUERIES : (n + 1) * QUERIES]
+            key[t, rows, :] = turn(flat[:, cols_q : cols_q + HEAD_DIM], cos_b, sin_b).astype(jnp.bfloat16)
+            value[t, rows, :] = flat[:, cols_q + HEAD_DIM : base].astype(jnp.bfloat16)
+
+    factor = HEAD_DIM ** (-0.5) * LOG2E
+    for first, count, seen in block_groups(length):
+        @pl.loop(0, pairs * count)
+        def _(n):
+            t = n // count
+            block = first + n % count
+            rows = pl.ds(pl.multiple_of(block * QUERIES, QUERIES), QUERIES)
+            raw = dot32(key[t, :seen, :], query[t, block], ((1,), (1,)))
+            low = bias[:seen, rows].astype(jnp.float32)
+            raw = raw * factor + jnp.concatenate([low, low], axis=1)
+            top = jnp.max(raw, axis=0, keepdims=True)
+            probs = jnp.exp2(raw - top)
+            total = jnp.sum(probs, axis=0, keepdims=True)
+            out = dot32(value[t, :seen, :], probs.astype(jnp.bfloat16), ((0,), (0,)))
+            out = (out * (1.0 / total)).T.astype(jnp.bfloat16)
+            lse[t, block] = top + jnp.log2(total)
+            for g in range(2):
+                mixed[t, rows, g * HEAD_DIM : (g + 1) * HEAD_DIM] = out[g * QUERIES : (g + 1) * QUERIES]
+
+    @pl.loop(0, length // ROWS)
+    def _(i):
+        rows = pl.ds(pl.multiple_of(i * ROWS, ROWS), ROWS)
+        total = dot32(mixed[0, rows, :], weights[0, :, base:], ((1,), (1,)))
+        for t in range(1, pairs):
+            total += dot32(mixed[t, rows, :], weights[t, :, base:], ((1,), (1,)))
+        part[rows, :] = total.astype(jnp.bfloat16)
+
+
+def attend_back_kernel(grad, weights, cos_ref, sin_ref, bias, query, key, value, lse, part, grad_qkv, heads, g_key, g_value):
+    length = grad.shape[0]
+    pairs = weights.shape[0]
+    cols_q = 2 * HEAD_DIM
+    base = 4 * HEAD_DIM
+    blocks = ROWS // QUERIES
+    scale = HEAD_DIM ** (-0.5)
+    factor = scale * LOG2E
+
+    @pl.loop(0, length // ROWS)
+    def _(i):
+        rows = pl.ds(pl.multiple_of(i * ROWS, ROWS), ROWS)
+        for t in range(pairs):
+            flat = dot32(grad[rows, :], weights[t, :, base:], ((1,), (0,))).astype(jnp.bfloat16)
+            for g in range(2):
+                for n in range(blocks):
+                    heads[t, i * blocks + n, g * QUERIES : (g + 1) * QUERIES, :] = flat[
+                        n * QUERIES : (n + 1) * QUERIES, g * HEAD_DIM : (g + 1) * HEAD_DIM
+                    ]
+    g_key[...] = jnp.zeros_like(g_key)
+    g_value[...] = jnp.zeros_like(g_value)
+    for first, count, seen in block_groups(length):
+        @pl.loop(0, pairs * count)
+        def _(n):
+            t = n // count
+            block = first + n % count
+            rows = pl.ds(pl.multiple_of(block * QUERIES, QUERIES), QUERIES)
+            low = bias[:seen, rows].astype(jnp.float32)
+            raw = dot32(key[t, :seen, :], query[t, block], ((1,), (1,)))
+            probs = jnp.exp2(raw * factor + jnp.concatenate([low, low], axis=1) - lse[t, block])
+            g_probs = dot32(value[t, :seen, :], heads[t, block], ((1,), (1,)))
+            weighed = probs * g_probs
+            along = jnp.sum(weighed, axis=0, keepdims=True)
+            g_scores = (weighed - probs * along).astype(jnp.bfloat16)
+            g_value[t, :seen, :] += dot32(probs.astype(jnp.bfloat16), heads[t, block], ((1,), (0,)))
+            g_key[t, :seen, :] += dot32(g_scores, query[t, block], ((1,), (0,)))
+            g_query = dot32(key[t, :seen, :], g_scores, ((0,), (0,))).T * scale
+            cos_b, sin_b = cos_ref[rows, :], sin_ref[rows, :]
+            for g in range(2):
+                grad_qkv[t, rows, g * HEAD_DIM : (g + 1) * HEAD_DIM] = turn(
+                    g_query[g * QUERIES : (g + 1) * QUERIES], cos_b, -sin_b
+                ).astype(jnp.bfloat16)
+
+    @pl.loop(0, length // ROWS)
+    def _(i):
+        rows = pl.ds(pl.multiple_of(i * ROWS, ROWS), ROWS)
+        cos_b, sin_b = cos_ref[rows, :], sin_ref[rows, :]
+        total = 0.0
+        for t in range(pairs):
+            grad_qkv[t, rows, cols_q : cols_q + HEAD_DIM] = turn(g_key[t, rows, :] * scale, cos_b, -sin_b).astype(jnp.bfloat16)
+            grad_qkv[t, rows, cols_q + HEAD_DIM : base] = g_value[t, rows, :].astype(jnp.bfloat16)
+            total += dot32(grad_qkv[t, rows, :], weights[t, :, :base], ((1,), (1,)))
+        part[rows, :] = total.astype(jnp.bfloat16)
+
+
+def local_call(kernel, out_shape, scratch, micros, *args):
+    vmem = pl.BlockSpec(memory_space=pltpu.VMEM)
+    return pl.pallas_call(
+        kernel,
+        out_shape=out_shape,
+        in_specs=[vmem] * len(args),
+        out_specs=jax.tree.map(lambda _: vmem, out_shape),
+        scratch_shapes=scratch,
+        compiler_params=pltpu.CompilerParams(vmem_limit_bytes=60 << 20),
+        cost_estimate=pl.CostEstimate(flops=0, bytes_accessed=int(micros * 3.6e6), transcendentals=0),
+    )(*args)
+
+
+def attend(normed, weights, cosine, sine_t, bias):
+    length, width = normed.shape
+    pairs = weights.shape[0]
+    blocks = length // QUERIES
+    bf16 = jnp.bfloat16
+    shape = jax.ShapeDtypeStruct
+    outs = [
+        shape((length, width), bf16),
+        shape((pairs, blocks, 2 * QUERIES, HEAD_DIM), bf16),
+        shape((pairs, length, HEAD_DIM), bf16),
+        shape((pairs, length, HEAD_DIM), bf16),
+        shape((pairs, blocks, 1, 2 * QUERIES), jnp.float32),
+        shape((pairs, length, 2 * HEAD_DIM), bf16),
+    ]
+    return local_call(attend_kernel, outs, [], 20, normed, weights, cosine, sine_t, bias)
+
+
+def attend_back(grad, weights, cosine, sine_t, bias, query, key, value, lse):
+    length, width = grad.shape
+    pairs = weights.shape[0]
+    bf16 = jnp.bfloat16
+    shape = jax.ShapeDtypeStruct
+    outs = [shape((length, width), bf16), shape((pairs, length, 4 * HEAD_DIM), bf16)]
+    scratch = [
+        pltpu.VMEM(query.shape, bf16),
+        pltpu.VMEM(key.shape, jnp.float32),
+        pltpu.VMEM(key.shape, jnp.float32),
+    ]
+    return local_call(
+        attend_back_kernel, outs, scratch, 30, grad, weights, cosine, sine_t, bias, query, key, value, lse
+    )
 
 
 def planned(
@@ -680,70 +1054,44 @@
             cut(w_up[layer], 1, units),
             cut(w_down[layer], 0, units).T,
         ], axis=1)))
-    gains = lax.all_gather(
-        jnp.concatenate([attn_gain, mlp_gain], 0), "fsdp", axis=1, tiled=True
-    ).astype(jnp.float32)
+    seq_pos, seq_valid = own(positions), own(valid)
+    gains, places = start_step(
+        jnp.pad(jnp.concatenate([attn_gain, mlp_gain], 0).astype(jnp.float32), ((0, 8 - 2 * layers), (0, 0))),
+        jnp.pad(jnp.stack([seq_pos, seq_valid]), ((0, 6), (0, 0))),
+    )
+    gains = gains.swapaxes(0, 1).reshape(8, width)
+    places = places.swapaxes(0, 1).reshape(8, length)
     gain_a = [gains[layer][None] for layer in range(layers)]
     gain_m = [gains[layers + layer][None] for layer in range(layers)]
-
-    seq_pos, seq_valid = own(positions), own(valid)
-    starts = own(piece_starts)
-    both = lax.all_gather(jnp.stack([seq_pos, seq_valid]), "ctx", axis=1, tiled=True)
-    pos_all, valid_all = both[0], both[1]
+    pos_all, valid_all = places[0], places[1]
+    stream = own(tokens).astype(jnp.float32)
+    grad = own(d_out).astype(jnp.float32)
+    valid_f = seq_valid.astype(jnp.float32)[:, None]
+    normed = gather_ctx(normalize(stream, gain_a[0]).astype(jnp.bfloat16))
+    down_grad = lax.all_gather(own(d_out), "ctx", axis=0, tiled=True)
+
     half_dim = HEAD_DIM // 2
     freqs = rope_base ** (-(jnp.arange(half_dim).astype(jnp.float32) * 2.0 / HEAD_DIM))
     angles = pos_all.astype(jnp.float32)[:, None] * freqs
-    cosine, sine_t = jnp.cos(angles)[None], jnp.sin(angles)[None]
+    cosine, sine_t = jnp.cos(angles), jnp.sin(angles)
+    cosine = jnp.concatenate([cosine, cosine], axis=1)
+    sine_t = jnp.concatenate([-sine_t, sine_t], axis=1)
+    starts = own(piece_starts)
     index = jnp.arange(length, dtype=jnp.int32)
     inside = (index[None, :] >= starts[:, None]) & (index[None, :] < starts[:, None] + PIECE_LEN)
     same_piece = jnp.any(inside[:, :, None] & inside[:, None, :], axis=0)
-    causal = index[None, :] <= index[:, None]
-    diagonal = index[None, :] == index[:, None]
-    allowed = (causal | same_piece) & ((valid_all[None, :] > 0) | diagonal)
-
-    valid_f = seq_valid.astype(jnp.float32)[:, None]
-    stream = own(tokens).astype(jnp.float32)
-    grad = own(d_out).astype(jnp.float32)
-    down_grad = gather_ctx(own(d_out)).reshape(length, width)
-    normed = gather_ctx(normalize(stream, gain_a[0]).astype(jnp.bfloat16))
-
-    def heads_of(flat, count):
-        return flat.reshape(length, count, HEAD_DIM).swapaxes(0, 1)
-
-    def flat_of(heads):
-        return heads.swapaxes(0, 1).reshape(length, -1)
-
-    def attn_scores(query, key):
-        raw = jnp.einsum(
-            "kgqd,knd->kgqn", query, key, preferred_element_type=jnp.float32
-        ) * score_scale
-        return jnp.where(allowed, raw, neg_big)
-
-    kv_total = heads_k * tp_count
+    causal = index[:, None] <= index[None, :]
+    diagonal = index[:, None] == index[None, :]
+    allowed = (causal | same_piece) & ((valid_all[:, None] > 0) | diagonal)
+    bias = jnp.where(allowed, 0.0, neg_big).astype(jnp.bfloat16)
+
     stat_rows = []
     saved = []
-    branch_out = None
     for layer in range(layers):
         normed_a = normed.reshape(length, width)
-        parts = [dot32(normed_a, attn_w[layer][t][:, : cols_q + 2 * cols_k], ((1,), (0,))) for t in range(tp_count)]
-        query = jnp.concatenate([heads_of(p[:, :cols_q], heads_q) for p in parts])
-        key = jnp.concatenate([heads_of(p[:, cols_q : cols_q + cols_k], heads_k) for p in parts])
-        value = jnp.concatenate([heads_of(p[:, cols_q + cols_k :], heads_k) for p in parts])
-        query = rotate(query, cosine, sine_t).astype(jnp.bfloat16).reshape(kv_total, group, length, HEAD_DIM)
-        key = rotate(key, cosine, sine_t).astype(jnp.bfloat16)
-        value = value.astype(jnp.bfloat16)
-        raw = attn_scores(query, key)
-        row_max = jnp.max(raw, axis=-1, keepdims=True)
-        log_total = row_max + jnp.log(jnp.sum(jnp.exp(raw - row_max), axis=-1, keepdims=True))
-        probs = jnp.exp(raw - log_total).astype(jnp.bfloat16)
-        mixed = jnp.einsum("kgqn,knd->kgqd", probs, value, preferred_element_type=jnp.float32)
-        mixed = mixed.astype(jnp.bfloat16).reshape(tp_count, heads_q, length, HEAD_DIM)
-        mixed = [flat_of(mixed[t]) for t in range(tp_count)]
-        part = sum(
-            dot32(mixed[t], attn_w[layer][t][:, cols_q + 2 * cols_k :], ((1,), (1,))) for t in range(tp_count)
-        )
+        part, query, key, value, lse, mixed = attend(normed_a, attn_w[layer], cosine, sine_t, bias)
         middle, normed_m, attn_sq = forward_step(
-            part.astype(jnp.bfloat16).reshape(4, rows, width), stream, gain_m[layer], valid_f
+            part.reshape(4, rows, width), stream, gain_m[layer], valid_f
         )
         normed_m = normed_m.reshape(length, width)
         gates = [dot32(normed_m, mlp_w[layer][t][:, :units], ((1,), (0,))) for t in range(tp_count)]
@@ -751,31 +1099,36 @@
         hidden = [(jax.nn.silu(g) * u).astype(jnp.bfloat16) for g, u in zip(gates, ups)]
         part = sum(dot32(hidden[t], mlp_w[layer][t][:, 2 * units :], ((1,), (1,))) for t in range(tp_count))
         part = part.astype(jnp.bfloat16).reshape(4, rows, width)
-        saved.append((stream, normed_a, query, key, value, log_total, mixed, middle, normed_m, gates, ups, hidden))
+        saved.append((stream, normed_a, query, key, value, lse, mixed, middle, normed_m, gates, ups, hidden))
         stat_rows.append(jnp.sum(valid_f * stream * stream))
         stat_rows.append(jnp.sum(attn_sq))
         if layer + 1 < layers:
             stream, normed, mlp_sq = forward_step(part, middle, gain_a[layer + 1], valid_f)
             stat_rows.append(jnp.sum(mlp_sq))
         else:
-            branch_out = scatter_ctx(part)
-            stat_rows.append(jnp.sum(valid_f * branch_out * branch_out))
-            stream = middle + branch_out
-    output = lax.all_gather(stream.astype(jnp.bfloat16), "tp", axis=0)
-    sums = lax.psum(
-        jnp.concatenate([jnp.stack(stat_rows), jnp.sum(valid_f)[None]]), ("fsdp", "ctx", "tp")
-    )
-    rms_stats = jnp.sqrt(sums[:-1] / (sums[-1] * width)).reshape(layers, 3)
+            last_part, last_middle = part, middle
+    stat_rows.append(0.0)
+    stat_rows.append(jnp.sum(valid_f))
+    stats = jnp.pad(jnp.stack(stat_rows)[None], ((0, 7), (0, 121)))
 
     def reduced(g):
-        return lax.psum_scatter(
-            g.astype(jnp.bfloat16).reshape(tp_count * width, -1), ("tp", "fsdp"), scatter_dimension=0, tiled=True
-        )
-
-    results = [None] * layers
-    input_grad = None
+        return lax.psum_scatter(g, "fsdp", scatter_dimension=0, tiled=True)
+
+    base = cols_q + 2 * cols_k
+    waiting = {}
+
+    def after(x, names):
+        names = [n for n in names if n in waiting]
+        if not names:
+            return x
+        x, done = lax.optimization_barrier((x, [waiting[n] for n in names]))
+        for n, value in zip(names, done):
+            waiting[n] = value
+        return x
+
     for layer in reversed(range(layers)):
-        stream_in, normed_a, query, key, value, log_total, mixed, middle, normed_m, gates, ups, hidden = saved[layer]
+        stream_in, normed_a, query, key, value, lse, mixed, middle, normed_m, gates, ups, hidden = saved[layer]
+        up_one = layer + 1
         grad_gate, grad_up, part = [], [], 0.0
         for t in range(tp_count):
             wt = mlp_w[layer][t]
@@ -785,72 +1138,79 @@
             grad_up.append((grad_hidden * gates[t] * sig).astype(jnp.bfloat16))
             part += dot32(grad_gate[t], wt[:, :units], ((1,), (1,)))
             part += dot32(grad_up[t], wt[:, units : 2 * units], ((1,), (1,)))
-        g_down = jnp.stack([dot32(down_grad, hidden[t], ((0,), (0,))).astype(jnp.bfloat16) for t in range(tp_count)])
-        g_gate = jnp.stack([dot32(normed_m, grad_gate[t], ((0,), (0,))).astype(jnp.bfloat16) for t in range(tp_count)])
-        g_up = jnp.stack([dot32(normed_m, grad_up[t], ((0,), (0,))).astype(jnp.bfloat16) for t in range(tp_count)])
-        share_mlp = jnp.concatenate([reduced(g_gate), reduced(g_up), reduced(g_down)], axis=1)
-        grad_mid, attn_grad, gm_rows = backward_step(
-            part.astype(jnp.bfloat16).reshape(4, rows, width), middle, gain_m[layer], grad
-        )
+        part = after(part.astype(jnp.bfloat16).reshape(4, rows, width), [(up_one, "mlp")])
+        grad_mid, attn_grad, gm_rows, g_mlp = backward_step(
+            5, part, middle, gain_m[layer], grad, [normed_m, down_grad], [grad_gate, grad_up, hidden], [0, 0, 1],
+            [[(1, 0), (1, 1)], [(1, 2), (0, 0)], [(0, 1)], [(0, 2)]],
+        )
+        waiting[layer, "mlp"] = reduced(g_mlp)
         attn_grad = attn_grad.reshape(length, width)
-        grad_heads = [dot32(attn_grad, attn_w[layer][t][:, cols_q + 2 * cols_k :], ((1,), (0,))).astype(jnp.bfloat16) for t in range(tp_count)]
-        g_out = [dot32(attn_grad, mixed[t], ((0,), (0,))).astype(jnp.bfloat16) for t in range(tp_count)]
-        gh = jnp.concatenate([heads_of(g, heads_q) for g in grad_heads]).reshape(kv_total, group, length, HEAD_DIM)
-        probs = jnp.exp(attn_scores(query, key) - log_total)
-        grad_probs = jnp.einsum("kgqd,knd->kgqn", gh, value, preferred_element_type=jnp.float32)
-        row_dots = jnp.sum(probs * grad_probs, axis=-1, keepdims=True)
-        grad_scores = (probs * (grad_probs - row_dots)).astype(jnp.bfloat16)
-        gq = jnp.einsum("kgqn,knd->kgqd", grad_scores, key, preferred_element_type=jnp.float32) * score_scale
-        gk = jnp.einsum("kgqn,kgqd->knd", grad_scores, query, preferred_element_type=jnp.float32) * score_scale
-        gv = jnp.einsum("kgqn,kgqd->knd", probs.astype(jnp.bfloat16), gh, preferred_element_type=jnp.float32)
-        gq = rotate(gq.reshape(kv_total * group, length, HEAD_DIM), cosine, -sine_t).astype(jnp.bfloat16)
-        gk = rotate(gk, cosine, -sine_t).astype(jnp.bfloat16)
-        gv = gv.astype(jnp.bfloat16)
-        part = 0.0
-        g_attn = []
-        for t in range(tp_count):
-            gqkv = jnp.concatenate([
-                flat_of(gq[t * heads_q : (t + 1) * heads_q]),
-                flat_of(gk[t * heads_k : (t + 1) * heads_k]),
-                flat_of(gv[t * heads_k : (t + 1) * heads_k]),
-            ], axis=1)
-            part += dot32(gqkv, attn_w[layer][t][:, : cols_q + 2 * cols_k], ((1,), (1,)))
-            g_attn.append(dot32(normed_a, gqkv, ((0,), (0,))).astype(jnp.bfloat16))
-        grad, down_grad, ga_rows = backward_step(
-            part.astype(jnp.bfloat16).reshape(4, rows, width), stream_in, gain_a[layer], grad_mid
-        )
-        down_grad = down_grad.reshape(length, width)
-        gain_grads = jnp.stack([jnp.sum(ga_rows, 0), jnp.sum(gm_rows, 0)], axis=1).astype(jnp.bfloat16)
-        g_attn = jnp.stack([jnp.concatenate([g_attn[t], g_out[t], gain_grads if t == 0 else jnp.zeros_like(gain_grads)], axis=1) for t in range(tp_count)])
-        share_attn = reduced(g_attn)
-        results[layer] = (share_attn, share_mlp)
-    input_grad = lax.all_gather(grad, "tp", axis=0)
-
-    outs = [[] for _ in range(9)]
-    for layer in range(layers):
-        share_attn, share_mlp = results[layer]
-        ga = lax.all_gather(share_attn, "ctx", axis=0).astype(jnp.float32)
-        gm = lax.all_gather(share_mlp, "ctx", axis=0).astype(jnp.float32)
-
-        def columns(a):
-            return a.swapaxes(0, 1).reshape(a.shape[1], -1)
-
-        def turned(a):
-            return a.swapaxes(1, 2).reshape(-1, a.shape[1])
-
-        base = cols_q + 2 * cols_k
-        gain_sum = lax.psum(jnp.sum(ga[:, :, base + cols_q :], 0), "tp")
-        outs[0].append(gain_sum[:, 0])
-        outs[1].append(columns(ga[:, :, :cols_q]))
-        outs[2].append(columns(ga[:, :, cols_q : cols_q + cols_k]))
-        outs[3].append(columns(ga[:, :, cols_q + cols_k : base]))
-        outs[4].append(turned(ga[:, :, base : base + cols_q]))
-        outs[5].append(gain_sum[:, 1])
-        outs[6].append(columns(gm[:, :, :units]))
-        outs[7].append(columns(gm[:, :, units : 2 * units]))
-        outs[8].append(turned(gm[:, :, 2 * units :]))
-    stacked = [jnp.stack(o) for o in outs]
-    return (output, input_grad, *stacked, rms_stats)
+        if (up_one, "mlp") in waiting:
+            waiting[up_one, "mlp_all"] = lax.all_gather(waiting[up_one, "mlp"], "ctx", axis=0)
+        part, gqkv = attend_back(attn_grad, attn_w[layer], cosine, sine_t, bias, query, key, value, lse)
+        part = after(part.reshape(4, rows, width), [(up_one, "attn"), (up_one, "mlp_all")])
+        came = backward_step(
+            6 if layer else 7, part, stream_in, gain_a[layer], grad_mid, [normed_a, attn_grad], [[gqkv], [mixed]], [0, 1],
+            [[(1, 0), (1, 1)], [(0, 0), (0, 1)], [], []], other_rows=gm_rows, last=layer == 0,
+        )
+        if layer:
+            grad, down_grad, _, g_attn = came
+            down_grad = down_grad.reshape(length, width)
+        else:
+            input_grad, _, g_attn = came
+        if (up_one, "attn") in waiting:
+            waiting[up_one, "attn_all"] = lax.all_gather(waiting[up_one, "attn"], "ctx", axis=0)
+        waiting[layer, "attn"] = reduced(after(g_attn, [(up_one, "attn_all"), (layer, "mlp")] if layer == 0 else []))
+    waiting[0, "mlp_all"] = lax.all_gather(waiting[0, "mlp"], "ctx", axis=0)
+    output, stats = end_step(last_part, last_middle, valid_f, stats)
+    rms_stats = jnp.sqrt(stats[0, : 3 * layers] / (stats[0, 3 * layers] * width)).reshape(layers, 3)
+    waiting[0, "attn_all"] = lax.all_gather(waiting[0, "attn"], "ctx", axis=0)
+    mlp_outs = place_outs(
+        [waiting[layer, "mlp_all"] for layer in range(layers)],
+        [(0, units, False), (units, units, False), (2 * units, units, True)],
+    )
+    attn_all = [waiting[layer, "attn_all"] for layer in range(layers)]
+    attn_outs = place_outs(
+        attn_all,
+        [(0, cols_q, False), (cols_q, cols_k, False), (cols_q + cols_k, cols_k, False), (base, cols_q, True)],
+    )
+    gain_sum = jnp.stack([
+        jnp.sum(a[:, :, base + cols_q : base + cols_q + 2].astype(jnp.float32), 0) for a in attn_all
+    ])
+    return (
+        output, input_grad, gain_sum[:, :, 0], *attn_outs, gain_sum[:, :, 1], *mlp_outs, rms_stats,
+    )
+
+
+def place_kernel(pieces, ctx_count, *refs):
+    ins, outs = refs[:-len(pieces)], refs[-len(pieces):]
+    for layer, came in enumerate(ins):
+        for (start, size, turn), out in zip(pieces, outs):
+            for c in range(ctx_count):
+                block = came[c, :, start : start + size].astype(jnp.float32)
+                if turn:
+                    out[layer, c * size : (c + 1) * size, :] = block.T
+                else:
+                    out[layer, :, c * size : (c + 1) * size] = block
+
+
+def place_outs(came, pieces):
+    ctx_count, depth, _ = came[0].shape
+    layers = len(came)
+    shapes = [
+        jax.ShapeDtypeStruct(
+            (layers, ctx_count * size, depth) if turn else (layers, depth, ctx_count * size), jnp.float32
+        )
+        for _, size, turn in pieces
+    ]
+    vmem = pl.BlockSpec(memory_space=pltpu.VMEM)
+    return pl.pallas_call(
+        functools.partial(place_kernel, pieces, ctx_count),
+        out_shape=shapes,
+        in_specs=[vmem] * layers,
+        out_specs=[vmem] * len(shapes),
+        compiler_params=pltpu.CompilerParams(vmem_limit_bytes=60 << 20),
+    )(*came)
 
 
 def fits(mesh):

time: 1680 us -> 1050 us (0.62)
  waiting for transfers between devices: 512 us -> 115 us
  Pallas kernels: 464 us -> 722 us
  matrix products: 299 us -> 95.8 us
  local copies, waits for them, and re-layouts: 176 us -> 63.9 us
  other arithmetic: 133 us -> 31.8 us
  blocking collectives: 65.8 us -> 0 us
    reduce_scatter x6 -> x4, waiting for transfers between devices: 418 us -> 63.9 us  [reduced(): return lax.psum_scatter(g, 'fsdp', scatter_dimension=0, tiled=True)]
    pallas_call x10 -> x16, Pallas kernels: 464 us -> 722 us  [the longest x10 575 us: linked_call(): pl.pallas_call(kernel, out_shape=out_shape, in_specs=[vmem] * len(args) +...]
    dot_general x12 -> x0, matrix products: 113 us -> none  [the longest x2 26.2 us: planned(): jnp.einsum('kgqd,knd->kgqn', gh, value, preferred_element_type=jnp.float32)]
    dot_general x60 -> x24, matrix products: 187 us -> 95.8 us  [dot32(): lax.dot_general(a, b, (dims, ((), ())), preferred_element_type=jnp.float32)]
    unnamed x352 -> x98, local copies, waits for them, and re-layouts: 83.4 us -> 10.9 us
    all_gather x6 -> x5, waiting for transfers between devices: 93.7 us -> 50.1 us  [the longest x1 36.5 us: planned(): lax.all_gather(waiting[up_one, 'attn'], 'ctx', axis=0)]
    another operation x30 -> x2, other arithmetic: 43.5 us -> 0.04 us  [the longest x1 0.03 us: planned(): jnp.stack([jnp.sum(a[:, :, base + cols_q:base + cols_q + 2].astype(jnp.fl...]
    psum x2 -> x0, blocking collectives: 42.3 us -> none  [the longest x1 39.6 us: planned(): lax.psum(jnp.concatenate([jnp.stack(stat_rows), jnp.sum(valid_f)[None]]),...]
  transfers between devices with their start and end apart: 18 -> 13, of which waited for: 10 -> 4; matrix products, arithmetic and copies ran while one was open for 19% -> 14% of each run, Pallas kernels for 18% -> 61%
where the time goes in v2:
time: 1050 us
  Pallas kernels  722 us (69%)
  waiting for transfers between devices  115 us (11%)
  matrix products  95.8 us (9%)
  local copies, waits for them, and re-layouts  63.9 us (6%)
  other arithmetic  31.8 us (3%)
  between operations  15.6 us (1%)
    pallas_call x10, Pallas kernels, linked_call(): pl.pallas_call(kernel, out_shape=out_shape, in_specs=[vmem] * len(args) +...  575 us
    pallas_call x4, Pallas kernels, local_call(): pl.pallas_call(kernel, out_shape=out_shape, in_specs=[vmem] * len(args),...  130 us
    dot_general x24, matrix products, dot32(): lax.dot_general(a, b, (dims, ((), ())), preferred_element_type=jnp.float32)  95.8 us
    reduce_scatter x4, waiting for transfers between devices, reduced(): return lax.psum_scatter(g, 'fsdp', scatter_dimension=0, tiled=True)  63.9 us
    all_gather x1, waiting for transfers between devices, planned(): lax.all_gather(waiting[up_one, 'attn'], 'ctx', axis=0)  36.5 us
    all_gather x2, local copies, waits for them, and re-layouts, whole(): lax.all_gather(w, ('tp', 'fsdp'), axis=0, tiled=True)  21.7 us
  transfers between devices with their start and end apart: 13, of which 4 were waited for; matrix products, arithmetic and copies ran while one was open for 14% of the time, Pallas kernels for 61%

profile of v2, /device:TPU:0, one launch (start us, length us, event | category | flops | bytes accessed | tf_op | source)
XLA Modules:
  0.0 1045.2 jit_solution(3664900207298102717)
XLA Ops:
  40.9 10.8 %shard_map.229 = (f32[4,8,384]{2,1,0:T(8,128)}, s32[4,8,288]{2,1,0:T(8,128)}) custom-call(f32[8,384]{1,0:T(8,128)} %fusion.53.gains, s32[8,288]{1,0:T(8,128)} %pad.16.places), custom_call_target="tpu_custom_call" | custom-call | bytes 18000000 | tf_op jit(solution)/shard_map/pallas_call | solution.py:747
  58.8 34.0 %shard_map.230 = bf16[4,288,1536]{2,1,0:T(8,128)(2,1)} custom-call(bf16[288,1536]{1,0:T(8,128)(2,1)} %multiply_convert_fusion.12.x_ref), custom_call_target="tpu_custom_call" | custom-call | bytes 111600000 | tf_op jit(solution)/shard_map/pallas_call | solution.py:747
  99.1 4.8 select_convert_fusion.bias
  103.9 6.1 copy.87
  109.9 30.6 %shard_map.231 = (bf16[1152,1536]{1,0:T(8,128)(2,1)}, bf16[2,9,256,96]{3,2,1,0:T(8,128)(2,1)}, bf16[2,1152,96]{2,1,0:T(8,128)(2,1)}, bf16[2,1152,96]{2,1,0:T(8,1...) custom-call(bf16[1152,1536]{1,0:T(8,128)(2,1)} %bitcast.120, bf16[2,1536,576]{2,1,0:T(8,128)(2,1)} %bitcast.116, ...), custom_call_target="tpu_custom_call" | custom-call | bytes 72000000 | tf_op jit(solution)/shard_map/pallas_call | solution.py:970
  140.5 64.5 %shard_map.232 = (f32[288,1536]{1,0:T(8,128)}, bf16[4,288,1536]{2,1,0:T(8,128)(2,1)}, f32[288,1]{1,0:T(8,128)}) custom-call(bf16[4,288,1536]{2,1,0:T(8,128)(2,1)} %bitcast.133, f32[288,1536]{1,0:T(8,128)} %bitcast_convert_fusion.1.stream.refs_1_, f32[1,1536]{1,0:T(1,128)} %bitcast.168, f32[288,1]{1,0:T(8,128)} %copy.88.valid), custom_call_target="tpu_custom_call" | custom-call | bytes 234000000 | tf_op jit(solution)/shard_map/pallas_call | solution.py:747
  205.1 15.6 %copy.94 = bf16[3072,576]{1,0:T(8,128)(2,1)} copy(bf16[3072,576]{0,1:T(8,128)(2,1)} %all-gather.19.cloned.1.call-done) | data formatting | bytes 7077888 | tf_op jit(solution)/shard_map/all_gather | solution.py:1040
  240.2 63.3 %shard_map.233 = (f32[288,1536]{1,0:T(8,128)}, bf16[4,288,1536]{2,1,0:T(8,128)(2,1)}, f32[288,1]{1,0:T(8,128)}) custom-call(bf16[4,288,1536]{2,1,0:T(8,128)(2,1)} %bitcast.135, f32[288,1536]{1,0:T(8,128)} %get-tuple-element.73.stream.refs_1_, f32[1,1536]{1,0:T(1,128)} %bitcast.170, f32[288,1]{1,0:T(8,128)} %copy.88.valid), custom_call_target="tpu_custom_call" | custom-call | bytes 234000000 | tf_op jit(solution)/shard_map/pallas_call | solution.py:747
  303.6 30.3 %shard_map.234 = (bf16[1152,1536]{1,0:T(8,128)(2,1)}, bf16[2,9,256,96]{3,2,1,0:T(8,128)(2,1)}, bf16[2,1152,96]{2,1,0:T(8,128)(2,1)}, bf16[2,1152,96]{2,1,0:T(8,1...) custom-call(bf16[1152,1536]{1,0:T(8,128)(2,1)} %bitcast.122, bf16[2,1536,576]{2,1,0:T(8,128)(2,1)} %bitcast.118, ...), custom_call_target="tpu_custom_call" | custom-call | bytes 72000000 | tf_op jit(solution)/shard_map/pallas_call | solution.py:970
  333.9 61.2 %shard_map.235 = (f32[288,1536]{1,0:T(8,128)}, bf16[4,288,1536]{2,1,0:T(8,128)(2,1)}, f32[288,1]{1,0:T(8,128)}) custom-call(bf16[4,288,1536]{2,1,0:T(8,128)(2,1)} %bitcast.134, f32[288,1536]{1,0:T(8,128)} %get-tuple-element.76.stream.refs_1_, f32[1,1536]{1,0:T(1,128)} %bitcast.172, f32[288,1]{1,0:T(8,128)} %copy.88.valid), custom_call_target="tpu_custom_call" | custom-call | bytes 234000000 | tf_op jit(solution)/shard_map/pallas_call | solution.py:747
  395.1 4.6 fusion.27
  411.6 7.2 multiply_convert_fusion.6
  418.9 4.3 fusion.25
  423.6 5.5 multiply_convert_fusion.4
  429.1 4.3 convolution_add_fusion.5
  437.2 5.3 fusion.2
  442.5 69.1 %shard_map.237 = (f32[288,1536]{1,0:T(8,128)}, bf16[4,288,1536]{2,1,0:T(8,128)(2,1)}, f32[16,1536]{1,0:T(8,128)}, bf16[1536,1536]{1,0:T(8,128)(2,1)}) custom-call(bf16[4,288,1536]{2,1,0:T(8,128)(2,1)} %bitcast.151, f32[288,1536]{1,0:T(8,128)} %get-tuple-element.78.middle.refs_1_, f32[1,1536]{1,0:T(1,128)} %bitcast.173, ...), custom_call_target="tpu_custom_call" | custom-call | bytes 234000000 | tf_op jit(solution)/shard_map/pallas_call | solution.py:747
  511.7 34.3 %shard_map.238 = (bf16[1152,1536]{1,0:T(8,128)(2,1)}, bf16[2,1152,384]{2,1,0:T(8,128)(2,1)}) custom-call(bf16[1152,1536]{1,0:T(8,128)(2,1)} %bitcast.126, bf16[2,1536,576]{2,1,0:T(8,128)(2,1)} %bitcast.119, f32[1152,96]{1,0:T(8,128)} %pad_maximum_fusion.2.cos_ref, f32[1152,96]{1,0:T(8,128)} %pad_maximum_fusion.3.sin_ref, ...), custom_call_target="tpu_custom_call" | custom-call | bytes 108000000 | tf_op jit(solution)/shard_map/pallas_call | solution.py:970
  546.1 70.5 %shard_map.239 = (f32[288,1536]{1,0:T(8,128)}, bf16[4,288,1536]{2,1,0:T(8,128)(2,1)}, f32[16,1536]{1,0:T(8,128)}, bf16[1536,640]{1,0:T(8,128)(2,1)}) custom-call(bf16[4,288,1536]{2,1,0:T(8,128)(2,1)} %bitcast.131, f32[288,1536]{1,0:T(8,128)} %get-tuple-element.76.stream.refs_1_, f32[1,1536]{1,0:T(1,128)} %bitcast.171, ...), custom_call_target="tpu_custom_call" | custom-call | bytes 234000000 | tf_op jit(solution)/shard_map/pallas_call | solution.py:747
  616.9 6.0 multiply_convert_fusion.2
  622.9 4.3 fusion.45
  642.1 96.4 %shard_map.240 = (f32[288,1536]{1,0:T(8,128)}, bf16[4,288,1536]{2,1,0:T(8,128)(2,1)}, f32[16,1536]{1,0:T(8,128)}, bf16[1536,1536]{1,0:T(8,128)(2,1)}) custom-call(bf16[4,288,1536]{2,1,0:T(8,128)(2,1)} %bitcast.150, f32[288,1536]{1,0:T(8,128)} %get-tuple-element.73.stream.refs_1_, f32[1,1536]{1,0:T(1,128)} %bitcast.169, ...), custom_call_target="tpu_custom_call" | custom-call | bytes 234000000 | tf_op jit(solution)/shard_map/pallas_call | solution.py:747
  738.6 34.4 %shard_map.241 = (bf16[1152,1536]{1,0:T(8,128)(2,1)}, bf16[2,1152,384]{2,1,0:T(8,128)(2,1)}) custom-call(bf16[1152,1536]{1,0:T(8,128)(2,1)} %bitcast.124, bf16[2,1536,576]{2,1,0:T(8,128)(2,1)} %bitcast.117, f32[1152,96]{1,0:T(8,128)} %pad_maximum_fusion.2.cos_ref, f32[1152,96]{1,0:T(8,128)} %pad_maximum_fusion.3.sin_ref, ...), custom_call_target="tpu_custom_call" | custom-call | bytes 108000000 | tf_op jit(solution)/shard_map/pallas_call | solution.py:970
  773.0 41.6 %shard_map.242 = (f32[2,288,1536]{2,1,0:T(8,128)}, f32[16,1536]{1,0:T(8,128)}, bf16[1536,640]{1,0:T(8,128)(2,1)}) custom-call(bf16[4,288,1536]{2,1,0:T(8,128)(2,1)} %bitcast.130, f32[288,1536]{1,0:T(8,128)} %bitcast_convert_fusion.1.stream.refs_1_, f32[1,1536]{1,0:T(1,128)} %bitcast.174, f32[288,1536]{1,0:T(8,128)} %get-tuple-element.106.refs_3_, ...), custom_call_target="tpu_custom_call" | custom-call | bytes 126000000 | tf_op jit(solution)/shard_map/pallas_call | solution.py:747
  814.7 20.2 %reduce-scatter.9.cloned.1.call-done = bf16[384,1536]{1,0:T(8,128)(2,1)} async-done(((bf16[1536,1536]{1,0:T(8,128)(2,1)}), bf16[384,1536]{1,0:T(8,128)(2,1)}) %reduce-scatter.9.cloned.1.call-update) | async-done | bytes 1179664 | tf_op jit(solution)/shard_map/reduce_scatter | solution.py:1115
  834.9 36.5 %all-gather.27.cloned.1.call-done = bf16[1536,640]{1,0:T(8,128)(2,1)} async-done(((bf16[384,640]{1,0:T(8,128)(2,1)}), bf16[1536,640]{1,0:T(8,128)(2,1)}) %all-gather.27.cloned.1.call-update) | async-done | bytes 1966096 | tf_op jit(solution)/shard_map/all_gather | solution.py:1162
  871.4 43.7 %reduce-scatter.11.cloned.1.call-done = bf16[384,640]{1,0:T(8,128)(2,1)} async-done(((bf16[1536,640]{1,0:T(8,128)(2,1)}), bf16[384,640]{1,0:T(8,128)(2,1)}) %reduce-scatter.11.cloned.1.call-update) | async-done | bytes 491536 | tf_op jit(solution)/shard_map/reduce_scatter | solution.py:1115
  927.3 5.2 fusion.1
  932.6 63.3 %shard_map.236 = (bf16[2,288,1536]{2,1,0:T(8,128)(2,1)}, f32[8,128]{1,0:T(8,128)}) custom-call(bf16[4,288,1536]{2,1,0:T(8,128)(2,1)} %bitcast.132, f32[288,1536]{1,0:T(8,128)} %get-tuple-element.78.middle.refs_1_, f32[288,1]{1,0:T(8,128)} %copy.88.valid, f32[8,128]{1,0:T(8,128)} %pad.17.stats), custom_call_target="tpu_custom_call" | custom-call | bytes 111600000 | tf_op jit(solution)/shard_map/pallas_call | solution.py:747
  1000.5 5.6 shard_map.243
  1008.6 13.7 %all-gather.31.cloned.1.call-done = bf16[1536,1536]{1,0:T(8,128)(2,1)} async-done(((bf16[384,1536]{1,0:T(8,128)(2,1)}), bf16[1536,1536]{1,0:T(8,128)(2,1)}) %all-gather.31.cloned.1.call-update) | async-done | bytes 4718608 | tf_op jit(solution)/shard_map/all_gather | solution.py:1164
  1022.2 11.8 %shard_map.244 = (f32[2,384,2048]{2,1,0:T(8,128)}, f32[2,384,2048]{2,1,0:T(8,128)}, f32[2,2048,384]{2,1,0:T(8,128)}) custom-call(bf16[4,384,1536]{2,1,0:T(8,128)(2,1)} %bitcast.129, bf16[4,384,1536]{2,1,0:T(8,128)(2,1)} %bitcast.128), custom_call_target="tpu_custom_call" | custom-call | tf_op jit(solution)/shard_map/pallas_call | solution.py:1207
  (216 shorter events, 120.4 us)
Async XLA Ops:
  7.2 96.7 %all-gather.15.cloned.1.call-start = ((), (), s32[]{:S(2)}) async-start(), calls=%async_computation.4 | async-start | bytes 3981312 | tf_op jit(solution)/shard_map/all_gather | solution.py:1040
  7.2 5.5 copy-start.22
  13.8 11.1 %copy-start.11 = (bf16[2,2048,384]{2,1,0:T(8,128)(2,1)S(1)}, bf16[2,2048,384]{2,1,0:T(8,128)(2,1)}, u32[]{:S(2)}) copy-start(bf16[2,2048,384]{2,1,0:T(8,128)(2,1)} %param.27) | copy-start | bytes 9437188
  17.7 187.4 %all-gather.19.cloned.1.call-start = ((), (), s32[]{:S(2)}) async-start(), calls=%async_computation.6 | async-start | bytes 3981312 | tf_op jit(solution)/shard_map/all_gather | solution.py:1040
  24.9 195.8 %all-gather.17.cloned.1.call-start = ((), (), s32[]{:S(2)}) async-start(), calls=%async_computation.5 | async-start | bytes 10616832 | tf_op jit(solution)/shard_map/all_gather | solution.py:1040
  31.5 363.6 %all-gather.21.cloned.1.call-start = ((), (), s32[]{:S(2)}) async-start(), calls=%async_computation.7 | async-start | bytes 10616832 | tf_op jit(solution)/shard_map/all_gather | solution.py:1040
  35.8 19.2 %copy-start.5 = (bf16[2,288,1536]{2,1,0:T(8,128)(2,1)S(1)}, bf16[2,288,1536]{2,1,0:T(8,128)(2,1)}, u32[]{:S(2)}) copy-start(bf16[2,288,1536]{2,1,0:T(8,128)(2,1)} %param.14) | copy-start | bytes 5308420
  35.8 375.8 %all-gather.23.cloned.1.call-start = ((), (), s32[]{:S(2)}) async-start(), calls=%async_computation.12 | async-start | bytes 4423680 | tf_op jit(solution)/shard_map/all_gather | solution.py:1071
  39.0 602.6 %reduce-scatter.5.cloned.1.call-start = ((), (), s32[]{:S(2)}) async-start(), calls=%async_computation.8 | async-start | bytes 5898240 | tf_op jit(solution)/shard_map/reduce_scatter | solution.py:1115
  39.7 19.1 %copy-start.30 = (f32[288]{0:T(512)}, f32[288]{0:T(512)S(1)}, u32[]{:S(2)}) copy-start(f32[288]{0:T(512)S(1)} %get-tuple-element.129) | copy-start | bytes 3460
  205.1 15.6 %copy-start.8 = (bf16[4,288,1536]{2,1,0:T(8,128)(2,1)S(1)}, bf16[4,288,1536]{2,1,0:T(8,128)(2,1)}, u32[]{:S(2)}) copy-start(bf16[4,288,1536]{2,1,0:T(8,128)(2,1)} %get-tuple-element.72) | copy-start | bytes 10616836
  395.1 6.3 copy-start.23
  418.8 10.3 copy-start.3
  418.8 4.7 copy-start.42
  429.1 8.1 copy-start.21
  511.7 261.3 %reduce-scatter.7.cloned.1.call-start = ((), (), s32[]{:S(2)}) async-start(), calls=%async_computation.9 | async-start | bytes 2457600 | tf_op jit(solution)/shard_map/reduce_scatter | solution.py:1115
  546.1 70.8 %copy-start.40 = (f32[1152,512]{1,0:T(8,128)S(1)}, f32[1152,512]{1,0:T(8,128)}, u32[]{:S(2)}) copy-start(f32[1152,512]{1,0:T(8,128)} %copy-done.39) | copy-start | bytes 7077892
  616.6 156.3 %all-gather.25.cloned.1.call-start = ((), (), s32[]{:S(2)}) async-start(), calls=%async_computation.13 | async-start | bytes 5898240 | tf_op jit(solution)/shard_map/all_gather | solution.py:1149
  622.9 8.1 slice-start
  627.3 5.4 copy-start.43
  641.6 193.3 %reduce-scatter.9.cloned.1.call-start = ((), (), s32[]{:S(2)}) async-start(), calls=%async_computation.10 | async-start | bytes 5898240 | tf_op jit(solution)/shard_map/reduce_scatter | solution.py:1115
  738.5 132.8 %all-gather.27.cloned.1.call-start = ((), (), s32[]{:S(2)}) async-start(), calls=%async_computation.14 | async-start | bytes 2457600 | tf_op jit(solution)/shard_map/all_gather | solution.py:1162
  773.0 142.2 %reduce-scatter.11.cloned.1.call-start = ((), (), s32[]{:S(2)}) async-start(), calls=%async_computation.11 | async-start | bytes 2457600 | tf_op jit(solution)/shard_map/reduce_scatter | solution.py:1115
  814.6 101.3 %copy-start.27 = (f32[288,1]{1,0:T(8,128)S(1)}, f32[288,1]{1,0:T(8,128)}, u32[]{:S(2)}) copy-start(f32[288,1]{1,0:T(8,128)} %get-tuple-element.79) | copy-start | bytes 3460
  814.6 101.9 %copy-start.28 = (f32[288,1]{1,0:T(8,128)S(1)}, f32[288,1]{1,0:T(8,128)}, u32[]{:S(2)}) copy-start(f32[288,1]{1,0:T(8,128)} %get-tuple-element.80) | copy-start | bytes 3460
  814.7 102.5 %copy-start.29 = (f32[288,1]{1,0:T(8,128)S(1)}, f32[288,1]{1,0:T(8,128)}, u32[]{:S(2)}) copy-start(f32[288,1]{1,0:T(8,128)} %get-tuple-element.81) | copy-start | bytes 3460
  814.7 103.2 %copy-start = (f32[288,1536]{1,0:T(8,128)S(1)}, f32[288,1536]{1,0:T(8,128)}, u32[]{:S(2)}) copy-start(f32[288,1536]{1,0:T(8,128)} %get-tuple-element.76.stream.refs_1_) | copy-start | bytes 5308420
  814.7 103.2 %copy-start.31 = (f32[288]{0:T(512)S(1)}, f32[288]{0:T(512)}, u32[]{:S(2)}) copy-start(f32[288]{0:T(512)} %copy-done.30) | copy-start | bytes 3460
  871.4 52.3 %copy-start.14 = (bf16[1152,512]{1,0:T(8,128)(2,1)S(1)}, bf16[1152,512]{1,0:T(8,128)(2,1)}, u32[]{:S(2)}) copy-start(bf16[1152,512]{1,0:T(8,128)(2,1)} %get-tuple-element.145.refs_10_) | copy-start | bytes 3538948
  871.4 129.1 %all-gather.29.cloned.1.call-start = ((), (), s32[]{:S(2)}) async-start(), calls=%async_computation.15 | async-start | bytes 2457600 | tf_op jit(solution)/shard_map/all_gather | solution.py:1167
  915.2 107.1 %all-gather.31.cloned.1.call-start = ((), (), s32[]{:S(2)}) async-start(), calls=%async_computation.16 | async-start | bytes 5898240 | tf_op jit(solution)/shard_map/all_gather | solution.py:1164
  1022.2 11.8 %copy-start.13 = (bf16[2,288,1536]{2,1,0:T(8,128)(2,1)S(1)}, bf16[2,288,1536]{2,1,0:T(8,128)(2,1)}, u32[]{:S(2)}) copy-start(bf16[2,288,1536]{2,1,0:T(8,128)(2,1)} %get-tuple-element.195) | copy-start | bytes 5308420
  (28 other events, 103.6 us)
Sparse Core Ops, SparseCore 0:
  17.8 45.4 all-gather.14
  65.5 40.5 all-gather.18
  108.2 89.5 all-gather.16
  199.2 89.1 all-gather.20
  290.1 46.9 all-gather.22
  511.8 89.8 reduce-scatter.4
  616.8 46.0 reduce-scatter.6
  664.7 79.4 all-gather.24
  746.5 88.3 reduce-scatter.8
  836.6 34.7 all-gather.26
  873.6 41.4 reduce-scatter.10
  916.8 43.9 all-gather.28
  962.6 59.5 all-gather.30

commit v3 on v2

--- a/solution.py
+++ b/solution.py
@@ -4,6 +4,7 @@
 import jax.numpy as jnp
 from jax import lax
 from jax.experimental import pallas as pl
+from jax.experimental.layout import Layout, with_layout_constraint
 from jax.experimental.pallas import tpu as pltpu
 from jax.sharding import PartitionSpec as P
 
@@ -411,11 +412,13 @@
     return copy
 
 
-def nothing():
-    pass
-
-
-def gather_rows(full, sems, place, work=(nothing, nothing)):
+def run(steps, work=()):
+    for n, _ in enumerate(steps):
+        if n < len(work):
+            work[n]()
+
+
+def gather_rows(full, sems, place):
     me, side_x, side_y, _ = place
     to_x, to_y = {"ctx": side_x}, {"ctx": side_y}
     half = full.shape[1] // 2
@@ -428,19 +431,22 @@
         send(full.at[me, top], full.at[me, top], sems, 2, to_y),
         send(full.at[me, low], full.at[me, low], sems, 3, to_x),
     ]
-    work[0]()
+    yield
     first[0].wait_recv()
     rest.append(send(full.at[side_x, top], full.at[side_x, top], sems, 4, to_y))
     first[1].wait_recv()
     rest.append(send(full.at[side_y, low], full.at[side_y, low], sems, 5, to_x))
-    work[1]()
-    for copy in rest:
-        copy.wait()
-    for copy in first:
+    yield
+    rest[0].wait_recv()
+    rest[1].wait_recv()
+    yield
+    rest[2].wait_recv()
+    rest[3].wait_recv()
+    for copy in first + rest:
         copy.wait_send()
 
 
-def scatter_rows(part, from_x, from_y, passed, last, sems, place, work=(nothing, nothing)):
+def scatter_rows(part, from_x, from_y, passed, last, sems, place):
     me, side_x, side_y, across = place
     to_x, to_y = {"ctx": side_x}, {"ctx": side_y}
     half = part.shape[1] // 2
@@ -463,14 +469,14 @@
             total = mine.astype(jnp.float32) + came[1, rows, :].astype(jnp.float32)
             passed[slot, rows, :] = total.astype(passed.dtype)
 
-    work[0]()
+    yield
     early[0].wait_recv()
     add_to(0, side_y, 0, from_x)
     rest.append(send(passed.at[0], last.at[0], sems, 4, to_y))
     early[1].wait_recv()
     add_to(1, side_x, half, from_y)
     rest.append(send(passed.at[1], last.at[1], sems, 5, to_x))
-    work[1]()
+    yield
     for copy in rest:
         copy.wait()
     for copy in early:
@@ -484,23 +490,7 @@
     return total + last[side, rows, :].astype(jnp.float32)
 
 
-def gather_kernel(x_ref, full_ref, local_sem, send_sems, recv_sems):
-    place = partners()
-    greet({"ctx": place[1]}, {"ctx": place[2]})
-    copy = pltpu.make_async_copy(x_ref, full_ref.at[place[0]], local_sem)
-    copy.start()
-    copy.wait()
-    gather_rows(full_ref, (send_sems, recv_sems), place)
-
-
-def forward_kernel(
-    part, stream, gain, valid, middle, full, branch_sq,
-    from_x, from_y, passed, last, send_a, recv_a, send_b, recv_b,
-):
-    place = partners()
-    me = place[0]
-    greet({"ctx": place[1]}, {"ctx": place[2]})
-    scatter_rows(part, from_x, from_y, passed, last, (send_a, recv_a), place)
+def norm_sum(part, stream, gain, valid, middle, full, branch_sq, from_x, from_y, last, me):
     half = part.shape[1] // 2
     step = 16
     for side in range(2):
@@ -517,7 +507,107 @@
             branch_sq[whole_rows, :] = valid[whole_rows, :] * jnp.sum(
                 branch * branch, axis=-1, keepdims=True
             )
-    gather_rows(full, (send_b, recv_b), place)
+
+
+def forward_kernel(
+    part, stream, gain, valid, middle, full, branch_sq,
+    from_x, from_y, passed, last, send_a, recv_a, send_b, recv_b,
+):
+    place = partners()
+    greet({"ctx": place[1]}, {"ctx": place[2]})
+    run(scatter_rows(part, from_x, from_y, passed, last, (send_a, recv_a), place))
+    norm_sum(part, stream, gain, valid, middle, full, branch_sq, from_x, from_y, last, place[0])
+    run(gather_rows(full, (send_b, recv_b), place))
+
+
+def rows_of(ref, lead, top_of, low_of):
+    half = ref.shape[-2] // 2
+    return jnp.concatenate([ref[(*lead, top_of, pl.ds(0, half))], ref[(*lead, low_of, pl.ds(half, half))]], axis=0)
+
+
+def put_rows(ref, lead, top_of, low_of, value):
+    half = ref.shape[-2] // 2
+    ref[(*lead, top_of, pl.ds(0, half))] = value[:half].astype(ref.dtype)
+    ref[(*lead, low_of, pl.ds(half, half))] = value[half:].astype(ref.dtype)
+
+
+def mlp_rows(full, weights, top_of, low_of, hidden, part, gate=None, up=None, back=None):
+    units = hidden.shape[-1]
+    x = rows_of(full, (), top_of, low_of)
+    total, g_total = 0.0, 0.0
+    for t in range(weights.shape[0]):
+        gate_act = dot32(x, weights[t, :, :units], ((1,), (0,)))
+        up_act = dot32(x, weights[t, :, units : 2 * units], ((1,), (0,)))
+        sig = jax.nn.sigmoid(gate_act)
+        unit = (gate_act * sig * up_act).astype(jnp.bfloat16)
+        put_rows(hidden, (t,), top_of, low_of, unit)
+        total += dot32(unit, weights[t, :, 2 * units :], ((1,), (1,)))
+        if back is None:
+            put_rows(gate, (t,), top_of, low_of, gate_act)
+            put_rows(up, (t,), top_of, low_of, up_act)
+        else:
+            g_total += mlp_back_rows(
+                rows_of(back[0], (), top_of, low_of), weights, t, top_of, low_of, gate_act, up_act, sig, back[1], back[2]
+            )
+    put_rows(part, (), top_of, low_of, total)
+    if back is not None:
+        put_rows(back[3], (), top_of, low_of, g_total)
+
+
+def mlp_back_rows(grad, weights, t, top_of, low_of, gate_act, up_act, sig, grad_gate, grad_up):
+    units = grad_gate.shape[-1]
+    g_hidden = dot32(grad, weights[t, :, 2 * units :], ((1,), (0,)))
+    g_gate = (g_hidden * up_act * sig * (1.0 + gate_act * (1.0 - sig))).astype(jnp.bfloat16)
+    g_up = (g_hidden * gate_act * sig).astype(jnp.bfloat16)
+    put_rows(grad_gate, (t,), top_of, low_of, g_gate)
+    put_rows(grad_up, (t,), top_of, low_of, g_up)
+    total = dot32(g_gate, weights[t, :, :units], ((1,), (1,)))
+    return total + dot32(g_up, weights[t, :, units : 2 * units], ((1,), (1,)))
+
+
+def in_turn(steps, place, work):
+    me, side_x, side_y, across = place
+    next(steps)
+    work(me, me)
+    next(steps)
+    work(side_x, side_y)
+    next(steps)
+    work(side_y, side_x)
+    run(steps)
+    work(across, across)
+
+
+def forward_mlp_kernel(back, part, stream, gain, valid, *refs):
+    refs = list(refs)
+    weights_in, grad_in = refs.pop(0), refs.pop(0) if back else None
+    middle, full, branch_sq, out = refs[:4]
+    del refs[:4]
+    hidden, one, two = refs[:3]
+    del refs[:3]
+    out_back = refs.pop(0) if back else None
+    from_x, from_y, passed, last, weights = refs[:5]
+    del refs[:5]
+    grad = refs.pop(0) if back else None
+    send_a, recv_a, send_b, recv_b, local_sems = refs
+    place = partners()
+    greet({"ctx": place[1]}, {"ctx": place[2]})
+    loads = [pltpu.make_async_copy(weights_in, weights, local_sems.at[0])]
+    if back:
+        loads.append(pltpu.make_async_copy(grad_in, grad, local_sems.at[1]))
+    for load in loads:
+        load.start()
+    run(scatter_rows(part, from_x, from_y, passed, last, (send_a, recv_a), place))
+    norm_sum(part, stream, gain, valid, middle, full, branch_sq, from_x, from_y, last, place[0])
+    for load in loads:
+        load.wait()
+
+    def work(top_of, low_of):
+        if back:
+            mlp_rows(full, weights, top_of, low_of, hidden, out, back=(grad, one, two, out_back))
+        else:
+            mlp_rows(full, weights, top_of, low_of, hidden, out, one, two)
+
+    in_turn(gather_rows(full, (send_b, recv_b), place), place, work)
 
 
 def backward_kernel(plan, *refs):
@@ -531,16 +621,21 @@
     count = len(plan.sizes)
     part, stream, gain, grad = take(4)
     other_rows = take(1)[0] if plan.attn else None
+    share = take(1)[0] if plan.last else None
+    gate, up, weights_in = take(3) if plan.mlp else (None, None, None)
     left_in = take(2)
     right_in = [take(n) for n in plan.pieces]
     grad_new = take(1)[0]
     full = None if plan.last else take(1)[0]
     gain_rows = take(1)[0]
     summed = take(1)[0]
+    gathered = take(1)[0] if plan.last else None
+    out, grad_gate, grad_up = take(3) if plan.mlp else (None, None, None)
     from_x, from_y, passed, last = take(4)
     left = take(2)
     right, sent, came = take(count), take(count), take(count)
     gain_sent, gain_came = take(2) if plan.attn else (None, None)
+    weights = take(1)[0] if plan.mlp else None
     send_a, recv_a, send_b, recv_b, send_c, recv_c, local_sems = refs
 
     place = partners()
@@ -561,6 +656,9 @@
     for group in loads:
         for load in group:
             load.start()
+    if plan.mlp:
+        weights_load = pltpu.make_async_copy(weights_in, weights, local_sems.at[2 + 2 * count])
+        weights_load.start()
     starts = [sum(plan.sizes[:p]) for p in range(count)]
     block = 256
     width = stream.shape[1]
@@ -603,7 +701,21 @@
                 (theirs if whose else ours)(p)
         return run
 
-    scatter_rows(part, from_x, from_y, passed, last, (send_a, recv_a), place, (work(0), work(1)))
+    if plan.last:
+        load = pltpu.make_async_copy(share, gathered.at[me], local_sems.at[2 + 2 * count])
+        load.start()
+        load.wait()
+        round_it = gather_rows(gathered, (send_b, recv_b), place)
+
+        def both(slot):
+            def now():
+                next(round_it)
+                work(slot)()
+            return now
+
+        run(scatter_rows(part, from_x, from_y, passed, last, (send_a, recv_a), place), (both(0), both(1)))
+    else:
+        run(scatter_rows(part, from_x, from_y, passed, last, (send_a, recv_a), place), (work(0), work(1)))
     half = part.shape[1] // 2
     step = 16
     gain_rows[...] = jnp.zeros_like(gain_rows)
@@ -636,12 +748,28 @@
         work(2)()
         work(3)()
         add_up()
+        run(round_it)
+    elif plan.mlp:
+        add_up()
+        weights_load.wait()
+
+        def back_rows(top_of, low_of):
+            total = 0.0
+            for t in range(weights.shape[0]):
+                gate_act = rows_of(gate, (t,), top_of, low_of).astype(jnp.float32)
+                total += mlp_back_rows(
+                    rows_of(full, (), top_of, low_of), weights, t, top_of, low_of, gate_act,
+                    rows_of(up, (t,), top_of, low_of).astype(jnp.float32), jax.nn.sigmoid(gate_act), grad_gate, grad_up,
+                )
+            put_rows(out, (), top_of, low_of, total)
+
+        in_turn(gather_rows(full, (send_b, recv_b), place), place, back_rows)
     else:
         def finish():
             work(3)()
             add_up()
 
-        gather_rows(full, (send_b, recv_b), place, (work(2), finish))
+        run(gather_rows(full, (send_b, recv_b), place), (work(2), finish))
     for copy in copies[count:]:
         copy.wait_recv()
     if plan.attn:
@@ -654,12 +782,18 @@
 
 
 class Stage:
-    def __init__(self, sizes, pieces, lefts, slots, attn, last):
+    def __init__(self, sizes, pieces, lefts, slots, attn, last, mlp):
         self.sizes, self.pieces, self.lefts, self.slots = sizes, pieces, lefts, slots
-        self.attn, self.last = attn, last
-
-
-def start_kernel(gains, places, all_gains, all_places, local_sems, send_a, recv_a, send_b, recv_b):
+        self.attn, self.last, self.mlp = attn, last, mlp
+
+
+def start_kernel(
+    gains, places, starts, x, gate, up, down,
+    all_gains, all_places, normed, bias, packed,
+    full, turned, local_sems, send_a, recv_a, send_b, recv_b, send_c, recv_c,
+):
+    place = partners()
+    me, side_x, side_y, across = place
     groups = (
         ("fsdp", gains, all_gains, (send_a, recv_a)),
         ("ctx", places, all_places, (send_b, recv_b)),
@@ -669,34 +803,90 @@
         count = lax.axis_size(axis)
         peers.append([lax.rem(lax.axis_index(axis) + step, count) for step in range(1, count)])
     greet(*[{groups[n][0]: peer} for n in range(2) for peer in peers[n]])
+    own = pltpu.make_async_copy(x, full.at[me], local_sems.at[0])
+    own.start()
     copies = []
     for n, (axis, src, dst, sems) in enumerate(groups):
-        me = lax.axis_index(axis)
+        mine = pltpu.make_async_copy(src, dst.at[lax.axis_index(axis)], local_sems.at[1 + n])
+        mine.start()
         for step, peer in enumerate(peers[n]):
-            copies.append(send(src, dst.at[me], sems, step, {axis: peer}))
-        mine = pltpu.make_async_copy(src, dst.at[me], local_sems.at[n])
-        mine.start()
+            copies.append(send(src, dst.at[lax.axis_index(axis)], sems, step, {axis: peer}))
         mine.wait()
+    layers, depth, units = packed.shape[0], packed.shape[1], turned.shape[1]
+    loads = []
+    for layer in range(layers):
+        cut = pl.ds(pl.multiple_of(me * units, units), units)
+        for n, (src, dst) in enumerate((
+            (gate.at[layer, :, cut], packed.at[layer, :, pl.ds(0, units)]),
+            (up.at[layer, :, cut], packed.at[layer, :, pl.ds(units, units)]),
+            (down.at[layer, cut], turned.at[layer]),
+        )):
+            loads.append(pltpu.make_async_copy(src, dst, local_sems.at[3 + 3 * layer + n]))
+    for load in loads:
+        load.start()
+    own.wait()
+    steps = gather_rows(full, (send_c, recv_c), place)
+    next(steps)
     for copy in copies:
         copy.wait()
-
-
-def end_kernel(
-    part, middle, valid, stats, out, all_stats,
-    from_x, from_y, passed, last, sums, stat_sent, stat_came, z_came, send_a, recv_a, send_c, recv_c, send_d, recv_d,
-):
+    gain = jnp.concatenate([all_gains[n, 0:1, :] for n in range(lax.axis_size("fsdp"))], axis=1)
+    rows = full.shape[1]
+    half = rows // 2
+    step = 16
+
+    def norm(top_of, low_of):
+        for part_no, owner in enumerate((top_of, low_of)):
+            @pl.loop(0, half // step)
+            def _(i):
+                here = pl.ds(pl.multiple_of(part_no * half + i * step, step), step)
+                row = full[owner, here, :].astype(jnp.float32)
+                inv_rms = lax.rsqrt(jnp.mean(row * row, axis=-1, keepdims=True) + epsilon)
+                normed[owner, here, :] = (row * inv_rms * gain).astype(normed.dtype)
+
+    def mask():
+        length = bias.shape[0]
+        block = 96
+        query = lax.broadcasted_iota(jnp.int32, (1, length), 1)
+        firsts = [starts[0:1, n : n + 1] for n in range(starts.shape[1])]
+        in_query = [jnp.where((query >= f) & (query < f + PIECE_LEN), 1, 0) for f in firsts]
+        for owner in range(all_places.shape[0]):
+            @pl.loop(0, rows // block)
+            def _(i):
+                here = pl.ds(pl.multiple_of(i * block, block), block)
+                key = owner * rows + i * block + lax.broadcasted_iota(jnp.int32, (block, 1), 0)
+                valid = all_places[owner, here, 1:2]
+                seen = 0
+                for f, row in zip(firsts, in_query):
+                    seen += jnp.where((key >= f) & (key < f + PIECE_LEN), 1, 0) * row
+                seen = jnp.where(key <= query, 1, seen) * valid
+                seen = jnp.where(key == query, 1, seen)
+                bias[pl.ds(pl.multiple_of(owner * rows + i * block, block), block), :] = jnp.where(
+                    seen > 0, 0.0, neg_big
+                ).astype(bias.dtype)
+
+    norm(me, me)
+    mask()
+    next(steps)
+    norm(side_x, side_y)
+    for load in loads:
+        load.wait()
+    for layer in range(layers):
+        packed[layer, :, 2 * units :] = turned[layer].astype(jnp.float32).T.astype(packed.dtype)
+    next(steps)
+    norm(side_y, side_x)
+    run(steps)
+    norm(across, across)
+
+
+def end_steps(part, middle, valid, out, branch_sq, from_x, from_y, passed, last, send_a, recv_a, send_c, recv_c):
     place = partners()
     me = place[0]
     side = lax.axis_index("tp")
-    depth = lax.axis_size("fsdp")
-    level = lax.axis_index("fsdp")
     sibling = {"tp": 1 - side}
-    others = [{"fsdp": lax.rem(level + step, depth)} for step in range(1, depth)]
-    greet({"ctx": place[1]}, {"ctx": place[2]}, sibling, *others)
-    scatter_rows(part, from_x, from_y, passed, last, (send_a, recv_a), place)
+    greet({"ctx": place[1]}, {"ctx": place[2]}, sibling)
+    yield from scatter_rows(part, from_x, from_y, passed, last, (send_a, recv_a), place)
     half = part.shape[1] // 2
     step = 16
-    sums[...] = jnp.zeros_like(sums)
     for part_no in range(2):
         @pl.loop(0, half // step)
         def _(i):
@@ -705,26 +895,86 @@
             whole_rows = pl.ds(pl.multiple_of(start, step), step)
             branch = own_sum(part, from_x, from_y, last, me, part_no, rows, start, step)
             out[side, whole_rows, :] = (middle[whole_rows, :] + branch).astype(out.dtype)
-            sums[...] += valid[whole_rows, :] * jnp.sum(branch * branch, axis=-1, keepdims=True)
-    handed = send(out.at[side], out.at[side], (send_c, recv_c), 0, sibling)
-    total = jnp.sum(sums[...], axis=0, keepdims=True)
-    lane = lax.broadcasted_iota(jnp.int32, (8, 128), 1)
-    held = stats[...] + jnp.where(lane == 5, total, 0.0)
+            branch_sq[whole_rows, :] = valid[whole_rows, :] * jnp.sum(
+                branch * branch, axis=-1, keepdims=True
+            )
+    send(out.at[side], out.at[side], (send_c, recv_c), 0, sibling).wait()
+
+
+def stat_steps(stats, all_stats, stat_sent, stat_came, z_came, sems, place):
+    depth = lax.axis_size("fsdp")
+    level = lax.axis_index("fsdp")
+    sibling = {"tp": 1 - lax.axis_index("tp")}
+    others = [{"fsdp": lax.rem(level + step, depth)} for step in range(1, depth)]
+    stat_sent[0] = stats[...]
     for n, peer in enumerate((sibling, {"ctx": place[1]}, {"ctx": place[2]})):
-        stat_sent[n] = held
-        send(stat_sent.at[n], stat_came.at[n], (send_d, recv_d), n, peer).wait()
-        held = held + stat_came[n]
-    z_came[level] = held
-    copies = [
-        send(z_came.at[level], z_came.at[level], (send_d, recv_d), 3 + n, peer) for n, peer in enumerate(others)
-    ]
+        copy = send(stat_sent.at[n], stat_came.at[n], sems, n, peer)
+        yield
+        copy.wait()
+        stat_sent[n + 1] = stat_sent[n] + stat_came[n]
+    z_came[level] = stat_sent[3]
+    copies = [send(z_came.at[level], z_came.at[level], sems, 3 + n, peer) for n, peer in enumerate(others)]
+    yield
     for copy in copies:
         copy.wait()
     held = z_came[0]
     for n in range(1, depth):
         held = held + z_came[n]
     all_stats[...] = held
-    handed.wait()
+
+
+def gather_steps(share, full, local_sem, send_sems, recv_sems):
+    place = partners()
+    greet({"ctx": place[1]}, {"ctx": place[2]})
+    copy = pltpu.make_async_copy(share, full.at[place[0]], local_sem)
+    copy.start()
+    copy.wait()
+    yield from gather_rows(full, (send_sems, recv_sems), place)
+
+
+def tail_kernel(
+    summed, share, stats, gathered, last_all, all_stats, z_came, stat_sent, stat_came, stat_z,
+    local_sem, send_a, recv_a, send_b, recv_b, send_c, recv_c, send_d, recv_d,
+):
+    place = partners()
+    me = place[0]
+    depth = lax.axis_size("fsdp")
+    level = lax.axis_index("fsdp")
+    peers = [lax.rem(level + step, depth) for step in range(1, depth)]
+    greet({"ctx": place[1]}, {"ctx": place[2]}, {"tp": 1 - lax.axis_index("tp")}, *[{"fsdp": peer} for peer in peers])
+    rows = share.shape[0]
+    counts = stat_steps(stats, all_stats, stat_sent, stat_came, stat_z, (send_c, recv_c), place)
+    next(counts)
+    copies = []
+    for step, peer in enumerate(peers):
+        block = summed.at[pl.ds(pl.multiple_of(peer * rows, rows), rows)]
+        copies.append(send(block, z_came.at[level], (send_a, recv_a), step, {"fsdp": peer}))
+    mine = pltpu.make_async_copy(share, gathered.at[me], local_sem)
+    mine.start()
+    mine.wait()
+    first = gather_rows(gathered, (send_b, recv_b), place)
+    next(first)
+    next(counts)
+    next(counts)
+    next(first)
+    next(counts)
+    run(counts)
+    for copy in copies:
+        copy.wait_recv()
+    step = 48
+
+    @pl.loop(0, rows // step)
+    def _(i):
+        part_rows = pl.ds(pl.multiple_of(i * step, step), step)
+        total = summed[pl.ds(pl.multiple_of(level * rows + i * step, step), step), :].astype(jnp.float32)
+        for peer in peers:
+            total += z_came[peer, part_rows, :].astype(jnp.float32)
+        last_all[me, part_rows, :] = total.astype(last_all.dtype)
+
+    run(gather_rows(last_all, (send_d, recv_d), place))
+    run(first)
+    for copy in copies:
+        copy.wait_send()
 
 
 def rs_scratch(rows, width):
@@ -759,14 +1009,6 @@
     )(*args, *far)
 
 
-def gather_ctx(x):
-    rows, width = x.shape
-    return linked_call(
-        gather_kernel, 1, jax.ShapeDtypeStruct((4, rows, width), x.dtype),
-        [pltpu.SemaphoreType.DMA] + dma_sems(6), 31, [x],
-    )
-
-
 def forward_step(part, stream, gain, valid):
     rows, width = stream.shape
     return linked_call(
@@ -781,59 +1023,99 @@
     )
 
 
-def backward_step(number, part, stream, gain, grad, lefts, rights, pairs, slots, other_rows=None, last=False):
+def forward_mlp_step(part, stream, gain, valid, weights, grad=None):
+    rows, width = stream.shape
+    pairs, units = weights.shape[0], weights.shape[2] // 3
+    bf16, f32 = jnp.bfloat16, jnp.float32
+    shape = jax.ShapeDtypeStruct
+    whole = shape((4, rows, width), bf16)
+    outs = [shape((rows, width), f32), whole, shape((rows, 1), f32), whole]
+    outs += [shape((pairs, 4, rows, units), bf16)] * 3
+    back = grad is not None
+    scratch = rs_scratch(rows, width) + [pltpu.VMEM(weights.shape, bf16)]
+    if back:
+        outs.append(whole)
+        scratch.append(pltpu.VMEM(whole.shape, bf16))
+    scratch += dma_sems(6) + dma_sems(6) + [pltpu.SemaphoreType.DMA((2,))]
+    return linked_call(
+        functools.partial(forward_mlp_kernel, back), 13 if back else 12, outs, scratch, 75,
+        [part, stream, gain, valid], [weights] + ([grad] if back else []),
+    )
+
+
+def backward_step(number, part, stream, gain, grad, lefts, rights, pairs, slots, other_rows=None, share=None, mlp=None):
     rows, width = stream.shape
     length = lefts[0].shape[0]
     sizes = [r[0].shape[-1] for r in rights]
     pieces = [len(r) for r in rights]
     attn = other_rows is not None
+    last = share is not None
     total = sum(sizes) + (64 if attn else 0)
     bf16, f32 = jnp.bfloat16, jnp.float32
     outs = [jax.ShapeDtypeStruct(((2,) if last else ()) + (rows, width), f32)]
     if not last:
         outs.append(jax.ShapeDtypeStruct((4, rows, width), bf16))
     outs += [jax.ShapeDtypeStruct((16, width), f32), jax.ShapeDtypeStruct((width, total), bf16)]
+    if last:
+        outs.append(jax.ShapeDtypeStruct((4, *share.shape), bf16))
+    if mlp is not None:
+        outs += [jax.ShapeDtypeStruct((4, rows, width), bf16)] + [jax.ShapeDtypeStruct(mlp[0].shape, bf16)] * 2
     scratch = rs_scratch(rows, width)
     scratch += [pltpu.VMEM((length, width), bf16)] * 2
     scratch += [pltpu.VMEM((2, length, n), bf16) for n in sizes]
     scratch += [pltpu.VMEM((width, n), bf16) for n in sizes] * 2
     if attn:
         scratch += [pltpu.VMEM((8, width), f32)] * 2
+    if mlp is not None:
+        scratch.append(pltpu.VMEM(mlp[2].shape, bf16))
     scratch += dma_sems(6) + dma_sems(6) + dma_sems(len(sizes) + 2)
-    scratch += [pltpu.SemaphoreType.DMA((2 + 2 * len(sizes),))]
+    scratch += [pltpu.SemaphoreType.DMA((3 + 2 * len(sizes),))]
     return linked_call(
-        functools.partial(backward_kernel, Stage(sizes, pieces, pairs, slots, attn, last)),
+        functools.partial(backward_kernel, Stage(sizes, pieces, pairs, slots, attn, last, mlp is not None)),
         number, outs, scratch, 35 if last else 65,
-        [part, stream, gain, grad] + ([other_rows] if attn else []),
-        list(lefts) + [half for r in rights for half in r],
-    )
-
-
-def end_step(part, middle, valid, stats):
-    rows, width = middle.shape
+        [part, stream, gain, grad] + ([other_rows] if attn else []) + ([share] if last else [])
+        + (list(mlp[:2]) if mlp is not None else []),
+        (list(mlp[2:]) if mlp is not None else []) + list(lefts) + [half for r in rights for half in r],
+    )
+
+
+def tail_step(summed, share, stats):
     depth = lax.axis_size("fsdp")
-    f32 = jnp.float32
+    shape = jax.ShapeDtypeStruct
+    bf16, f32 = jnp.bfloat16, jnp.float32
+    last = (share.shape[0], summed.shape[1])
+    outs = [shape((4, *share.shape), bf16), shape((4, *last), bf16), shape((8, 128), f32)]
     return linked_call(
-        end_kernel, 4,
-        (jax.ShapeDtypeStruct((2, rows, width), jnp.bfloat16), jax.ShapeDtypeStruct((8, 128), f32)),
-        rs_scratch(rows, width)
-        + [pltpu.VMEM((16, 1), f32), pltpu.VMEM((3, 8, 128), f32), pltpu.VMEM((3, 8, 128), f32)]
-        + [pltpu.VMEM((depth, 8, 128), f32)]
-        + dma_sems(6) + dma_sems(1) + dma_sems(3 + depth),
-        31, [part, middle, valid, stats],
-    )
-
-
-def start_step(gains, places):
+        tail_kernel, 10, outs,
+        [pltpu.VMEM((depth, *last), bf16), pltpu.VMEM((4, 8, 128), f32), pltpu.VMEM((3, 8, 128), f32)]
+        + [pltpu.VMEM((depth, 8, 128), f32), pltpu.SemaphoreType.DMA]
+        + dma_sems(depth) + dma_sems(6) + dma_sems(3 + depth) + dma_sems(6),
+        60, [summed, share, stats],
+    )
+
+
+def start_step(gains, places, starts, x, gate, up, down):
     depth, across = lax.axis_size("fsdp"), lax.axis_size("ctx")
+    layers, rows = gate.shape[:2]
+    units = gate.shape[2] // across
+    length = across * x.shape[0]
+    bf16 = jnp.bfloat16
+    shape = jax.ShapeDtypeStruct
     return linked_call(
         start_kernel, 8,
         (
-            jax.ShapeDtypeStruct((depth, *gains.shape), gains.dtype),
-            jax.ShapeDtypeStruct((across, *places.shape), places.dtype),
+            shape((depth, *gains.shape), gains.dtype),
+            shape((across, *places.shape), places.dtype),
+            shape((across, *x.shape), bf16),
+            shape((length, length), bf16),
+            shape((layers, rows, 3 * units), bf16),
         ),
-        [pltpu.SemaphoreType.DMA((2,))] + dma_sems(depth) + dma_sems(across),
-        5, [gains, places],
+        [
+            pltpu.VMEM((across, *x.shape), bf16),
+            pltpu.VMEM((layers, units, rows), bf16),
+            pltpu.SemaphoreType.DMA((3 + 3 * layers,)),
+        ] + dma_sems(depth) + dma_sems(across) + dma_sems(6),
+        38, [gains, places, starts, x], [gate, up, down],
     )
 
 
@@ -862,7 +1144,16 @@
     return groups
 
 
-def attend_kernel(normed, weights, cos_ref, sin_ref, bias, part, query, key, value, lse, mixed):
+def attend_kernel(
+    normed, weights, cos_ref, sin_ref, bias, share, part, query, key, value, lse, mixed, gathered, *sems
+):
+    job = gather_steps(share, gathered, *sems)
+    next(job)
+    attend_rows(normed, weights, cos_ref, sin_ref, bias, part, query, key, value, lse, mixed, lambda: next(job))
+    run(job)
+
+
+def attend_rows(normed, weights, cos_ref, sin_ref, bias, part, query, key, value, lse, mixed, between=lambda: None):
     length = normed.shape[0]
     pairs = weights.shape[0]
     cols_q = 2 * HEAD_DIM
@@ -900,17 +1191,33 @@
             lse[t, block] = top + jnp.log2(total)
             for g in range(2):
                 mixed[t, rows, g * HEAD_DIM : (g + 1) * HEAD_DIM] = out[g * QUERIES : (g + 1) * QUERIES]
+        if first == 0:
+            between()
 
     @pl.loop(0, length // ROWS)
     def _(i):
         rows = pl.ds(pl.multiple_of(i * ROWS, ROWS), ROWS)
-        total = dot32(mixed[0, rows, :], weights[0, :, base:], ((1,), (1,)))
+        total = dot32(mixed[0, rows, :], weights[0, :, base : base + cols_q], ((1,), (1,)))
         for t in range(1, pairs):
-            total += dot32(mixed[t, rows, :], weights[t, :, base:], ((1,), (1,)))
+            total += dot32(mixed[t, rows, :], weights[t, :, base : base + cols_q], ((1,), (1,)))
         part[rows, :] = total.astype(jnp.bfloat16)
 
 
-def attend_back_kernel(grad, weights, cos_ref, sin_ref, bias, query, key, value, lse, part, grad_qkv, heads, g_key, g_value):
+def attend_back_kernel(steps, counts, *refs):
+    refs = list(refs)
+
+    def take(count):
+        taken = refs[:count]
+        del refs[:count]
+        return taken
+
+    grad, weights, cos_ref, sin_ref, bias, query, key, value, lse = take(9)
+    job_refs = take(counts[0])
+    part, grad_qkv = take(2)
+    job_refs += take(counts[1])
+    heads, g_key, g_value = take(3)
+    job = steps(*job_refs, *refs)
+    next(job)
     length = grad.shape[0]
     pairs = weights.shape[0]
     cols_q = 2 * HEAD_DIM
@@ -923,7 +1230,7 @@
     def _(i):
         rows = pl.ds(pl.multiple_of(i * ROWS, ROWS), ROWS)
         for t in range(pairs):
-            flat = dot32(grad[rows, :], weights[t, :, base:], ((1,), (0,))).astype(jnp.bfloat16)
+            flat = dot32(grad[rows, :], weights[t, :, base : base + cols_q], ((1,), (0,))).astype(jnp.bfloat16)
             for g in range(2):
                 for n in range(blocks):
                     heads[t, i * blocks + n, g * QUERIES : (g + 1) * QUERIES, :] = flat[
@@ -952,6 +1259,8 @@
                 grad_qkv[t, rows, g * HEAD_DIM : (g + 1) * HEAD_DIM] = turn(
                     g_query[g * QUERIES : (g + 1) * QUERIES], cos_b, -sin_b
                 ).astype(jnp.bfloat16)
+        if first == 0:
+            next(job)
 
     @pl.loop(0, length // ROWS)
     def _(i):
@@ -963,6 +1272,7 @@
             grad_qkv[t, rows, cols_q + HEAD_DIM : base] = g_value[t, rows, :].astype(jnp.bfloat16)
             total += dot32(grad_qkv[t, rows, :], weights[t, :, :base], ((1,), (1,)))
         part[rows, :] = total.astype(jnp.bfloat16)
+    run(job)
 
 
 def local_call(kernel, out_shape, scratch, micros, *args):
@@ -978,7 +1288,7 @@
     )(*args)
 
 
-def attend(normed, weights, cosine, sine_t, bias):
+def attend(normed, weights, cosine, sine_t, bias, share=None):
     length, width = normed.shape
     pairs = weights.shape[0]
     blocks = length // QUERIES
@@ -992,22 +1302,34 @@
         shape((pairs, blocks, 1, 2 * QUERIES), jnp.float32),
         shape((pairs, length, 2 * HEAD_DIM), bf16),
     ]
-    return local_call(attend_kernel, outs, [], 20, normed, weights, cosine, sine_t, bias)
-
-
-def attend_back(grad, weights, cosine, sine_t, bias, query, key, value, lse):
+    if share is None:
+        return local_call(attend_rows, outs, [], 30, normed, weights, cosine, sine_t, bias)
+    return linked_call(
+        attend_kernel, 11, outs + [shape((4, *share.shape), bf16)], [pltpu.SemaphoreType.DMA] + dma_sems(6), 35,
+        [normed, weights, cosine, sine_t, bias, share],
+    )
+
+
+def attend_back(grad, weights, cosine, sine_t, bias, query, key, value, lse, share=None, end=None):
     length, width = grad.shape
     pairs = weights.shape[0]
-    bf16 = jnp.bfloat16
+    bf16, f32 = jnp.bfloat16, jnp.float32
     shape = jax.ShapeDtypeStruct
     outs = [shape((length, width), bf16), shape((pairs, length, 4 * HEAD_DIM), bf16)]
-    scratch = [
-        pltpu.VMEM(query.shape, bf16),
-        pltpu.VMEM(key.shape, jnp.float32),
-        pltpu.VMEM(key.shape, jnp.float32),
-    ]
-    return local_call(
-        attend_back_kernel, outs, scratch, 30, grad, weights, cosine, sine_t, bias, query, key, value, lse
+    scratch = [pltpu.VMEM(query.shape, bf16), pltpu.VMEM(key.shape, f32), pltpu.VMEM(key.shape, f32)]
+    if end is None:
+        steps, number, more = gather_steps, 9, [share]
+        more_outs = [shape((4, *share.shape), bf16)]
+        scratch += [pltpu.SemaphoreType.DMA] + dma_sems(6)
+    else:
+        steps, number, more = end_steps, 4, end
+        rows = end[1].shape[0]
+        more_outs = [shape((2, rows, width), bf16), shape((rows, 1), f32)]
+        scratch += rs_scratch(rows, width) + dma_sems(6) + dma_sems(1)
+    return linked_call(
+        functools.partial(attend_back_kernel, steps, (len(more), len(more_outs))),
+        number, outs + more_outs, scratch, 40,
+        [grad, weights, cosine, sine_t, bias, query, key, value, lse, *more],
     )
 
 
@@ -1024,11 +1346,9 @@
     length = rows * ctx_count
     heads_q = HEADS // tp_count // ctx_count
     heads_k = KV_HEADS // tp_count // ctx_count
-    group = HEADS // KV_HEADS
     cols_q = heads_q * HEAD_DIM
     cols_k = heads_k * HEAD_DIM
     units = w_gate.shape[2] // ctx_count
-    score_scale = HEAD_DIM ** (-0.5)
 
     def own(a):
         return lax.dynamic_index_in_dim(a, side, 0, keepdims=False)
@@ -1041,81 +1361,79 @@
             tp_count, width, w.shape[1]
         )
 
-    attn_w, mlp_w = [], []
-    for layer in range(layers):
-        attn_w.append(whole(jnp.concatenate([
+    def pack(*pieces):
+        return with_layout_constraint(jnp.concatenate(pieces, axis=1), Layout(major_to_minor=(0, 1)))
+
+    def pack_attn(layer):
+        return pack(
             cut(w_query[layer], 1, cols_q),
             cut(w_key[layer], 1, cols_k),
             cut(w_value[layer], 1, cols_k),
             cut(w_out[layer], 0, cols_q).T,
-        ], axis=1)))
-        mlp_w.append(whole(jnp.concatenate([
-            cut(w_gate[layer], 1, units),
-            cut(w_up[layer], 1, units),
-            cut(w_down[layer], 0, units).T,
-        ], axis=1)))
+            jnp.zeros((w_query.shape[1], 64), w_query.dtype),
+        )
+
+    attn_w = [whole(pack_attn(0))]
+    packed_attn = [None] + [pack_attn(layer) for layer in range(1, layers)]
+    mlp_w = []
     seq_pos, seq_valid = own(positions), own(valid)
-    gains, places = start_step(
+    starts = own(piece_starts)
+    gains, places, normed, bias, packed = start_step(
         jnp.pad(jnp.concatenate([attn_gain, mlp_gain], 0).astype(jnp.float32), ((0, 8 - 2 * layers), (0, 0))),
-        jnp.pad(jnp.stack([seq_pos, seq_valid]), ((0, 6), (0, 0))),
-    )
+        jnp.pad(jnp.stack([seq_pos, seq_valid], axis=1), ((0, 0), (0, 6))),
+        starts[None], own(tokens), w_gate, w_up, w_down,
+    )
+    packed_mlp = [packed[layer] for layer in range(layers)]
     gains = gains.swapaxes(0, 1).reshape(8, width)
-    places = places.swapaxes(0, 1).reshape(8, length)
     gain_a = [gains[layer][None] for layer in range(layers)]
     gain_m = [gains[layers + layer][None] for layer in range(layers)]
-    pos_all, valid_all = places[0], places[1]
+    pos_all = places[:, :, 0].reshape(length)
     stream = own(tokens).astype(jnp.float32)
     grad = own(d_out).astype(jnp.float32)
     valid_f = seq_valid.astype(jnp.float32)[:, None]
-    normed = gather_ctx(normalize(stream, gain_a[0]).astype(jnp.bfloat16))
-    down_grad = lax.all_gather(own(d_out), "ctx", axis=0, tiled=True)
-
+    mlp_w.append(whole(packed_mlp[0]))
     half_dim = HEAD_DIM // 2
     freqs = rope_base ** (-(jnp.arange(half_dim).astype(jnp.float32) * 2.0 / HEAD_DIM))
     angles = pos_all.astype(jnp.float32)[:, None] * freqs
     cosine, sine_t = jnp.cos(angles), jnp.sin(angles)
     cosine = jnp.concatenate([cosine, cosine], axis=1)
     sine_t = jnp.concatenate([-sine_t, sine_t], axis=1)
-    starts = own(piece_starts)
-    index = jnp.arange(length, dtype=jnp.int32)
-    inside = (index[None, :] >= starts[:, None]) & (index[None, :] < starts[:, None] + PIECE_LEN)
-    same_piece = jnp.any(inside[:, :, None] & inside[:, None, :], axis=0)
-    causal = index[:, None] <= index[None, :]
-    diagonal = index[:, None] == index[None, :]
-    allowed = (causal | same_piece) & ((valid_all[:, None] > 0) | diagonal)
-    bias = jnp.where(allowed, 0.0, neg_big).astype(jnp.bfloat16)
-
     stat_rows = []
     saved = []
     for layer in range(layers):
         normed_a = normed.reshape(length, width)
-        part, query, key, value, lse, mixed = attend(normed_a, attn_w[layer], cosine, sine_t, bias)
-        middle, normed_m, attn_sq = forward_step(
-            part.reshape(4, rows, width), stream, gain_m[layer], valid_f
-        )
+        if layer:
+            part, query, key, value, lse, mixed = attend(normed_a, attn_w[layer], cosine, sine_t, bias)
+        else:
+            part, query, key, value, lse, mixed, down_grad = attend(
+                normed_a, attn_w[layer], cosine, sine_t, bias, own(d_out)
+            )
+        came = forward_mlp_step(
+            part.reshape(4, rows, width), stream, gain_m[layer], valid_f, mlp_w[layer],
+            down_grad if layer + 1 == layers else None,
+        )
+        middle, normed_m, attn_sq, mlp_part = came[:4]
+        if layer + 1 < layers:
+            normed_m, packed_attn[layer + 1], packed_mlp[layer + 1] = lax.optimization_barrier(
+                (normed_m, packed_attn[layer + 1], packed_mlp[layer + 1])
+            )
+            attn_w.append(whole(packed_attn[layer + 1]))
+            mlp_w.append(whole(packed_mlp[layer + 1]))
         normed_m = normed_m.reshape(length, width)
-        gates = [dot32(normed_m, mlp_w[layer][t][:, :units], ((1,), (0,))) for t in range(tp_count)]
-        ups = [dot32(normed_m, mlp_w[layer][t][:, units : 2 * units], ((1,), (0,))) for t in range(tp_count)]
-        hidden = [(jax.nn.silu(g) * u).astype(jnp.bfloat16) for g, u in zip(gates, ups)]
-        part = sum(dot32(hidden[t], mlp_w[layer][t][:, 2 * units :], ((1,), (1,))) for t in range(tp_count))
-        part = part.astype(jnp.bfloat16).reshape(4, rows, width)
-        saved.append((stream, normed_a, query, key, value, lse, mixed, middle, normed_m, gates, ups, hidden))
+        saved.append((stream, normed_a, query, key, value, lse, mixed, middle, normed_m, came[4:]))
         stat_rows.append(jnp.sum(valid_f * stream * stream))
         stat_rows.append(jnp.sum(attn_sq))
         if layer + 1 < layers:
-            stream, normed, mlp_sq = forward_step(part, middle, gain_a[layer + 1], valid_f)
+            stream, normed, mlp_sq = forward_step(mlp_part, middle, gain_a[layer + 1], valid_f)
             stat_rows.append(jnp.sum(mlp_sq))
-        else:
-            last_part, last_middle = part, middle
-    stat_rows.append(0.0)
-    stat_rows.append(jnp.sum(valid_f))
-    stats = jnp.pad(jnp.stack(stat_rows)[None], ((0, 7), (0, 121)))
+    last_part, last_middle = mlp_part, middle
 
     def reduced(g):
         return lax.psum_scatter(g, "fsdp", scatter_dimension=0, tiled=True)
 
     base = cols_q + 2 * cols_k
     waiting = {}
+    mlp_all, attn_all = [None] * layers, [None] * layers
 
     def after(x, names):
         names = [n for n in names if n in waiting]
@@ -1127,90 +1445,111 @@
         return x
 
     for layer in reversed(range(layers)):
-        stream_in, normed_a, query, key, value, lse, mixed, middle, normed_m, gates, ups, hidden = saved[layer]
+        stream_in, normed_a, query, key, value, lse, mixed, middle, normed_m, units_kept = saved[layer]
         up_one = layer + 1
-        grad_gate, grad_up, part = [], [], 0.0
-        for t in range(tp_count):
-            wt = mlp_w[layer][t]
-            grad_hidden = dot32(down_grad, wt[:, 2 * units :], ((1,), (0,)))
-            sig = jax.nn.sigmoid(gates[t])
-            grad_gate.append((grad_hidden * ups[t] * sig * (1.0 + gates[t] * (1.0 - sig))).astype(jnp.bfloat16))
-            grad_up.append((grad_hidden * gates[t] * sig).astype(jnp.bfloat16))
-            part += dot32(grad_gate[t], wt[:, :units], ((1,), (1,)))
-            part += dot32(grad_up[t], wt[:, units : 2 * units], ((1,), (1,)))
-        part = after(part.astype(jnp.bfloat16).reshape(4, rows, width), [(up_one, "mlp")])
+        hidden = units_kept[0].reshape(tp_count, length, units)
+        if up_one == layers:
+            grad_gate, grad_up, part = units_kept[1:]
+        grad_gate = grad_gate.reshape(tp_count, length, units)
+        grad_up = grad_up.reshape(tp_count, length, units)
+        part = after(part, [(up_one, "mlp")])
         grad_mid, attn_grad, gm_rows, g_mlp = backward_step(
-            5, part, middle, gain_m[layer], grad, [normed_m, down_grad], [grad_gate, grad_up, hidden], [0, 0, 1],
+            5, part, middle, gain_m[layer], grad, [normed_m, down_grad.reshape(length, width)],
+            [[grad_gate], [grad_up], [hidden]], [0, 0, 1],
             [[(1, 0), (1, 1)], [(1, 2), (0, 0)], [(0, 1)], [(0, 2)]],
         )
         waiting[layer, "mlp"] = reduced(g_mlp)
         attn_grad = attn_grad.reshape(length, width)
-        if (up_one, "mlp") in waiting:
-            waiting[up_one, "mlp_all"] = lax.all_gather(waiting[up_one, "mlp"], "ctx", axis=0)
-        part, gqkv = attend_back(attn_grad, attn_w[layer], cosine, sine_t, bias, query, key, value, lse)
-        part = after(part.reshape(4, rows, width), [(up_one, "attn"), (up_one, "mlp_all")])
+        if layer + 1 == layers:
+            part, gqkv, output, mlp_sq = attend_back(
+                attn_grad, attn_w[layer], cosine, sine_t, bias, query, key, value, lse,
+                end=[last_part, last_middle, valid_f],
+            )
+            stat_rows += [jnp.sum(mlp_sq), jnp.sum(valid_f)]
+        else:
+            part, gqkv, mlp_all[up_one] = attend_back(
+                attn_grad, attn_w[layer], cosine, sine_t, bias, query, key, value, lse,
+                share=waiting[up_one, "mlp"],
+            )
+        part = after(part.reshape(4, rows, width), [(up_one, "attn")])
         came = backward_step(
             6 if layer else 7, part, stream_in, gain_a[layer], grad_mid, [normed_a, attn_grad], [[gqkv], [mixed]], [0, 1],
-            [[(1, 0), (1, 1)], [(0, 0), (0, 1)], [], []], other_rows=gm_rows, last=layer == 0,
+            [[(1, 0), (1, 1)], [(0, 0), (0, 1)], [], []], other_rows=gm_rows, share=None if layer else waiting[1, "attn"],
+            mlp=[*saved[layer - 1][-1][1:], mlp_w[layer - 1]] if layer else None,
         )
         if layer:
-            grad, down_grad, _, g_attn = came
-            down_grad = down_grad.reshape(length, width)
+            grad, down_grad, _, g_attn, part, grad_gate, grad_up = came
         else:
-            input_grad, _, g_attn = came
-        if (up_one, "attn") in waiting:
-            waiting[up_one, "attn_all"] = lax.all_gather(waiting[up_one, "attn"], "ctx", axis=0)
-        waiting[layer, "attn"] = reduced(after(g_attn, [(up_one, "attn_all"), (layer, "mlp")] if layer == 0 else []))
-    waiting[0, "mlp_all"] = lax.all_gather(waiting[0, "mlp"], "ctx", axis=0)
-    output, stats = end_step(last_part, last_middle, valid_f, stats)
+            input_grad, _, g_attn, attn_all[1] = came
+        if layer:
+            waiting[layer, "attn"] = reduced(g_attn)
+    stats = jnp.pad(jnp.stack(stat_rows)[None], ((0, 7), (0, 121)))
+    mlp_all[0], attn_all[0], stats = tail_step(g_attn, waiting[0, "mlp"], stats)
     rms_stats = jnp.sqrt(stats[0, : 3 * layers] / (stats[0, 3 * layers] * width)).reshape(layers, 3)
-    waiting[0, "attn_all"] = lax.all_gather(waiting[0, "attn"], "ctx", axis=0)
-    mlp_outs = place_outs(
-        [waiting[layer, "mlp_all"] for layer in range(layers)],
+    placed = place_outs(
+        attn_all, mlp_all,
+        [(0, cols_q, False), (cols_q, cols_k, False), (cols_q + cols_k, cols_k, False), (base, cols_q, True)],
         [(0, units, False), (units, units, False), (2 * units, units, True)],
-    )
-    attn_all = [waiting[layer, "attn_all"] for layer in range(layers)]
-    attn_outs = place_outs(
-        attn_all,
-        [(0, cols_q, False), (cols_q, cols_k, False), (cols_q + cols_k, cols_k, False), (base, cols_q, True)],
     )
     gain_sum = jnp.stack([
         jnp.sum(a[:, :, base + cols_q : base + cols_q + 2].astype(jnp.float32), 0) for a in attn_all
     ])
     return (
-        output, input_grad, gain_sum[:, :, 0], *attn_outs, gain_sum[:, :, 1], *mlp_outs, rms_stats,
-    )
-
-
-def place_kernel(pieces, ctx_count, *refs):
-    ins, outs = refs[:-len(pieces)], refs[-len(pieces):]
-    for layer, came in enumerate(ins):
-        for (start, size, turn), out in zip(pieces, outs):
-            for c in range(ctx_count):
-                block = came[c, :, start : start + size].astype(jnp.float32)
-                if turn:
-                    out[layer, c * size : (c + 1) * size, :] = block.T
+        output, input_grad, gain_sum[:, :, 0], *placed[:4], gain_sum[:, :, 1], *placed[4:], rms_stats,
+    )
+
+
+def place_kernel(moves, count, *refs):
+    refs = list(refs)
+    outs_count = 1 + max(out for pieces in moves for _, _, _, out, _ in pieces)
+    ins, outs = refs[:count], refs[count : count + outs_count]
+    held = refs[count + outs_count : 2 * count + outs_count]
+    laid = refs[2 * count + outs_count : -2]
+    in_sems, out_sems = refs[-2:]
+    loads = [pltpu.make_async_copy(ins[n], held[n], in_sems.at[n]) for n in range(count)]
+    for load in loads:
+        load.start()
+    stores = []
+    for n, pieces in enumerate(moves):
+        loads[n].wait()
+        for start, size, flip, out, layer in pieces:
+            for c in range(held[n].shape[0]):
+                block = held[n][c, :, start : start + size].astype(jnp.float32)
+                if flip:
+                    laid[out][layer, c * size : (c + 1) * size, :] = block.T
                 else:
-                    out[layer, :, c * size : (c + 1) * size] = block
-
-
-def place_outs(came, pieces):
-    ctx_count, depth, _ = came[0].shape
-    layers = len(came)
-    shapes = [
-        jax.ShapeDtypeStruct(
-            (layers, ctx_count * size, depth) if turn else (layers, depth, ctx_count * size), jnp.float32
-        )
-        for _, size, turn in pieces
-    ]
-    vmem = pl.BlockSpec(memory_space=pltpu.VMEM)
+                    laid[out][layer, :, c * size : (c + 1) * size] = block
+            store = pltpu.make_async_copy(laid[out].at[layer], outs[out].at[layer], out_sems.at[len(stores)])
+            store.start()
+            stores.append(store)
+    for store in stores:
+        store.wait()
+
+
+def place_outs(attn_all, mlp_all, attn_pieces, mlp_pieces):
+    layers = len(attn_all)
+    shapes = []
+    for came, pieces in ((attn_all, attn_pieces), (mlp_all, mlp_pieces)):
+        ctx_count, depth, _ = came[0].shape
+        for _, size, flip in pieces:
+            wide = ctx_count * size
+            shapes.append((layers, wide, depth) if flip else (layers, depth, wide))
+    ins, moves = [], []
+    for layer in reversed(range(layers)):
+        for came, pieces, base in ((mlp_all, mlp_pieces, len(attn_pieces)), (attn_all, attn_pieces, 0)):
+            ins.append(came[layer])
+            moves.append([(*piece, base + n, layer) for n, piece in enumerate(pieces)])
+    hbm = pl.BlockSpec(memory_space=pl.ANY)
     return pl.pallas_call(
-        functools.partial(place_kernel, pieces, ctx_count),
-        out_shape=shapes,
-        in_specs=[vmem] * layers,
-        out_specs=[vmem] * len(shapes),
+        functools.partial(place_kernel, moves, len(ins)),
+        out_shape=[jax.ShapeDtypeStruct(s, jnp.float32) for s in shapes],
+        in_specs=[hbm] * len(ins),
+        out_specs=[hbm] * len(shapes),
+        scratch_shapes=[pltpu.VMEM(a.shape, a.dtype) for a in ins]
+        + [pltpu.VMEM(s, jnp.float32) for s in shapes]
+        + [pltpu.SemaphoreType.DMA((len(ins),)), pltpu.SemaphoreType.DMA((sum(len(m) for m in moves),))],
         compiler_params=pltpu.CompilerParams(vmem_limit_bytes=60 << 20),
-    )(*came)
+    )(*ins)
 
 
 def fits(mesh):

time: 1050 us -> 945 us (0.900)
  matrix products: 95.8 us -> 0 us
  Pallas kernels: 722 us -> 797 us
  local copies, waits for them, and re-layouts: 63.9 us -> 26.5 us
  waiting for transfers between devices: 115 us -> 78.9 us
  other arithmetic: 31.8 us -> 17.6 us
    pallas_call x10 -> x12, Pallas kernels: 575 us -> 754 us  [linked_call(): pl.pallas_call(kernel, out_shape=out_shape, in_specs=[vmem] * len(args) +...]
    pallas_call x4 -> x1, Pallas kernels: 130 us -> 30.5 us  [local_call(): pl.pallas_call(kernel, out_shape=out_shape, in_specs=[vmem] * len(args),...]
    dot_general x24 -> x0, matrix products: 95.8 us -> none  [dot32(): lax.dot_general(a, b, (dims, ((), ())), preferred_element_type=jnp.float32)]
    all_gather x4, waiting for transfers between devices: 0.07 us -> 78.2 us  [whole(): lax.all_gather(w, ('tp', 'fsdp'), axis=0, tiled=True)]
    reduce_scatter x4 -> x3, waiting for transfers between devices: 63.9 us -> 0.04 us  [reduced(): return lax.psum_scatter(g, 'fsdp', scatter_dimension=0, tiled=True)]
    all_gather x5 -> x0, waiting for transfers between devices: 50.1 us -> none  [the longest x1 36.5 us: planned(): lax.all_gather(waiting[up_one, 'attn'], 'ctx', axis=0)]
    all_gather x2 -> x0, local copies, waits for them, and re-layouts: 21.7 us -> none  [whole(): lax.all_gather(w, ('tp', 'fsdp'), axis=0, tiled=True)]
    dynamic_slice x16 -> x8, local copies, waits for them, and re-layouts: 12.8 us -> 1.88 us  [cut(): return lax.dynamic_slice_in_dim(w, me * count, count, axis)]
  transfers between devices with their start and end apart: 13 -> 7, of which waited for: 4 -> 2; matrix products, arithmetic and copies ran while one was open for 14% -> 3% of each run, Pallas kernels for 61% -> 52%
where the time goes in v3:
time: 945 us; the launch traced here: 936 us
  Pallas kernels  797 us (84%)
  waiting for transfers between devices  78.9 us (8%)
  local copies, waits for them, and re-layouts  26.5 us (3%)
  other arithmetic  17.6 us (2%)
  between operations  15.7 us (2%)
    pallas_call x12, Pallas kernels, linked_call(): pl.pallas_call(kernel, out_shape=out_shape, in_specs=[vmem] * len(args) +...  754 us
    all_gather x4, waiting for transfers between devices, whole(): lax.all_gather(w, ('tp', 'fsdp'), axis=0, tiled=True)  78.2 us
    pallas_call x1, Pallas kernels, local_call(): pl.pallas_call(kernel, out_shape=out_shape, in_specs=[vmem] * len(args),...  30.5 us
  transfers between devices with their start and end apart: 7, of which 2 were waited for; matrix products, arithmetic and copies ran while one was open for 3% of the time, Pallas kernels for 52%

profile of v3, /device:TPU:0, one launch (start us, length us, event | category | flops | bytes accessed | tf_op | source)
XLA Modules:
  0.0 936.0 jit_solution(1234665559914602177)
XLA Ops:
  7.3 1.9 fusion.15
  9.2 1.9 fusion.14
  11.7 1.2 dynamic-slice_bitcast_fusion.6
  12.9 1.1 concatenate.16
  16.0 4.0 fusion.10
  20.0 49.2 %shard_map.229 = (f32[4,8,384]{2,1,0:T(8,128)}, s32[4,288,8]{2,1,0:T(8,128)}, bf16[4,288,1536]{2,1,0:T(8,128)(2,1)}, bf16[1152,1152]{1,0:T(8,128)(2,1)}, bf16[2,384,1536]{2,1,0:T(8,128)(2,1)}) custom-call(f32[8,384]{1,0:T(8,128)} %fusion.6.gains, s32[288,8]{1,0:T(8,128)} %pad.16.places, s32[1,2]{1,0:T(1,128)} %constant_dynamic-slice_fusion.2.starts, ...), custom_call_target="tpu_custom_call" | custom-call | bytes 136800000 | tf_op jit(solution)/shard_map/pallas_call | solution.py:997
  69.2 3.2 slice_bitcast_fusion
  74.1 1.1 concatenate.19
  75.8 2.1 fusion.2
  80.0 40.1 %shard_map.230 = (bf16[1152,1536]{1,0:T(8,128)(2,1)}, bf16[2,9,256,96]{3,2,1,0:T(8,128)(2,1)}, bf16[2,1152,96]{2,1,0:T(8,128)(2,1)}, bf16[2,1152,96]{2,1,0:T(8,1...) custom-call(bf16[1152,1536]{1,0:T(8,128)(2,1)} %bitcast.84, ...), custom_call_target="tpu_custom_call" | custom-call | bytes 126000000 | tf_op jit(solution)/shard_map/pallas_call | solution.py:997
  120.1 41.3 %all-gather.12.cloned.1.call-done = bf16[1,3072,1536]{2,1,0:T(8,128)(2,1)} async-done(((bf16[1,384,1536]{2,1,0:T(8,128)(2,1)}), bf16[1,3072,1536]{2,1,0:T(8,128)(2,1)}) %all-gather.12.cloned.1.call-update) | async-done | bytes 9437200 | tf_op jit(solution)/shard_map/all_gather | solution.py:1360
  161.4 72.6 %shard_map.231 = (f32[288,1536]{1,0:T(8,128)}, bf16[4,288,1536]{2,1,0:T(8,128)(2,1)}, f32[288,1]{1,0:T(8,128)}, bf16[4,288,1536]{2,1,0:T(8,128)(2,1)}, bf16[2,4,...) custom-call(bf16[4,288,1536]{2,1,0:T(8,128)(2,1)} %bitcast.93, ...), custom_call_target="tpu_custom_call" | custom-call | bytes 270000000 | tf_op jit(solution)/shard_map/pallas_call | solution.py:997
  234.7 66.0 %shard_map.232 = (f32[288,1536]{1,0:T(8,128)}, bf16[4,288,1536]{2,1,0:T(8,128)(2,1)}, f32[288,1]{1,0:T(8,128)}) custom-call(bf16[4,288,1536]{2,1,0:T(8,128)(2,1)} %get-tuple-element.95.part, f32[288,1536]{1,0:T(8,128)} %get-tuple-element.96.stream.refs_1_, f32[1,1536]{1,0:T(1,128)} %bitcast.111, f32[288,1]{1,0:T(8,128)} %convert_element_type.54.valid.refs_11_), custom_call_target="tpu_custom_call" | custom-call | bytes 234000000 | tf_op jit(solution)/shard_map/pallas_call | solution.py:997
  300.7 30.5 %shard_map.233 = (bf16[1152,1536]{1,0:T(8,128)(2,1)}, bf16[2,9,256,96]{3,2,1,0:T(8,128)(2,1)}, bf16[2,1152,96]{2,1,0:T(8,128)(2,1)}, bf16[2,1152,96]{2,1,0:T(8,1...) custom-call(bf16[1152,1536]{1,0:T(8,128)(2,1)} %bitcast.80, bf16[2,1536,640]{2,1,0:T(8,128)(2,1)} %bitcast.76, ...), custom_call_target="tpu_custom_call" | custom-call | bytes 108000000 | tf_op jit(solution)/shard_map/pallas_call | solution.py:1280
  331.2 36.8 %all-gather.10.cloned.1.call-done = bf16[3072,1536]{1,0:T(8,128)(2,1)} async-done(((bf16[384,1536]{1,0:T(8,128)(2,1)}), bf16[3072,1536]{1,0:T(8,128)(2,1)}) %all-gather.10.cloned.1.call-update) | async-done | bytes 9437200 | tf_op jit(solution)/shard_map/all_gather | solution.py:1360
  368.1 84.9 %shard_map.234 = (f32[288,1536]{1,0:T(8,128)}, bf16[4,288,1536]{2,1,0:T(8,128)(2,1)}, f32[288,1]{1,0:T(8,128)}, bf16[4,288,1536]{2,1,0:T(8,128)(2,1)}, bf16[2,4,...) custom-call(bf16[4,288,1536]{2,1,0:T(8,128)(2,1)} %bitcast.92, ...), custom_call_target="tpu_custom_call" | custom-call | bytes 270000000 | tf_op jit(solution)/shard_map/pallas_call | solution.py:997
  453.0 69.3 %shard_map.235 = (f32[288,1536]{1,0:T(8,128)}, bf16[4,288,1536]{2,1,0:T(8,128)(2,1)}, f32[16,1536]{1,0:T(8,128)}, bf16[1536,1536]{1,0:T(8,128)(2,1)}) custom-call(bf16[4,288,1536]{2,1,0:T(8,128)(2,1)} %get-tuple-element.104.refs_0_, f32[288,1536]{1,0:T(8,128)} %get-tuple-element.105.refs_1_.refs_10_, f32[1,1536]{1,0:T(1,128)} %bitcast.108, ...), custom_call_target="tpu_custom_call" | custom-call | bytes 234000000 | tf_op jit(solution)/shard_map/pallas_call | solution.py:997
  522.4 47.9 %shard_map.236 = (bf16[1152,1536]{1,0:T(8,128)(2,1)}, bf16[2,1152,384]{2,1,0:T(8,128)(2,1)}, bf16[2,288,1536]{2,1,0:T(8,128)(2,1)}, f32[288,1]{1,0:T(8,128)}) custom-call(bf16[1152,1536]{1,0:T(8,128)(2,1)} %bitcast.82, bf16[2,1536,640]{2,1,0:T(8,128)(2,1)} %bitcast.77, f32[1152,96]{1,0:T(8,128)} %pad_maximum_fusion.cos_ref.refs_2_, ...), custom_call_target="tpu_custom_call" | custom-call | bytes 144000000 | tf_op jit(solution)/shard_map/pallas_call | solution.py:997
  570.3 79.7 %shard_map.237 = (f32[288,1536]{1,0:T(8,128)}, bf16[4,288,1536]{2,1,0:T(8,128)(2,1)}, f32[16,1536]{1,0:T(8,128)}, bf16[1536,640]{1,0:T(8,128)(2,1)}, bf16[4,288,...) custom-call(bf16[4,288,1536]{2,1,0:T(8,128)(2,1)} %bitcast.90, ...), custom_call_target="tpu_custom_call" | custom-call | bytes 234000000 | tf_op jit(solution)/shard_map/pallas_call | solution.py:997
  650.2 70.4 %shard_map.238 = (f32[288,1536]{1,0:T(8,128)}, bf16[4,288,1536]{2,1,0:T(8,128)(2,1)}, f32[16,1536]{1,0:T(8,128)}, bf16[1536,1536]{1,0:T(8,128)(2,1)}) custom-call(bf16[4,288,1536]{2,1,0:T(8,128)(2,1)} %get-tuple-element.126.refs_0_, f32[288,1536]{1,0:T(8,128)} %get-tuple-element.96.stream.refs_1_, f32[1,1536]{1,0:T(1,128)} %bitcast.110, ...), custom_call_target="tpu_custom_call" | custom-call | bytes 234000000 | tf_op jit(solution)/shard_map/pallas_call | solution.py:997
  722.7 1.5 fusion.1
  725.6 4.6 stack.52
  730.8 49.5 %shard_map.239 = (bf16[1152,1536]{1,0:T(8,128)(2,1)}, bf16[2,1152,384]{2,1,0:T(8,128)(2,1)}, bf16[4,384,1536]{2,1,0:T(8,128)(2,1)}) custom-call(bf16[1152,1536]{1,0:T(8,128)(2,1)} %bitcast.86, bf16[2,1536,640]{2,1,0:T(8,128)(2,1)} %bitcast.79, f32[1152,96]{1,0:T(8,128)} %pad_maximum_fusion.cos_ref.refs_2_, f32[1152,96]{1,0:T(8,128)} %pad_maximum_fusion.1.sin_ref.refs_3_, ...), custom_call_target="tpu_custom_call" | custom-call | bytes 144000000 | tf_op jit(solution)/shard_map/pallas_call | solution.py:997
  780.3 55.3 %shard_map.240 = (f32[2,288,1536]{2,1,0:T(8,128)}, f32[16,1536]{1,0:T(8,128)}, bf16[1536,640]{1,0:T(8,128)(2,1)}, bf16[4,384,640]{2,1,0:T(8,128)(2,1)}) custom-call(bf16[4,288,1536]{2,1,0:T(8,128)(2,1)} %bitcast.91, f32[288,1536]{1,0:T(8,128)} %get-tuple-element.193.stream.refs_1_, f32[1,1536]{1,0:T(1,128)} %bitcast.113, ...), custom_call_target="tpu_custom_call" | custom-call | bytes 126000000 | tf_op jit(solution)/shard_map/pallas_call | solution.py:997
  835.5 1.2 convert_reduce_fusion
  836.8 68.8 %shard_map.241 = (bf16[4,384,1536]{2,1,0:T(8,128)(2,1)}, bf16[4,384,640]{2,1,0:T(8,128)(2,1)}, f32[8,128]{1,0:T(8,128)}) custom-call(bf16[1536,640]{1,0:T(8,128)(2,1)} %get-tuple-element.148.summed, bf16[384,1536]{1,0:T(8,128)(2,1)} %reduce-scatter.8.cloned.1.call-done.share, f32[8,128]{1,0:T(8,128)} %pad.17.stats), custom_call_target="tpu_custom_call" | custom-call | bytes 216000000 | tf_op jit(solution)/shard_map/pallas_call | solution.py:997
  905.7 1.3 slice.99
  908.9 1.2 convert_reduce_fusion.1
  911.4 12.8 %shard_map.242 = (f32[2,384,768]{2,1,0:T(8,128)}, f32[2,384,384]{2,1,0:T(8,128)}, f32[2,384,384]{2,1,0:T(8,128)}, f32[2,768,384]{2,1,0:T(8,128)}, f32[2,384,2048...) custom-call(bf16[4,384,1536]{2,1,0:T(8,128)(2,1)} %get-tuple-element.156.refs_0_, ...), custom_call_target="tpu_custom_call" | custom-call | tf_op jit(solution)/shard_map/pallas_call | solution.py:1543
  924.3 1.2 copy.55
  925.5 1.4 copy-done.4
  926.9 1.8 copy.56
  (92 shorter events, 14.5 us)
Async XLA Ops:
  7.2 7.7 copy-start
  7.2 3.9 copy-start.6
  7.2 72.8 %all-gather.6.cloned.1.call-start = ((), (), s32[]{:S(2)}) async-start(), calls=%async_computation.3 | async-start | bytes 4423680 | tf_op jit(solution)/shard_map/all_gather | solution.py:1360
  9.2 2.0 copy-start.7
  11.3 2.7 copy-start.14
  11.3 2.7 copy-start.17
  11.3 4.1 copy-start.15
  11.3 4.0 copy-start.16
  13.9 147.5 %all-gather.12.cloned.1.call-start = ((), (), s32[]{:S(2)}) async-start(), calls=%async_computation.9 | async-start | bytes 10616832 | tf_op jit(solution)/shard_map/all_gather | solution.py:1360
  72.4 1.1 copy-start.8
  72.4 2.8 copy-start.13
  72.4 228.3 %all-gather.8.cloned.1.call-start = ((), (), s32[]{:S(2)}) async-start(), calls=%async_computation.4 | async-start | bytes 4423680 | tf_op jit(solution)/shard_map/all_gather | solution.py:1360
  234.0 134.0 %all-gather.10.cloned.1.call-start = ((), (), s32[]{:S(2)}) async-start(), calls=%async_computation.5 | async-start | bytes 10616832 | tf_op jit(solution)/shard_map/all_gather | solution.py:1360
  234.6 415.6 %reduce-scatter.4.cloned.1.call-start = ((), (), s32[]{:S(2)}) async-start(), calls=%async_computation.6 | async-start | bytes 5898240 | tf_op jit(solution)/shard_map/reduce_scatter | solution.py:1432
  522.3 257.9 %reduce-scatter.6.cloned.1.call-start = ((), (), s32[]{:S(2)}) async-start(), calls=%async_computation.7 | async-start | bytes 2457600 | tf_op jit(solution)/shard_map/reduce_scatter | solution.py:1432
  650.1 186.7 %reduce-scatter.8.cloned.1.call-start = ((), (), s32[]{:S(2)}) async-start(), calls=%async_computation.8 | async-start | bytes 5898240 | tf_op jit(solution)/shard_map/reduce_scatter | solution.py:1432
  720.5 0.9 copy-start.9
  720.6 1.5 copy-start.10
  720.6 2.2 copy-start.2
  720.6 2.2 copy-start.3
  720.6 3.7 copy-start.11
  720.6 4.3 copy-start.12
  911.4 12.9 %copy-start.5 = (bf16[2,288,1536]{2,1,0:T(8,128)(2,1)S(1)}, bf16[2,288,1536]{2,1,0:T(8,128)(2,1)}, u32[]{:S(2)}) copy-start(bf16[2,288,1536]{2,1,0:T(8,128)(2,1)} %get-tuple-element.211) | copy-start | bytes 5308420
  924.3 2.6 copy-start.4
  924.3 4.4 copy-start.1
Sparse Core Ops, SparseCore 0:
  14.1 48.4 all-gather.5
  72.5 88.8 all-gather.11
  234.2 42.2 all-gather.7
  278.5 89.5 all-gather.9
  522.5 83.7 reduce-scatter.3
  650.2 39.0 reduce-scatter.5
  720.7 82.8 reduce-scatter.7

commit v4 on v0

--- a/solution.py
+++ b/solution.py
@@ -1,7 +1,15 @@
+import functools
+
 import jax
 import jax.numpy as jnp
 from jax import lax
+from jax.experimental import pallas as pl
+from jax.experimental.layout import Layout, with_layout_constraint
+from jax.experimental.pallas import tpu as pltpu
 from jax.sharding import PartitionSpec as P
+
+MESH = pl.DeviceIdType.MESH
+FSDP, CTX, TP = "fsdp", "ctx", "tp"
 
 HEADS = 16
 KV_HEADS = 8
@@ -53,7 +61,7 @@
     return jnp.where(allowed[:, None, None], raw_scores, neg_big)
 
 
-def local(
+def general(
     tokens,
     positions,
     valid,
@@ -71,13 +79,13 @@
 ):
     seq_count, shard_len, model_width = tokens.shape
     tok_rows = seq_count * shard_len
-    tp_count = lax.axis_size("tp")
+    tp_count = lax.axis_size(TP)
     local_heads = HEADS // tp_count
     local_kv = KV_HEADS // tp_count
     group_size = HEADS // KV_HEADS
     score_scale = HEAD_DIM ** (-0.5)
-    seq_length = shard_len * lax.axis_size("ctx")
-    start_tok = lax.axis_index("ctx") * shard_len
+    seq_length = shard_len * lax.axis_size(CTX)
+    start_tok = lax.axis_index(CTX) * shard_len
     query_index = start_tok + jnp.arange(shard_len, dtype=jnp.int32)
     key_index = jnp.arange(seq_length, dtype=jnp.int32)
     cosine, sine_t = rope_tables(positions, HEAD_DIM)
@@ -97,15 +105,15 @@
     stat_rows = []
     for layer_no in range(layer_count):
         weights = (
-            lax.all_gather(attn_gain[layer_no], "fsdp", axis=0, tiled=True),
-            lax.all_gather(w_query[layer_no], "fsdp", axis=0, tiled=True),
-            lax.all_gather(w_key[layer_no], "fsdp", axis=0, tiled=True),
-            lax.all_gather(w_value[layer_no], "fsdp", axis=0, tiled=True),
-            lax.all_gather(w_out[layer_no], "fsdp", axis=1, tiled=True),
-            lax.all_gather(mlp_gain[layer_no], "fsdp", axis=0, tiled=True),
-            lax.all_gather(w_gate[layer_no], "fsdp", axis=0, tiled=True),
-            lax.all_gather(w_up[layer_no], "fsdp", axis=0, tiled=True),
-            lax.all_gather(w_down[layer_no], "fsdp", axis=1, tiled=True),
+            lax.all_gather(attn_gain[layer_no], FSDP, axis=0, tiled=True),
+            lax.all_gather(w_query[layer_no], FSDP, axis=0, tiled=True),
+            lax.all_gather(w_key[layer_no], FSDP, axis=0, tiled=True),
+            lax.all_gather(w_value[layer_no], FSDP, axis=0, tiled=True),
+            lax.all_gather(w_out[layer_no], FSDP, axis=1, tiled=True),
+            lax.all_gather(mlp_gain[layer_no], FSDP, axis=0, tiled=True),
+            lax.all_gather(w_gate[layer_no], FSDP, axis=0, tiled=True),
+            lax.all_gather(w_up[layer_no], FSDP, axis=0, tiled=True),
+            lax.all_gather(w_down[layer_no], FSDP, axis=1, tiled=True),
         )
         gain_a, w_q, w_k, w_v, w_o, gain_m, w_g, w_u, w_d = weights
         normed_a = normalize(stream, gain_a).astype(jnp.bfloat16)
@@ -131,9 +139,9 @@
             .reshape(seq_count, shard_len, local_kv * HEAD_DIM)
         )
         key_all, value_all, valid_all = (
-            lax.all_gather(key_local, "ctx", axis=1, tiled=True),
-            lax.all_gather(value_local, "ctx", axis=1, tiled=True),
-            lax.all_gather(valid.astype(jnp.bfloat16), "ctx", axis=1, tiled=True),
+            lax.all_gather(key_local, CTX, axis=1, tiled=True),
+            lax.all_gather(value_local, CTX, axis=1, tiled=True),
+            lax.all_gather(valid.astype(jnp.bfloat16), CTX, axis=1, tiled=True),
         )
         allowed = (causal[None] | same_piece) & ((valid_all[:, None, :] > 0.5) | diagonal[None])
         key_heads = key_all.reshape(seq_count, seq_length, local_kv, HEAD_DIM)
@@ -149,7 +157,7 @@
         )
         mixed_b = mixed_heads.astype(jnp.bfloat16).reshape(tok_rows, local_heads * HEAD_DIM)
         attn_branch = lax.psum(
-            jnp.dot(mixed_b, w_o, preferred_element_type=jnp.float32).astype(jnp.bfloat16), "tp"
+            jnp.dot(mixed_b, w_o, preferred_element_type=jnp.float32).astype(jnp.bfloat16), TP
         ).astype(jnp.float32)
         middle = stream + attn_branch
         normed_m = normalize(middle, gain_m).astype(jnp.bfloat16)
@@ -157,7 +165,7 @@
         up_act = jnp.dot(normed_m, w_u, preferred_element_type=jnp.float32)
         hidden = (jax.nn.silu(gate_act) * up_act).astype(jnp.bfloat16)
         mlp_branch = lax.psum(
-            jnp.dot(hidden, w_d, preferred_element_type=jnp.float32).astype(jnp.bfloat16), "tp"
+            jnp.dot(hidden, w_d, preferred_element_type=jnp.float32).astype(jnp.bfloat16), TP
         ).astype(jnp.float32)
         stat_rows.append(
             jnp.stack(
@@ -190,7 +198,7 @@
         stream = middle + mlp_branch
     output = stream.astype(jnp.bfloat16).reshape(seq_count, shard_len, model_width)
     total_squares, total_count = lax.psum(
-        (jnp.stack(stat_rows), jnp.sum(valid_flat)), ("fsdp", "ctx")
+        (jnp.stack(stat_rows), jnp.sum(valid_flat)), (FSDP, CTX)
     )
     rms_stats = jnp.sqrt(total_squares / (total_count * model_width))
     grad_stream = d_out.astype(jnp.float32).reshape(tok_rows, model_width)
@@ -213,15 +221,15 @@
             kept_weights,
         ) = saved[layer_no]
         weights = (
-            lax.all_gather(attn_gain[layer_no], "fsdp", axis=0, tiled=True),
-            lax.all_gather(w_query[layer_no], "fsdp", axis=0, tiled=True),
-            lax.all_gather(w_key[layer_no], "fsdp", axis=0, tiled=True),
-            lax.all_gather(w_value[layer_no], "fsdp", axis=0, tiled=True),
-            lax.all_gather(w_out[layer_no], "fsdp", axis=1, tiled=True),
-            lax.all_gather(mlp_gain[layer_no], "fsdp", axis=0, tiled=True),
-            lax.all_gather(w_gate[layer_no], "fsdp", axis=0, tiled=True),
-            lax.all_gather(w_up[layer_no], "fsdp", axis=0, tiled=True),
-            lax.all_gather(w_down[layer_no], "fsdp", axis=1, tiled=True),
+            lax.all_gather(attn_gain[layer_no], FSDP, axis=0, tiled=True),
+            lax.all_gather(w_query[layer_no], FSDP, axis=0, tiled=True),
+            lax.all_gather(w_key[layer_no], FSDP, axis=0, tiled=True),
+            lax.all_gather(w_value[layer_no], FSDP, axis=0, tiled=True),
+            lax.all_gather(w_out[layer_no], FSDP, axis=1, tiled=True),
+            lax.all_gather(mlp_gain[layer_no], FSDP, axis=0, tiled=True),
+            lax.all_gather(w_gate[layer_no], FSDP, axis=0, tiled=True),
+            lax.all_gather(w_up[layer_no], FSDP, axis=0, tiled=True),
+            lax.all_gather(w_down[layer_no], FSDP, axis=1, tiled=True),
         )
         gain_a, w_q, w_k, w_v, w_o, gain_m, w_g, w_u, w_d = weights
         grad_mlp = grad_stream.astype(jnp.bfloat16)
@@ -237,7 +245,7 @@
                 jnp.einsum("rf,df->rd", grad_gate, w_g, preferred_element_type=jnp.float32)
                 + jnp.einsum("rf,df->rd", grad_up, w_u, preferred_element_type=jnp.float32)
             ).astype(jnp.bfloat16),
-            "tp",
+            TP,
         ).astype(jnp.float32)
         g_gate = jnp.einsum("rd,rf->df", normed_m, grad_gate, preferred_element_type=jnp.float32)
         g_up = jnp.einsum("rd,rf->df", normed_m, grad_up, preferred_element_type=jnp.float32)
@@ -279,7 +287,7 @@
                 grad_key_all.reshape(seq_count, seq_length, local_kv * HEAD_DIM).astype(
                     jnp.bfloat16
                 ),
-                "ctx",
+                CTX,
                 scatter_dimension=1,
                 tiled=True,
             ).astype(jnp.float32),
@@ -287,7 +295,7 @@
                 grad_value_all.reshape(seq_count, seq_length, local_kv * HEAD_DIM).astype(
                     jnp.bfloat16
                 ),
-                "ctx",
+                CTX,
                 scatter_dimension=1,
                 tiled=True,
             ).astype(jnp.float32),
@@ -307,7 +315,7 @@
                 + jnp.einsum("rh,dh->rd", grad_key_b, w_k, preferred_element_type=jnp.float32)
                 + jnp.einsum("rh,dh->rd", grad_value_b, w_v, preferred_element_type=jnp.float32)
             ).astype(jnp.bfloat16),
-            "tp",
+            TP,
         ).astype(jnp.float32)
         g_query = jnp.einsum(
             "rd,rh->dh", normed_a, grad_query_b, preferred_element_type=jnp.float32
@@ -320,42 +328,42 @@
         grad_stream = grad_middle + grad_from_attn_norm
         grad_terms = (g_gain_a, g_query, g_key, g_value, g_out, g_gain_m, g_gate, g_up, g_down)
         shares = (
-            lax.psum_scatter(grad_terms[0], ("fsdp", "ctx"), scatter_dimension=0, tiled=True),
-            lax.psum_scatter(grad_terms[1], ("fsdp", "ctx"), scatter_dimension=0, tiled=True),
-            lax.psum_scatter(grad_terms[2], ("fsdp", "ctx"), scatter_dimension=0, tiled=True),
-            lax.psum_scatter(grad_terms[3], ("fsdp", "ctx"), scatter_dimension=0, tiled=True),
-            lax.psum_scatter(grad_terms[4], ("fsdp", "ctx"), scatter_dimension=1, tiled=True),
-            lax.psum_scatter(grad_terms[5], ("fsdp", "ctx"), scatter_dimension=0, tiled=True),
-            lax.psum_scatter(grad_terms[6], ("fsdp", "ctx"), scatter_dimension=0, tiled=True),
-            lax.psum_scatter(grad_terms[7], ("fsdp", "ctx"), scatter_dimension=0, tiled=True),
-            lax.psum_scatter(grad_terms[8], ("fsdp", "ctx"), scatter_dimension=1, tiled=True),
+            lax.psum_scatter(grad_terms[0], (FSDP, CTX), scatter_dimension=0, tiled=True),
+            lax.psum_scatter(grad_terms[1], (FSDP, CTX), scatter_dimension=0, tiled=True),
+            lax.psum_scatter(grad_terms[2], (FSDP, CTX), scatter_dimension=0, tiled=True),
+            lax.psum_scatter(grad_terms[3], (FSDP, CTX), scatter_dimension=0, tiled=True),
+            lax.psum_scatter(grad_terms[4], (FSDP, CTX), scatter_dimension=1, tiled=True),
+            lax.psum_scatter(grad_terms[5], (FSDP, CTX), scatter_dimension=0, tiled=True),
+            lax.psum_scatter(grad_terms[6], (FSDP, CTX), scatter_dimension=0, tiled=True),
+            lax.psum_scatter(grad_terms[7], (FSDP, CTX), scatter_dimension=0, tiled=True),
+            lax.psum_scatter(grad_terms[8], (FSDP, CTX), scatter_dimension=1, tiled=True),
         )
         results[layer_no] = (
-            lax.all_gather(shares[0].astype(jnp.bfloat16), "ctx", axis=0, tiled=True).astype(
+            lax.all_gather(shares[0].astype(jnp.bfloat16), CTX, axis=0, tiled=True).astype(
                 jnp.float32
             ),
-            lax.all_gather(shares[1].astype(jnp.bfloat16), "ctx", axis=0, tiled=True).astype(
+            lax.all_gather(shares[1].astype(jnp.bfloat16), CTX, axis=0, tiled=True).astype(
                 jnp.float32
             ),
-            lax.all_gather(shares[2].astype(jnp.bfloat16), "ctx", axis=0, tiled=True).astype(
+            lax.all_gather(shares[2].astype(jnp.bfloat16), CTX, axis=0, tiled=True).astype(
                 jnp.float32
             ),
-            lax.all_gather(shares[3].astype(jnp.bfloat16), "ctx", axis=0, tiled=True).astype(
+            lax.all_gather(shares[3].astype(jnp.bfloat16), CTX, axis=0, tiled=True).astype(
                 jnp.float32
             ),
-            lax.all_gather(shares[4].astype(jnp.bfloat16), "ctx", axis=1, tiled=True).astype(
+            lax.all_gather(shares[4].astype(jnp.bfloat16), CTX, axis=1, tiled=True).astype(
                 jnp.float32
             ),
-            lax.all_gather(shares[5].astype(jnp.bfloat16), "ctx", axis=0, tiled=True).astype(
+            lax.all_gather(shares[5].astype(jnp.bfloat16), CTX, axis=0, tiled=True).astype(
                 jnp.float32
             ),
-            lax.all_gather(shares[6].astype(jnp.bfloat16), "ctx", axis=0, tiled=True).astype(
+            lax.all_gather(shares[6].astype(jnp.bfloat16), CTX, axis=0, tiled=True).astype(
                 jnp.float32
             ),
-            lax.all_gather(shares[7].astype(jnp.bfloat16), "ctx", axis=0, tiled=True).astype(
+            lax.all_gather(shares[7].astype(jnp.bfloat16), CTX, axis=0, tiled=True).astype(
                 jnp.float32
             ),
-            lax.all_gather(shares[8].astype(jnp.bfloat16), "ctx", axis=1, tiled=True).astype(
+            lax.all_gather(shares[8].astype(jnp.bfloat16), CTX, axis=1, tiled=True).astype(
                 jnp.float32
             ),
         )
@@ -380,35 +388,1346 @@
     )
 
 
+def partners():
+    me = lax.axis_index(CTX)
+    return me, me ^ 1, me ^ 2, me ^ 3
+
+
+def greet(*places):
+    barrier = pltpu.get_barrier_semaphore()
+    for place in places:
+        pl.semaphore_signal(barrier, inc=1, device_id=place, device_id_type=MESH)
+    pl.semaphore_wait(barrier, len(places))
+
+
+def send(src, dst, sems, slot, place):
+    copy = pltpu.make_async_remote_copy(
+        src_ref=src,
+        dst_ref=dst,
+        send_sem=sems[0].at[slot],
+        recv_sem=sems[1].at[slot],
+        device_id=place,
+        device_id_type=MESH,
+    )
+    copy.start()
+    return copy
+
+
+def run(steps, work=()):
+    for n, _ in enumerate(steps):
+        if n < len(work):
+            work[n]()
+
+
+def gather_rows(full, sems, place, own):
+    me, side_x, side_y, _ = place
+    to_x, to_y = {CTX: side_x}, {CTX: side_y}
+    half = full.shape[1] // 2
+    top, low = pl.ds(0, half), pl.ds(half, half)
+    first = [
+        send(own.at[top], full.at[me, top], sems, 0, to_x),
+        send(own.at[low], full.at[me, low], sems, 1, to_y),
+    ]
+    rest = [
+        send(own.at[top], full.at[me, top], sems, 2, to_y),
+        send(own.at[low], full.at[me, low], sems, 3, to_x),
+    ]
+    yield
+    first[0].wait_recv()
+    rest.append(send(full.at[side_x, top], full.at[side_x, top], sems, 4, to_y))
+    first[1].wait_recv()
+    rest.append(send(full.at[side_y, low], full.at[side_y, low], sems, 5, to_x))
+    yield
+    rest[0].wait_recv()
+    rest[1].wait_recv()
+    yield
+    rest[2].wait_recv()
+    rest[3].wait_recv()
+    for copy in first + rest:
+        copy.wait_send()
+
+
+def dot32(a, b, dims):
+    return lax.dot_general(a, b, (dims, ((), ())), preferred_element_type=jnp.float32)
+
+
+def start_kernel(r):
+    place = partners()
+    me, side_x, side_y, across = place
+    groups = (
+        (FSDP, r.gains, r.all_gains, (r.gain_send, r.gain_recv)),
+        (CTX, r.places, r.all_places, (r.place_send, r.place_recv)),
+    )
+    peers = []
+    for axis, _, _, _ in groups:
+        count = lax.axis_size(axis)
+        peers.append([lax.rem(lax.axis_index(axis) + step, count) for step in range(1, count)])
+    full = r.full
+    own = pltpu.make_async_copy(r.x.at[lax.axis_index(TP)], full.at[me], r.load.at[0])
+    own.start()
+    greet(*[{groups[n][0]: peer} for n in range(2) for peer in peers[n]])
+    copies = []
+    for n, (axis, src, dst, sems) in enumerate(groups):
+        mine = pltpu.make_async_copy(src, dst.at[lax.axis_index(axis)], r.load.at[1 + n])
+        mine.start()
+        for step, peer in enumerate(peers[n]):
+            copies.append(send(src, dst.at[lax.axis_index(axis)], sems, step, {axis: peer}))
+        mine.wait()
+    packed = [getattr(r, f"packed_{layer}") for layer in range(r.gate.shape[0])]
+    layers, units = len(packed), r.turned.shape[1]
+    loads = []
+    for layer in range(layers):
+        cut = pl.ds(pl.multiple_of(me * units, units), units)
+        for n, (src, dst) in enumerate((
+            (r.gate.at[layer, :, cut], packed[layer].at[:, pl.ds(0, units)]),
+            (r.up.at[layer, :, cut], packed[layer].at[:, pl.ds(units, units)]),
+            (r.down.at[layer, cut], r.turned.at[layer]),
+        )):
+            loads.append(pltpu.make_async_copy(src, dst, r.load.at[3 + 3 * layer + n]))
+    for load in loads:
+        load.start()
+    steps = gather_rows(full, (r.ag_send, r.ag_recv), place, r.x.at[lax.axis_index(TP)])
+    next(steps)
+    own.wait()
+    for copy in copies:
+        copy.wait()
+    gain = jnp.concatenate([r.all_gains[n, 0:1, :] for n in range(lax.axis_size(FSDP))], axis=1)
+    rows = full.shape[1]
+    half = rows // 2
+    step = 16
+
+    def norm(top_of, low_of):
+        for part_no, owner in enumerate((top_of, low_of)):
+            @pl.loop(0, half // step)
+            def _(i):
+                here = pl.ds(pl.multiple_of(part_no * half + i * step, step), step)
+                row = full[owner, here, :].astype(jnp.float32)
+                inv_rms = lax.rsqrt(jnp.mean(row * row, axis=-1, keepdims=True) + epsilon)
+                r.normed[owner, here, :] = (row * inv_rms * gain).astype(jnp.bfloat16)
+
+    def mask():
+        length = r.bias.shape[1]
+        block = 96
+        query = lax.broadcasted_iota(jnp.int32, (1, length), 1)
+        firsts = [r.starts[0:1, n : n + 1] for n in range(r.starts.shape[1])]
+        in_query = [jnp.where((query >= f) & (query < f + PIECE_LEN), 1, 0) for f in firsts]
+        for owner in range(r.all_places.shape[0]):
+            @pl.loop(0, rows // block)
+            def _(i):
+                here = pl.ds(pl.multiple_of(i * block, block), block)
+                key = owner * rows + i * block + lax.broadcasted_iota(jnp.int32, (block, 1), 0)
+                valid = r.all_places[owner, here, 1:2]
+                seen = 0
+                for f, row in zip(firsts, in_query):
+                    seen += jnp.where((key >= f) & (key < f + PIECE_LEN), 1, 0) * row
+                seen = jnp.where(key <= query, 1, seen) * valid
+                seen = jnp.where(key == query, 1, seen)
+                added = jnp.where(seen > 0, 0.0, neg_big).astype(jnp.bfloat16)
+                keys = pl.ds(pl.multiple_of(owner * rows + i * block, block), block)
+                for n in range(r.all_places.shape[0]):
+                    one = added[:, n * rows : (n + 1) * rows]
+                    r.bias[n, keys, :] = jnp.concatenate([one, one], axis=1)
+
+    norm(me, me)
+    mask()
+    r.keep("bias")
+    next(steps)
+    norm(side_x, side_y)
+    for load in loads:
+        load.wait()
+    for layer in range(layers):
+        packed[layer][:, 2 * units :] = r.turned[layer].astype(jnp.float32).T.astype(jnp.bfloat16)
+        r.keep(f"packed_{layer}")
+    next(steps)
+    norm(side_y, side_x)
+    run(steps)
+    norm(across, across)
+
+
+def stat_steps(r, place):
+    depth = lax.axis_size(FSDP)
+    level = lax.axis_index(FSDP)
+    others = [{FSDP: lax.rem(level + step, depth)} for step in range(1, depth)]
+    here = (r.stat_send, r.stat_recv)
+    layers = len(r.attn_stats)
+    lane = lax.broadcasted_iota(jnp.int32, (8, 128), 1)
+    tile = jnp.zeros((8, 128), jnp.float32)
+    wanted = [(3 * layers, r.attn_stats[0], 2)]
+    for layer in range(layers):
+        wanted += [(3 * layer, r.attn_stats[layer], 1), (3 * layer + 1, r.attn_stats[layer], 0)]
+        wanted.append((3 * layer + 2, r.mlp_stats[layer], 0))
+    for to, ref, at in wanted:
+        row = jnp.sum(ref[...], axis=0, keepdims=True)
+        value = jnp.sum(jnp.where(lane[0:1] == at, row, 0.0), axis=1, keepdims=True)
+        tile += jnp.where(lane == to, value, 0.0)
+    width = r.width
+    r.stat_sent[0, :, pl.ds(width, 128)] = tile
+    r.stat_sent[0, :, pl.ds(0, width)] = jnp.zeros((8, width), jnp.float32)
+    for n, ref in enumerate(r.gain_rows):
+        r.stat_sent[0, n : n + 1, pl.ds(0, width)] = jnp.sum(ref[...], axis=0, keepdims=True)
+    for n, peer in enumerate((sibling(), {CTX: place[1]}, {CTX: place[2]})):
+        copy = send(r.stat_sent.at[n], r.stat_came.at[n], here, n, peer)
+        yield
+        copy.wait()
+        r.stat_sent[n + 1] = r.stat_sent[n] + r.stat_came[n]
+    r.stat_z[level] = r.stat_sent[3]
+    copies = [send(r.stat_z.at[level], r.stat_z.at[level], here, 3 + n, peer) for n, peer in enumerate(others)]
+    yield
+    for copy in copies:
+        copy.wait()
+    part = width // depth
+    here = pl.ds(pl.multiple_of(level * part, 128), part)
+    gains, held = r.stat_z[0, :, here], r.stat_z[0, :, pl.ds(width, 128)]
+    for n in range(1, depth):
+        gains += r.stat_z[n, :, here]
+        held += r.stat_z[n, :, pl.ds(width, 128)]
+    r.gains[...] = gains
+    count = jnp.sum(jnp.where(lane[0:1] == 3 * layers, held[0:1], 0.0), axis=1, keepdims=True)
+    r.all_stats[...] = jnp.sqrt(held / (count * r.width))
+
+
+def tail_kernel(width, r):
+    r.width = width
+    place = partners()
+    me = place[0]
+    depth = lax.axis_size(FSDP)
+    level = lax.axis_index(FSDP)
+    peers = [lax.rem(level + step, depth) for step in range(1, depth)]
+    mine = pltpu.make_async_copy(r.share, r.gathered.at[me], r.load.at[0])
+    mine.start()
+    greet_near(place, sibling(), *[{FSDP: peer} for peer in peers])
+    rows = r.share.shape[0]
+    half = rows // 2
+    r.gain_rows = [r.gain_rows_0, r.gain_rows_1, r.gain_rows_2, r.gain_rows_3]
+    r.attn_stats = [r.attn_stats_0, r.attn_stats_1]
+    r.mlp_stats = [r.mlp_stats_0, r.mlp_stats_1]
+    counts = stat_steps(r, place)
+    copies = []
+    for part_no in range(2):
+        copies.append([])
+        for step, peer in enumerate(peers):
+            block = r.summed.at[pl.ds(pl.multiple_of(peer * rows + part_no * half, half), half)]
+            copies[part_no].append(
+                send(block, r.z_came.at[part_no, level], (r.z_send, r.z_recv), part_no * depth + step, {FSDP: peer})
+            )
+    first = gather_rows(r.gathered, (r.ag_send, r.ag_recv), place, r.share)
+    next(first)
+    next(counts)
+    next(first)
+    next(counts)
+    next(counts)
+    next(counts)
+    run(counts)
+    step = 48
+    lasts = (r.last_0, r.last_1)
+    steps = []
+    for part_no in range(2):
+        for copy in copies[part_no]:
+            copy.wait_recv()
+
+        @pl.loop(0, half // step)
+        def _(i):
+            here = pl.ds(pl.multiple_of(i * step, step), step)
+            start = pl.multiple_of(level * rows + part_no * half + i * step, step)
+            total = r.summed[pl.ds(start, step), :].astype(jnp.float32)
+            for peer in peers:
+                total += r.z_came[part_no, peer, here, :].astype(jnp.float32)
+            lasts[part_no][me, here, :] = total.astype(jnp.bfloat16)
+
+        steps.append(gather_rows(lasts[part_no], ((r.l0_send, r.l0_recv), (r.l1_send, r.l1_recv))[part_no], place, lasts[part_no].at[me]))
+        next(steps[part_no])
+        if part_no == 0:
+            next(steps[0])
+    run(first)
+    mine.wait()
+    r.keep("gathered")
+    run(steps[0])
+    run(steps[1])
+    for copy in copies[0] + copies[1]:
+        copy.wait_send()
+
+
+class Scatter:
+    def __init__(self, part, buffers, sems, place):
+        self.part, self.sems, self.place = part, sems, place
+        self.from_x, self.from_y, self.passed, self.last = buffers
+        self.half = part.shape[1] // 2
+        self.copies = {}
+
+    def send(self, slot, src, dst, axis_peer):
+        self.copies[slot] = send(src, dst, self.sems, slot, {CTX: axis_peer})
+
+    def across(self):
+        _, side_x, side_y, far = self.place
+        self.send(0, self.part.at[far, pl.ds(0, self.half)], self.from_x.at[1], side_x)
+        self.send(1, self.part.at[far, pl.ds(self.half, self.half)], self.from_y.at[1], side_y)
+
+    def x_out(self, some=None):
+        side_x = self.place[1]
+        slot, rows = self.cut(some)
+        self.send(slot, self.part.at[side_x, rows], self.from_x.at[0, rows], side_x)
+
+    def y_out(self, some=None):
+        side_y = self.place[2]
+        slot, rows = self.cut(some)
+        below = pl.ds(self.half + rows.start, rows.size)
+        self.send(slot + 1, self.part.at[side_y, below], self.from_y.at[0, rows], side_y)
+
+    def cut(self, some):
+        if some is None:
+            return 2, pl.ds(0, self.half)
+        first = self.half // 48 * 16
+        return (2, pl.ds(0, first)) if some == 0 else (6, pl.ds(first, self.half - first))
+
+    def add_to(self, slot, owner, start, came):
+        step = 16
+
+        @pl.loop(0, self.half // step)
+        def _(i):
+            rows = pl.ds(pl.multiple_of(i * step, step), step)
+            mine = self.part[owner, pl.ds(pl.multiple_of(start + i * step, step), step), :]
+            total = mine.astype(jnp.float32) + came[1, rows, :].astype(jnp.float32)
+            self.passed[slot, rows, :] = total.astype(self.passed.dtype)
+
+    def forward(self):
+        _, side_x, side_y, _ = self.place
+        self.copies[0].wait_recv()
+        self.add_to(0, side_y, 0, self.from_x)
+        self.send(4, self.passed.at[0], self.last.at[0], side_y)
+        self.copies[1].wait_recv()
+        self.add_to(1, side_x, self.half, self.from_y)
+        self.send(5, self.passed.at[1], self.last.at[1], side_x)
+
+    def finish(self):
+        for slot in self.copies:
+            if slot > 1:
+                self.copies[slot].wait_recv()
+        for slot in self.copies:
+            self.copies[slot].wait_send()
+
+    def each_row(self, work, step=16):
+        me = self.place[0]
+        for side in range(2):
+            came = self.from_x if side == 0 else self.from_y
+
+            @pl.loop(0, self.half // step)
+            def _(i):
+                rows = pl.ds(pl.multiple_of(i * step, step), step)
+                whole = pl.ds(pl.multiple_of(side * self.half + i * step, step), step)
+                total = self.part[me, whole, :].astype(jnp.float32)
+                total += came[0, rows, :].astype(jnp.float32)
+                work(whole, total + self.last[side, rows, :].astype(jnp.float32))
+
+
+def scatter_steps(scatter):
+    scatter.across()
+    scatter.x_out()
+    scatter.y_out()
+    yield
+    scatter.forward()
+    yield
+    scatter.finish()
+
+
+class WeightGrads:
+    def __init__(self, lefts, rights, sent, came, summed, sems):
+        self.lefts, self.rights, self.sent, self.came, self.summed, self.sems = lefts, rights, sent, came, summed, sems
+        self.sizes = [r.shape[-1] for r in rights]
+        self.side = lax.axis_index(TP)
+        self.copies = []
+
+    def product(self, p, t, put):
+        block = 256
+        left, right = self.lefts[p], self.rights[p]
+        width = left.shape[-1]
+
+        @pl.loop(0, width // block)
+        def _(i):
+            cols = pl.ds(pl.multiple_of(i * block, block), block)
+            one = left[:, :, cols].reshape(-1, block)
+            put(cols, dot32(one, right[t].reshape(one.shape[0], -1), ((0,), (0,))).astype(jnp.bfloat16))
+
+    def theirs(self, p):
+        def put(rows, value):
+            self.sent[p][rows, : self.sizes[p]] = value
+
+        self.product(p, 1 - self.side, put)
+        self.copies.append(send(self.sent[p], self.came[p], self.sems, p, {TP: 1 - self.side}))
+
+    def cols(self, p):
+        start = sum(self.sizes[:p])
+        return slice(start, start + self.sizes[p])
+
+    def ours(self, p):
+        def put(rows, value):
+            self.summed[rows, self.cols(p)] = value
+
+        self.product(p, self.side, put)
+
+    def add_up(self):
+        step = 64
+        for p, copy in enumerate(self.copies):
+            copy.wait_recv()
+
+            @pl.loop(0, self.summed.shape[0] // step)
+            def _(i):
+                rows = pl.ds(pl.multiple_of(i * step, step), step)
+                total = self.summed[rows, self.cols(p)].astype(jnp.float32) + self.came[p][rows, : self.sizes[p]].astype(jnp.float32)
+                self.summed[rows, self.cols(p)] = total.astype(jnp.bfloat16)
+
+    def close(self):
+        for copy in self.copies:
+            copy.wait_send()
+
+
+def add_stats(stats, valid, *values):
+    lane = lax.broadcasted_iota(jnp.int32, stats.shape, 1)
+    total = stats[...] + jnp.where(lane == 2, valid, 0.0)
+    for n, value in enumerate(values):
+        total += jnp.where(lane == n, valid * jnp.sum(value * value, axis=-1, keepdims=True), 0.0)
+    stats[...] = total
+
+
+def norm_sum(scatter, stream, gain, valid, middle, normed, stats):
+    stats[...] = jnp.zeros_like(stats)
+
+    def work(rows, branch):
+        before = stream[rows, :].astype(jnp.float32)
+        total = before + branch
+        middle[rows, :] = total
+        inv_rms = lax.rsqrt(jnp.mean(total * total, axis=-1, keepdims=True) + epsilon)
+        normed[rows, :] = (total * inv_rms * gain[...]).astype(normed.dtype)
+        add_stats(stats, valid[rows, :], branch, before)
+
+    scatter.each_row(work)
+
+
+def norm_sum_back(scatter, stream, gain, grad, gain_rows, put):
+    gain_rows[...] = jnp.zeros_like(gain_rows)
+
+    def work(rows, got):
+        x = stream[rows, :].astype(jnp.float32)
+        inv_rms = lax.rsqrt(jnp.mean(x * x, axis=-1, keepdims=True) + epsilon)
+        scaled = gain[...] * got
+        along = jnp.mean(scaled * x, axis=-1, keepdims=True)
+        put(rows, grad[rows, :].astype(jnp.float32) + inv_rms * scaled - x * (inv_rms * inv_rms * inv_rms * along))
+        gain_rows[...] += got * x * inv_rms
+
+    scatter.each_row(work)
+
+
+def rows_of(ref, lead, top_of, low_of):
+    half = ref.shape[-2] // 2
+    return jnp.concatenate([ref[(*lead, top_of, pl.ds(0, half))], ref[(*lead, low_of, pl.ds(half, half))]], axis=0)
+
+
+def put_rows(ref, lead, top_of, low_of, value):
+    half = ref.shape[-2] // 2
+    ref[(*lead, top_of, pl.ds(0, half))] = value[:half].astype(ref.dtype)
+    ref[(*lead, low_of, pl.ds(half, half))] = value[half:].astype(ref.dtype)
+
+
+def greet_near(place, *more):
+    greet({CTX: place[1]}, {CTX: place[2]}, *more)
+
+
+def sibling():
+    return {TP: 1 - lax.axis_index(TP)}
+
+
+def mlp_rows(r, top_of, low_of, back):
+    units = r.hidden.shape[-1]
+    x = rows_of(r.full, (), top_of, low_of)
+    total, g_total = 0.0, 0.0
+    for t in range(r.weights.shape[0]):
+        gate_act = dot32(x, r.weights[t, :, :units], ((1,), (0,)))
+        up_act = dot32(x, r.weights[t, :, units : 2 * units], ((1,), (0,)))
+        sig = jax.nn.sigmoid(gate_act)
+        unit = (gate_act * sig * up_act).astype(jnp.bfloat16)
+        put_rows(r.hidden, (t,), top_of, low_of, unit)
+        total += dot32(unit, r.weights[t, :, 2 * units :], ((1,), (1,)))
+        if back:
+            g_total += mlp_back_rows(r, rows_of(r.grad_all, (), top_of, low_of), t, top_of, low_of, gate_act, up_act, sig)
+        else:
+            put_rows(r.gate, (t,), top_of, low_of, gate_act)
+            put_rows(r.up, (t,), top_of, low_of, up_act)
+    put_rows(r.part_out if back else r.part, (), top_of, low_of, total)
+    if back:
+        put_rows(r.part, (), top_of, low_of, g_total)
+
+
+def mlp_back_rows(r, grad, t, top_of, low_of, gate_act, up_act, sig):
+    units = r.grad_gate.shape[-1]
+    g_hidden = dot32(grad, r.weights[t, :, 2 * units :], ((1,), (0,)))
+    g_gate = (g_hidden * up_act * sig * (1.0 + gate_act * (1.0 - sig))).astype(jnp.bfloat16)
+    g_up = (g_hidden * gate_act * sig).astype(jnp.bfloat16)
+    put_rows(r.grad_gate, (t,), top_of, low_of, g_gate)
+    put_rows(r.grad_up, (t,), top_of, low_of, g_up)
+    total = dot32(g_gate, r.weights[t, :, :units], ((1,), (1,)))
+    return total + dot32(g_up, r.weights[t, :, units : 2 * units], ((1,), (1,)))
+
+
+def gathered_work(r, place, scatter, work, rows_own, own, cut=True):
+    me, side_x, side_y, across = place
+    steps = gather_rows(r.full, (r.ag_send, r.ag_recv), place, rows_own)
+    next(steps)
+    own.wait()
+    work(me, me)
+    next(steps)
+    work(side_x, side_y)
+    next(steps)
+    work(side_y, side_x)
+    scatter.x_out(0 if cut else None)
+    scatter.y_out(0 if cut else None)
+    run(steps)
+    work(across, across)
+    scatter.across()
+    if cut:
+        scatter.x_out(1)
+        scatter.y_out(1)
+
+
+def mlp_kernel(r):
+    place = partners()
+    me = place[0]
+    own = pltpu.make_async_copy(r.normed, r.full.at[me], r.load.at[0])
+    own.start()
+    greet_near(place)
+    scatter = Scatter(r.part, (r.from_x, r.from_y, r.passed, r.last), (r.rs_send, r.rs_recv), place)
+
+    def work(top_of, low_of):
+        r.need("weights")
+        mlp_rows(r, top_of, low_of, False)
+
+    gathered_work(r, place, scatter, work, r.normed, own)
+    r.keep("full", "hidden", "gate", "up")
+    scatter.forward()
+    scatter.finish()
+    r.need("middle")
+    norm_sum(scatter, r.middle, r.gain, r.valid, r.stream, r.normed_next, r.stats)
+
+
+def mlp_back_kernel(both, r):
+    place = partners()
+    me = place[0]
+    own = pltpu.make_async_copy(r.rows_own, r.full.at[me], r.load.at[0])
+    own.start()
+    greet_near(place, sibling())
+    scatter = Scatter(r.part, (r.from_x, r.from_y, r.passed, r.last), (r.rs_send, r.rs_recv), place)
+
+    def both_rows(top_of, low_of):
+        r.need("weights", "grad_all")
+        mlp_rows(r, top_of, low_of, True)
+
+    def back_rows(top_of, low_of):
+        r.need("weights", "grad_gate", "grad_up")
+        total = 0.0
+        grad = rows_of(r.full, (), top_of, low_of)
+        for t in range(r.weights.shape[0]):
+            gate_act = rows_of(r.grad_gate, (t,), top_of, low_of).astype(jnp.float32)
+            up_act = rows_of(r.grad_up, (t,), top_of, low_of).astype(jnp.float32)
+            total += mlp_back_rows(r, grad, t, top_of, low_of, gate_act, up_act, jax.nn.sigmoid(gate_act))
+        put_rows(r.part, (), top_of, low_of, total)
+
+    gathered_work(r, place, scatter, both_rows if both else back_rows, r.rows_own, own, not both)
+    if both:
+        r.keep("part_out")
+        job = None
+    else:
+        job = gather_part(r.share, 0, r.gathered, r.load.at[1], r.ja_send, r.ja_recv, place)
+        next(job)
+    normed, grad = (r.full, r.grad_all) if both else (r.normed, r.full)
+    r.need("normed", "hidden")
+    units = r.hidden.shape[-1]
+    sent = [r.weights.at[0, :, pl.ds(p * units, units)] for p in range(3)]
+    sums = WeightGrads(
+        [normed, normed, grad], [r.grad_gate, r.grad_up, r.hidden], sent, [r.came_0, r.came_1, r.came_2],
+        r.summed, (r.tp_send, r.tp_recv),
+    )
+    sums.theirs(0)
+    sums.theirs(1)
+    scatter.forward()
+    sums.theirs(2)
+    sums.ours(0)
+    if job:
+        next(job)
+    sums.ours(1)
+    sums.ours(2)
+    sums.add_up()
+    r.keep("summed")
+    scatter.finish()
+    r.need("middle", "grad")
+
+    def put(rows, total):
+        r.grad_new[rows, :] = total
+        r.grad_rows[rows, :] = total.astype(r.grad_rows.dtype)
+
+    norm_sum_back(scatter, r.middle, r.gain, r.grad, r.gain_rows, put)
+    if job:
+        run(job)
+        r.keep("gathered")
+    sums.close()
+
+
+LOG2E = 1.4426950408889634
+
+
+def turn(x, cos_row, sin_row):
+    half_dim = HEAD_DIM // 2
+    swapped = jnp.concatenate([x[:, half_dim:], x[:, :half_dim]], axis=1)
+    return x * cos_row + swapped * sin_row
+
+
+def project_rows(r, full, top_of, low_of):
+    cols_q, base = 2 * HEAD_DIM, 4 * HEAD_DIM
+    x = rows_of(full, (), top_of, low_of)
+    cos_b, sin_b = rows_of(r.cosine, (), top_of, low_of), rows_of(r.sine, (), top_of, low_of)
+    for t in range(r.weights.shape[0]):
+        flat = dot32(x, r.weights[t, :, :base], ((1,), (0,)))
+        for g in range(2):
+            put_rows(r.query, (t, g), top_of, low_of, turn(flat[:, g * HEAD_DIM : (g + 1) * HEAD_DIM], cos_b, sin_b))
+        put_rows(r.key, (t,), top_of, low_of, turn(flat[:, cols_q : cols_q + HEAD_DIM], cos_b, sin_b))
+        put_rows(r.value, (t,), top_of, low_of, flat[:, cols_q + HEAD_DIM : base])
+
+
+def attend_rows(r, owner):
+    base = 4 * HEAD_DIM
+    pairs, _, rows, _ = r.key.shape
+    factor = HEAD_DIM ** (-0.5) * LOG2E
+
+    for t in range(pairs):
+        key = r.key[t].reshape(-1, HEAD_DIM)
+        value = r.value[t].reshape(-1, HEAD_DIM)
+        query = jnp.concatenate([r.query[t, 0, owner], r.query[t, 1, owner]], axis=0)
+        raw = dot32(key, query, ((1,), (1,)))
+        raw = raw * factor + r.bias[owner].astype(jnp.float32)
+        top = jnp.max(raw, axis=0, keepdims=True)
+        probs = jnp.exp2(raw - top)
+        total = jnp.sum(probs, axis=0, keepdims=True)
+        out = dot32(value, probs.astype(jnp.bfloat16), ((0,), (0,))) * (1.0 / total)
+        fill = -out.shape[1] % 128
+        out = jnp.concatenate([out, jnp.zeros((HEAD_DIM, fill), jnp.float32)], axis=1).T.astype(jnp.bfloat16)
+        r.lse[t, owner] = top + jnp.log2(total)
+        for g in range(2):
+            r.mixed[t, owner, :, g * HEAD_DIM : (g + 1) * HEAD_DIM] = out[g * rows : (g + 1) * rows]
+
+    total = 0.0
+    for t in range(pairs):
+        total += dot32(r.mixed[t, owner], r.weights[t, :, base : base + 2 * HEAD_DIM], ((1,), (1,)))
+    r.part[owner] = total.astype(r.part.dtype)
+
+
+def attend_kernel(first, r):
+    place = partners()
+    me, side_x, side_y, across = place
+    rows_own = r.share.at[lax.axis_index(TP)] if first else r.normed
+    own = pltpu.make_async_copy(rows_own, r.full.at[me], r.load.at[0])
+    own.start()
+    greet_near(place)
+    steps = gather_rows(r.full, (r.ag_send, r.ag_recv), place, rows_own)
+    next(steps)
+    own.wait()
+    rows = r.normed if first else r.full
+    r.need("weights", "cosine", "sine", "normed")
+    if first:
+        for owner in range(4):
+            project_rows(r, rows, owner, owner)
+    else:
+        project_rows(r, rows, me, me)
+        next(steps)
+        project_rows(r, rows, side_x, side_y)
+        next(steps)
+        project_rows(r, rows, side_y, side_x)
+        run(steps)
+        project_rows(r, rows, across, across)
+        r.keep("full")
+    r.keep("query", "key", "value")
+    scatter = Scatter(r.part, (r.from_x, r.from_y, r.passed, r.last), (r.rs_send, r.rs_recv), place)
+    r.need("bias")
+    attend_rows(r, across)
+    scatter.across()
+    if first:
+        next(steps)
+    attend_rows(r, side_x)
+    scatter.x_out()
+    attend_rows(r, side_y)
+    scatter.y_out()
+    scatter.forward()
+    attend_rows(r, me)
+    r.keep("lse", "mixed")
+    if first:
+        run(steps)
+        r.keep("full")
+    scatter.finish()
+    r.need("stream")
+    norm_sum(scatter, r.stream, r.gain, r.valid, r.middle, r.normed_next, r.stats)
+
+
+def attend_back_kernel(last, r):
+    place = partners()
+    me, side_x, side_y, across = place
+    own = pltpu.make_async_copy(r.rows_own, r.full.at[me], r.load.at[0])
+    own.start()
+    greet_near(place, sibling())
+    cols_q, base = 2 * HEAD_DIM, 4 * HEAD_DIM
+    pairs = r.weights.shape[0]
+    rows = r.full.shape[1]
+    scale = HEAD_DIM ** (-0.5)
+    factor = scale * LOG2E
+    order = (me, side_x, side_y, across)
+    masks = [pltpu.make_async_copy(r.bias_in.at[owner], r.bias.at[n % 2], r.bias_load.at[n]) for n, owner in enumerate(order)]
+    masks[0].start()
+    masks[1].start()
+    r.g_key[...] = jnp.zeros_like(r.g_key)
+    r.g_value[...] = jnp.zeros_like(r.g_value)
+
+    def project(top_of, low_of):
+        r.need("weights")
+        x = rows_of(r.full, (), top_of, low_of)
+        for t in range(pairs):
+            flat = dot32(x, r.weights[t, :, base : base + cols_q], ((1,), (0,)))
+            for g in range(2):
+                put_rows(r.heads, (t, g), top_of, low_of, flat[:, g * HEAD_DIM : (g + 1) * HEAD_DIM])
+
+    def two(ref, t, owner):
+        return jnp.concatenate([ref[t, 0, owner], ref[t, 1, owner]], axis=0)
+
+    def queries_back(n):
+        owner = order[n]
+        masks[n].wait()
+        for t in range(pairs):
+            query, heads = two(r.query, t, owner), two(r.heads, t, owner)
+            mixed = r.mixed[t, owner].astype(jnp.float32)
+            mixed = jnp.concatenate([mixed[:, :HEAD_DIM], mixed[:, HEAD_DIM:]], axis=0)
+            along = lax.dot_general(
+                jnp.ones((8, HEAD_DIM), jnp.float32), heads.astype(jnp.float32) * mixed, (((1,), (1,)), ((), ())),
+                precision=lax.Precision.HIGHEST, preferred_element_type=jnp.float32,
+            )[0:1]
+            lse = r.lse[t, owner]
+            r.g_query[...] = jnp.zeros_like(r.g_query)
+
+            @pl.loop(0, jnp.minimum(owner + 2, 4))
+            def _(kept):
+                here = pl.ds(pl.multiple_of(kept * rows, 16), rows)
+                key, value = r.key[t, kept], r.value[t, kept]
+                raw = dot32(key, query, ((1,), (1,)))
+                probs = jnp.exp2(raw * factor + r.bias[n % 2, here, :].astype(jnp.float32) - lse)
+                g_probs = dot32(value, heads, ((1,), (1,)))
+                g_scores = (probs * (g_probs - along)).astype(jnp.bfloat16)
+                r.g_value[t, kept] += dot32(probs.astype(jnp.bfloat16), heads, ((1,), (0,)))
+                r.g_key[t, kept] += dot32(g_scores, query, ((1,), (0,)))
+                r.g_query[...] += dot32(key, g_scores, ((0,), (0,)))
+
+            fill = jnp.zeros((HEAD_DIM, -2 * rows % 128), jnp.float32)
+            g_query = jnp.concatenate([r.g_query[...], fill], axis=1).T * scale
+            for g in range(2):
+                r.grad_qkv[t, owner, :, g * HEAD_DIM : (g + 1) * HEAD_DIM] = turn(
+                    g_query[g * rows : (g + 1) * rows], r.cosine[owner], -r.sine[owner]
+                ).astype(jnp.bfloat16)
+        if n + 2 < 4:
+            masks[n + 2].start()
+
+    steps = gather_rows(r.full, (r.ag_send, r.ag_recv), place, r.rows_own)
+    next(steps)
+    own.wait()
+    project(me, me)
+    r.need("key", "value", "query", "lse", "mixed", "cosine", "sine")
+    queries_back(0)
+    next(steps)
+    jobs = [
+        gather_part(r.share_a, 1, r.gathered_a, r.load.at[1], r.ja_send, r.ja_recv, place),
+        gather_part(r.share_b, None, r.gathered_b, r.load.at[2], r.jb_send, r.jb_recv, place),
+    ] if last else [end_steps(r, place)]
+    for job in jobs:
+        next(job)
+    project(side_x, side_y)
+    next(steps)
+    project(side_y, side_x)
+    queries_back(1)
+    queries_back(2)
+    run(steps)
+    project(across, across)
+    queries_back(3)
+
+    @pl.loop(0, 4)
+    def _(owner):
+        for t in range(pairs):
+            r.grad_qkv[t, owner, :, cols_q : cols_q + HEAD_DIM] = turn(
+                r.g_key[t, owner] * scale, r.cosine[owner], -r.sine[owner]
+            ).astype(jnp.bfloat16)
+            r.grad_qkv[t, owner, :, cols_q + HEAD_DIM :] = r.g_value[t, owner].astype(jnp.bfloat16)
+
+    def branch(owner):
+        total = 0.0
+        for t in range(pairs):
+            total += dot32(r.grad_qkv[t, owner], r.weights[t, :, :base], ((1,), (1,)))
+        r.part[owner] = total.astype(r.part.dtype)
+
+    scatter = Scatter(r.part, (r.from_x, r.from_y, r.passed, r.last), (r.rs_send, r.rs_recv), place)
+    branch(across)
+    scatter.across()
+    branch(side_x)
+    scatter.x_out()
+    branch(side_y)
+    scatter.y_out()
+    branch(me)
+    r.need("normed")
+    sums = WeightGrads(
+        [r.normed, r.full], [r.grad_qkv, r.mixed],
+        [r.weights.at[0, :, pl.ds(0, base)], r.weights.at[1, :, pl.ds(0, r.came_1.shape[1])]], [r.came_0, r.came_1],
+        r.summed, (r.tp_send, r.tp_recv),
+    )
+    sums.theirs(0)
+    for job in jobs:
+        next(job)
+    scatter.forward()
+    sums.theirs(1)
+    sums.ours(0)
+    sums.ours(1)
+    r.summed[:, base + cols_q :] = jnp.zeros((r.summed.shape[0], r.summed.shape[1] - base - cols_q), jnp.bfloat16)
+    sums.add_up()
+    r.keep("summed")
+    scatter.finish()
+    r.need("stream", "grad")
+    side = lax.axis_index(TP)
+
+    def put(here, total):
+        if last:
+            r.grad_new[side, here, :] = total
+        else:
+            r.grad_new[here, :] = total
+            r.grad_rows[here, :] = total.astype(r.grad_rows.dtype)
+
+    norm_sum_back(scatter, r.stream, r.gain, r.grad, r.gain_rows, put)
+    handed = []
+    if last:
+        handed.append(send(r.grad_new.at[side], r.grad_new.at[side], (r.tp_send, r.tp_recv), 2, sibling()))
+    for job in jobs:
+        run(job)
+    if last:
+        r.keep("gathered_a", "gathered_b")
+    else:
+        r.keep("out")
+    for copy in handed:
+        copy.wait()
+    sums.close()
+
+
+def end_steps(r, place):
+    side = lax.axis_index(TP)
+    r.need("end_part")
+    scatter = Scatter(
+        r.end_part, (r.end_from_x, r.end_from_y, r.end_passed, r.end_last), (r.end_send, r.end_recv), place
+    )
+    yield from scatter_steps(scatter)
+
+    r.stats[...] = jnp.zeros_like(r.stats)
+
+    def work(rows, branch):
+        r.out[side, rows, :] = (r.end_middle[rows, :] + branch).astype(r.out.dtype)
+        add_stats(r.stats, r.valid[rows, :], branch)
+
+    r.need("end_middle")
+    scatter.each_row(work)
+    send(r.out.at[side], r.out.at[side], (r.out_send, r.out_recv), 0, sibling()).wait()
+
+
+def gather_part(share, part_no, full, local_sem, send_sems, recv_sems, place):
+    rows = full.shape[1]
+    src = share if part_no is None else share.at[pl.ds(part_no * rows, rows)]
+    copy = pltpu.make_async_copy(src, full.at[place[0]], local_sem)
+    copy.start()
+    yield from gather_rows(full, (send_sems, recv_sems), place, src)
+    copy.wait()
+
+
+class Refs:
+    def need(self, *names):
+        for name in names:
+            if name in self.loads:
+                self.loads.pop(name).wait()
+
+    def keep(self, *names):
+        for name in names:
+            src, dst, sem = self.late[name]
+            store = pltpu.make_async_copy(src, dst, sem)
+            store.start()
+            self.stores.append(store)
+
+
+def linked(kernel, number, micros, near, far, lazy, outs, late, scratch):
+    names = [*near, *far, *lazy, *outs, *late, *scratch]
+    halves = [name for name, value in lazy.items() if isinstance(value, tuple)]
+    lazy = {name: value[0] if name in halves else value for name, value in lazy.items()}
+    lazy_rooms = [pltpu.VMEM(v.shape[1:] if name in halves else v.shape, v.dtype) for name, v in lazy.items()]
+    lazy_names, late_names = list(lazy), list(late)
+
+    def body(*refs):
+        r = Refs()
+        count = len(names)
+        rest = list(refs[count:])
+        by_name = dict(zip(names, refs))
+        r.loads, r.late, r.stores = {}, {}, []
+        held = rest[: len(lazy) + len(late)]
+        for n, name in enumerate(lazy_names):
+            src = by_name[name].at[lax.axis_index(TP)] if name in halves else by_name[name]
+            r.loads[name] = pltpu.make_async_copy(src, held[n], rest[-2].at[n])
+            by_name[name] = held[n]
+        for n, name in enumerate(late_names):
+            r.late[name] = (held[len(lazy) + n], by_name[name], rest[-1].at[n])
+            by_name[name] = held[len(lazy) + n]
+        for name, ref in by_name.items():
+            setattr(r, name, ref)
+        for load in r.loads.values():
+            load.start()
+        kernel(r)
+        r.need(*lazy_names)
+        for store in r.stores:
+            store.wait()
+
+    vmem = pl.BlockSpec(memory_space=pltpu.VMEM)
+    hbm = pl.BlockSpec(memory_space=pl.ANY)
+    came = pl.pallas_call(
+        body,
+        out_shape=[*outs.values(), *late.values()],
+        in_specs=[vmem] * len(near) + [hbm] * (len(far) + len(lazy)),
+        out_specs=[vmem] * len(outs) + [hbm] * len(late),
+        scratch_shapes=[
+            *scratch.values(), *lazy_rooms, *map(room, late.values()),
+            pltpu.SemaphoreType.DMA((max(1, len(lazy)),)), pltpu.SemaphoreType.DMA((max(1, len(late)),)),
+        ],
+        compiler_params=pltpu.CompilerParams(
+            collective_id=number, has_side_effects=True, vmem_limit_bytes=61 << 20
+        ),
+        cost_estimate=pl.CostEstimate(flops=0, bytes_accessed=int(micros * 3.6e6), transcendentals=0),
+    )(*near.values(), *far.values(), *lazy.values())
+    result = Refs()
+    for name, value in zip([*outs, *late], came):
+        setattr(result, name, value)
+    return result
+
+
+def sems(name, count):
+    return {f"{name}_send": pltpu.SemaphoreType.DMA((count,)), f"{name}_recv": pltpu.SemaphoreType.DMA((count,))}
+
+
+def sum_room(rows, width, prefix=""):
+    names = ("from_x", "from_y", "passed", "last")
+    return {prefix + name: pltpu.VMEM((2, rows // 2, width), jnp.bfloat16) for name in names}
+
+
+def shape16(*dims):
+    return jax.ShapeDtypeStruct(dims, jnp.bfloat16)
+
+
+def shape32(*dims):
+    return jax.ShapeDtypeStruct(dims, jnp.float32)
+
+
+def room(like):
+    return pltpu.VMEM(like.shape, like.dtype)
+
+
+def mlp_step(normed, middle, gain, valid, weights):
+    rows, width = middle.shape
+    pairs, units = weights.shape[0], weights.shape[2] // 3
+    kept = shape16(pairs, 4, rows, units)
+    return linked(
+        mlp_kernel, 12, 75,
+        dict(gain=gain, valid=valid), dict(normed=normed), dict(weights=weights, middle=middle),
+        dict(stream=shape32(rows, width), normed_next=shape16(rows, width), stats=shape32(16, 128)),
+        dict(full=shape16(4, rows, width), hidden=kept, gate=kept, up=kept),
+        dict(
+            part=pltpu.VMEM((4, rows, width), jnp.bfloat16), load=pltpu.SemaphoreType.DMA((1,)),
+            **sum_room(rows, width), **sems("ag", 6), **sems("rs", 8),
+        ),
+    )
+
+
+def mlp_back_step(rows_own, middle, gain, grad, weights, grad_all=None, kept=None, share=None):
+    rows, width = middle.shape
+    pairs, units = weights.shape[0], weights.shape[2] // 3
+    both = grad_all is not None
+    whole, unit = shape16(4, rows, width), shape16(pairs, 4, rows, units)
+    far = dict(rows_own=rows_own)
+    lazy = dict(weights=weights)
+    late = dict(summed=shape16(width, 3 * units))
+    scratch = dict(
+        full=room(whole), part=room(whole), load=pltpu.SemaphoreType.DMA((2,)),
+        **{f"came_{p}": pltpu.VMEM((width, units), jnp.bfloat16) for p in range(3)},
+        **sum_room(rows, width), **sems("ag", 6), **sems("rs", 8), **sems(TP, 3),
+    )
+    if both:
+        lazy["grad_all"] = grad_all
+        late["part_out"] = whole
+        scratch.update(grad_gate=room(unit), grad_up=room(unit), hidden=room(unit))
+    else:
+        far["share"] = share
+        lazy.update(grad_gate=kept.gate, grad_up=kept.up, hidden=kept.hidden, normed=kept.full)
+        late["gathered"] = shape16(4, share.shape[0] // 2, share.shape[1])
+        scratch.update(**sems("ja", 6))
+    lazy.update(middle=middle, grad=grad)
+    return linked(
+        functools.partial(mlp_back_kernel, both), 13 if both else 5, 85,
+        dict(gain=gain), far, lazy,
+        dict(grad_new=shape32(rows, width), grad_rows=shape16(rows, width), gain_rows=shape32(16, width)),
+        late, scratch,
+    )
+
+
+def attend_step(normed, stream, gain, valid, weights, cosine, sine, bias, share=None):
+    first = share is not None
+    rows, width = stream[0].shape[1:] if first else stream.shape
+    pairs = weights.shape[0]
+    far, lazy = {}, dict(weights=weights, cosine=cosine, sine=sine)
+    if first:
+        far["share"] = share
+        lazy["normed"] = normed
+    else:
+        far["normed"] = normed
+    lazy.update(bias=bias, stream=stream)
+    return linked(
+        functools.partial(attend_kernel, first), 11 if first else 9, 75,
+        dict(gain=gain, valid=valid), far, lazy,
+        dict(middle=shape32(rows, width), normed_next=shape16(rows, width), stats=shape32(16, 128)),
+        dict(
+            full=shape16(4, rows, width), query=shape16(pairs, 2, 4, rows, HEAD_DIM),
+            key=shape16(pairs, 4, rows, HEAD_DIM), value=shape16(pairs, 4, rows, HEAD_DIM),
+            lse=shape32(pairs, 4, 1, 2 * rows), mixed=shape16(pairs, 4, rows, 2 * HEAD_DIM),
+        ),
+        dict(
+            part=pltpu.VMEM((4, rows, width), jnp.bfloat16), load=pltpu.SemaphoreType.DMA((1,)),
+            **sum_room(rows, width), **sems("ag", 6), **sems("rs", 8),
+        ),
+    )
+
+
+def attend_back_step(
+    rows_own, stream, gain, grad, weights, cosine, sine, bias, kept, normed, shares=None, end=None
+):
+    rows, width = rows_own.shape
+    pairs = weights.shape[0]
+    length = 4 * rows
+    last = shares is not None
+    whole = shape16(4, rows, width)
+    near = dict(gain=gain)
+    far = dict(rows_own=rows_own, bias_in=bias)
+    lazy = dict(
+        weights=weights, key=kept.key, value=kept.value, query=kept.query, lse=kept.lse, mixed=kept.mixed,
+        cosine=cosine, sine=sine, normed=normed, stream=stream, grad=grad,
+    )
+    sizes = (4 * HEAD_DIM, 2 * HEAD_DIM)
+    total = sum(sizes) + 64
+    outs = dict(gain_rows=shape32(16, width))
+    late = dict(summed=shape16(width, total))
+    scratch = dict(
+        full=room(whole), part=room(whole),
+        heads=room(kept.query), g_key=pltpu.VMEM(kept.key.shape, jnp.float32),
+        g_value=pltpu.VMEM(kept.key.shape, jnp.float32), g_query=pltpu.VMEM((HEAD_DIM, 2 * rows), jnp.float32),
+        grad_qkv=pltpu.VMEM((pairs, 4, rows, sizes[0]), jnp.bfloat16),
+        bias=pltpu.VMEM((2, length, 2 * rows), jnp.bfloat16), bias_load=pltpu.SemaphoreType.DMA((4,)),
+        came_0=pltpu.VMEM((width, sizes[0]), jnp.bfloat16), came_1=pltpu.VMEM((width, 256), jnp.bfloat16),
+        load=pltpu.SemaphoreType.DMA((3,)),
+        **sum_room(rows, width), **sems("ag", 6), **sems("rs", 8), **sems(TP, 4),
+    )
+    if last:
+        far.update(share_a=shares[0], share_b=shares[1])
+        outs.update(grad_new=shape32(2, rows, width))
+        late.update(
+            gathered_a=shape16(4, shares[0].shape[0] // 2, shares[0].shape[1]),
+            gathered_b=shape16(4, *shares[1].shape),
+        )
+        scratch.update(**sems("ja", 6), **sems("jb", 6))
+    else:
+        lazy = dict(end_part=end[0], **lazy, end_middle=end[1])
+        near["valid"] = end[2]
+        outs.update(grad_new=shape32(rows, width), grad_rows=shape16(rows, width), stats=shape32(16, 128))
+        late["out"] = shape16(2, rows, width)
+        scratch.update(**sum_room(rows, width, "end_"), **sems("end", 6), **sems("out", 1))
+    return linked(
+        functools.partial(attend_back_kernel, last), 7 if last else 6, 100, near, far, lazy, outs, late, scratch,
+    )
+
+
+def tail_step(summed, share, attn_stats, mlp_stats, gain_rows):
+    depth = lax.axis_size(FSDP)
+    half, cols = share.shape[0] // 2, summed.shape[1]
+    last = shape16(4, half, cols)
+    wide = summed.shape[0] + 128
+    return linked(
+        functools.partial(tail_kernel, summed.shape[0]), 10, 60,
+        dict(
+            summed=summed,
+            **{f"attn_stats_{layer}": a for layer, a in enumerate(attn_stats)},
+            **{f"mlp_stats_{layer}": a for layer, a in enumerate(mlp_stats)},
+            **{f"gain_rows_{n}": a for n, a in enumerate(gain_rows)},
+        ),
+        dict(share=share), {},
+        dict(last_0=last, last_1=last, all_stats=shape32(8, 128), gains=shape32(8, summed.shape[0] // depth)), dict(gathered=shape16(4, *share.shape)),
+        dict(
+            z_came=pltpu.VMEM((2, depth, half, cols), jnp.bfloat16), stat_sent=pltpu.VMEM((4, 8, wide), jnp.float32),
+            stat_came=pltpu.VMEM((3, 8, wide), jnp.float32), stat_z=pltpu.VMEM((depth, 8, wide), jnp.float32),
+            load=pltpu.SemaphoreType.DMA((1,)), **sems("z", 2 * depth), **sems("ag", 6), **sems("stat", 3 + depth),
+            **sems("l0", 6), **sems("l1", 6),
+        ),
+    )
+
+
+def start_step(gains, places, starts, x, gate, up, down):
+    depth, across = lax.axis_size(FSDP), lax.axis_size(CTX)
+    layers, rows = gate.shape[:2]
+    units = gate.shape[2] // across
+    own = x.shape[1:]
+    length = across * own[0]
+    return linked(
+        start_kernel, 8, 38,
+        dict(gains=gains, places=places, starts=starts), dict(x=x, gate=gate, up=up, down=down), {},
+        dict(
+            all_gains=jax.ShapeDtypeStruct((depth, *gains.shape), gains.dtype),
+            all_places=jax.ShapeDtypeStruct((across, *places.shape), places.dtype),
+            normed=shape16(across, *own),
+        ),
+        dict(
+            bias=shape16(across, length, 2 * own[0]),
+            **{f"packed_{layer}": shape16(rows, 3 * units) for layer in range(layers)},
+        ),
+        dict(
+            full=pltpu.VMEM((across, *own), jnp.bfloat16), turned=pltpu.VMEM((layers, units, rows), jnp.bfloat16),
+            load=pltpu.SemaphoreType.DMA((3 + 3 * layers,)), **sems("gain", depth), **sems("place", across),
+            **sems("ag", 6),
+        ),
+    )
+
+
+def planned(
+    tokens, positions, valid, piece_starts, d_out,
+    attn_gain, w_query, w_key, w_value, w_out, mlp_gain, w_gate, w_up, w_down,
+):
+    seq_count, rows, width = tokens.shape
+    layers = attn_gain.shape[0]
+    ctx_count = lax.axis_size(CTX)
+    tp_count = lax.axis_size(TP)
+    me = lax.axis_index(CTX)
+    side = lax.axis_index(TP)
+    length = rows * ctx_count
+    heads_q = HEADS // tp_count // ctx_count
+    heads_k = KV_HEADS // tp_count // ctx_count
+    cols_q = heads_q * HEAD_DIM
+    cols_k = heads_k * HEAD_DIM
+    units = w_gate.shape[2] // ctx_count
+
+    def own(a):
+        return lax.dynamic_index_in_dim(a, side, 0, keepdims=False)
+
+    def cut(w, axis, count):
+        return lax.dynamic_slice_in_dim(w, me * count, count, axis)
+
+    def whole(w):
+        return lax.all_gather(w, (TP, FSDP), axis=0, tiled=True).reshape(
+            tp_count, width, w.shape[1]
+        )
+
+    def pack(*pieces):
+        return with_layout_constraint(jnp.concatenate(pieces, axis=1), Layout(major_to_minor=(0, 1)))
+
+    def pack_attn(layer):
+        return pack(
+            cut(w_query[layer], 1, cols_q),
+            cut(w_key[layer], 1, cols_k),
+            cut(w_value[layer], 1, cols_k),
+            cut(w_out[layer], 0, cols_q).T,
+            jnp.zeros((w_query.shape[1], 64), w_query.dtype),
+        )
+
+    attn_w = [whole(pack_attn(0))]
+    packed_attn = [None] + [pack_attn(layer) for layer in range(1, layers)]
+    mlp_w = []
+    seq_pos, seq_valid = own(positions), own(valid)
+    starts = own(piece_starts)
+    begun = start_step(
+        jnp.pad(jnp.concatenate([attn_gain, mlp_gain], 0).astype(jnp.float32), ((0, 8 - 2 * layers), (0, 0))),
+        jnp.pad(jnp.stack([seq_pos, seq_valid], axis=1), ((0, 0), (0, 6))),
+        starts[None], tokens, w_gate, w_up, w_down,
+    )
+    normed, bias = begun.normed, begun.bias
+    packed_mlp = [getattr(begun, f"packed_{layer}") for layer in range(layers)]
+    gains = begun.all_gains.swapaxes(0, 1).reshape(8, width)
+    places = begun.all_places
+    gain_a = [gains[layer][None] for layer in range(layers)]
+    gain_m = [gains[layers + layer][None] for layer in range(layers)]
+    pos_all = places[:, :, 0].reshape(length)
+    valid_f = seq_valid.astype(jnp.float32)[:, None]
+    grad = (d_out,)
+    mlp_w.append(whole(packed_mlp[0]))
+    half_dim = HEAD_DIM // 2
+    freqs = rope_base ** (-(jnp.arange(half_dim).astype(jnp.float32) * 2.0 / HEAD_DIM))
+    angles = pos_all.astype(jnp.float32)[:, None] * freqs
+    cosine, sine_t = jnp.cos(angles), jnp.sin(angles)
+    cosine = jnp.concatenate([cosine, cosine], axis=1)
+    sine_t = jnp.concatenate([-sine_t, sine_t], axis=1)
+    cosine, sine_t = lax.optimization_barrier(
+        (cosine.reshape(ctx_count, rows, HEAD_DIM), sine_t.reshape(ctx_count, rows, HEAD_DIM))
+    )
+
+    streams, attends, mlps = [(tokens,)], [], []
+    for layer in range(layers):
+        kept = attend_step(
+            normed, streams[layer], gain_m[layer], valid_f, attn_w[layer], cosine, sine_t, bias,
+            None if layer else d_out,
+        )
+        if layer == 0:
+            grad_all, kept.full = kept.full, normed
+        attends.append(kept)
+        if layer + 1 < layers:
+            normed_m, packed_attn[layer + 1], packed_mlp[layer + 1] = lax.optimization_barrier(
+                (kept.normed_next, packed_attn[layer + 1], packed_mlp[layer + 1])
+            )
+            attn_w.append(whole(packed_attn[layer + 1]))
+            mlp_w.append(whole(packed_mlp[layer + 1]))
+            mlps.append(mlp_step(normed_m, kept.middle, gain_a[layer + 1], valid_f, mlp_w[layer]))
+            streams.append(mlps[layer].stream)
+            normed = mlps[layer].normed_next
+
+    def reduced(g):
+        return lax.psum_scatter(g, FSDP, scatter_dimension=0, tiled=True)
+
+    down_rows = None
+    attn_gains, mlp_gains = [], []
+    for layer in reversed(range(layers)):
+        kept = attends[layer]
+        if layer + 1 == layers:
+            came = mlp_back_step(kept.normed_next, kept.middle, gain_m[layer], grad, mlp_w[layer], grad_all=grad_all)
+            end = [came.part_out, kept.middle, valid_f]
+        else:
+            came = mlp_back_step(
+                down_rows, kept.middle, gain_m[layer], grad, mlp_w[layer], kept=mlps[layer], share=shares[0]
+            )
+        mlp_share = reduced(came.summed)
+        mlp_gains.insert(0, came.gain_rows)
+        back = attend_back_step(
+            came.grad_rows, streams[layer], gain_a[layer], came.grad_new, attn_w[layer], cosine, sine_t, bias,
+            kept, kept.full, None if layer else shares, end if layer else None,
+        )
+        attn_gains.insert(0, back.gain_rows)
+        if layer:
+            grad, output = back.grad_new, back.out
+            down_rows, mlp_share, summed = lax.optimization_barrier((back.grad_rows, mlp_share, back.summed))
+            shares = [mlp_share, reduced(summed)]
+            last_stats = back.stats
+    ended = tail_step(
+        back.summed, mlp_share, [kept.stats for kept in attends], [kept.stats for kept in mlps] + [last_stats],
+        attn_gains + mlp_gains,
+    )
+    input_grad = back.grad_new
+    mlp_all = [[ended.gathered], [came.gathered, back.gathered_a]]
+    attn_all = [[ended.last_0, ended.last_1], [back.gathered_b]]
+    rms_stats = ended.all_stats[0, : 3 * layers].reshape(layers, 3)
+    base = cols_q + 2 * cols_k
+    placed = place_outs(
+        attn_all, mlp_all,
+        [(0, cols_q, False), (cols_q, cols_k, False), (cols_q + cols_k, cols_k, False), (base, cols_q, True)],
+        [(0, units, False), (units, units, False), (2 * units, units, True)],
+    )
+    gains = ended.gains
+    return (
+        output, input_grad, gains[:layers], *placed[:4], gains[layers : 2 * layers], *placed[4:], rms_stats,
+    )
+
+
+def place_kernel(moves, count, *refs):
+    refs = list(refs)
+    outs_count = 1 + max(out for _, _, pieces in moves for _, _, _, out in pieces)
+    ins, outs = refs[:count], refs[count : count + outs_count]
+    del refs[: count + outs_count]
+    held, laid = refs[:count], refs[count:-2]
+    in_sems, out_sems = refs[-2:]
+    loads = [pltpu.make_async_copy(ins[n], held[n], in_sems.at[n]) for n in range(count)]
+    for load in loads:
+        load.start()
+    stores = []
+    for n, (layer, first, pieces) in enumerate(moves):
+        loads[n].wait()
+        rows = held[n].shape[1]
+        for start, size, flip, out in pieces:
+            for c in range(held[n].shape[0]):
+                block = held[n][c, :, start : start + size].astype(jnp.float32)
+                if flip:
+                    laid[out][layer, c * size : (c + 1) * size, first : first + rows] = block.T
+                else:
+                    laid[out][layer, first : first + rows, c * size : (c + 1) * size] = block
+            if any(layer == l and out == o for l, _, more in moves[n + 1 :] for _, _, _, o in more):
+                continue
+            store = pltpu.make_async_copy(laid[out].at[layer], outs[out].at[layer], out_sems.at[len(stores)])
+            store.start()
+            stores.append(store)
+    for store in stores:
+        store.wait()
+
+
+def place_outs(attn_all, mlp_all, attn_pieces, mlp_pieces):
+    layers = len(attn_all)
+    shapes = []
+    for came, pieces in ((attn_all, attn_pieces), (mlp_all, mlp_pieces)):
+        ctx_count = came[0][0].shape[0]
+        depth = sum(a.shape[1] for a in came[0])
+        for _, size, flip in pieces:
+            wide = ctx_count * size
+            shapes.append((layers, wide, depth) if flip else (layers, depth, wide))
+    ins, moves = [], []
+    for layer in reversed(range(layers)):
+        for came, pieces, base in ((mlp_all, mlp_pieces, len(attn_pieces)), (attn_all, attn_pieces, 0)):
+            first = 0
+            for a in came[layer]:
+                ins.append(a)
+                moves.append((layer, first, [(*piece, base + n) for n, piece in enumerate(pieces)]))
+                first += a.shape[1]
+    hbm = pl.BlockSpec(memory_space=pl.ANY)
+    return pl.pallas_call(
+        functools.partial(place_kernel, moves, len(ins)),
+        out_shape=[jax.ShapeDtypeStruct(s, jnp.float32) for s in shapes],
+        in_specs=[hbm] * len(ins),
+        out_specs=[hbm] * len(shapes),
+        scratch_shapes=[pltpu.VMEM(a.shape, a.dtype) for a in ins]
+        + [pltpu.VMEM(s, jnp.float32) for s in shapes]
+        + [pltpu.SemaphoreType.DMA((len(ins),)), pltpu.SemaphoreType.DMA((layers * len(shapes),))],
+        compiler_params=pltpu.CompilerParams(vmem_limit_bytes=60 << 20),
+    )(*ins)
+
+
+def fits(mesh):
+    tp_count, ctx_count = mesh.shape[TP], mesh.shape[CTX]
+    return ctx_count == 4 and tp_count == 2
+
+
 def solution(mesh):
     in_specs = (
-        P("fsdp", "ctx", None),
-        P("fsdp", "ctx"),
-        P("fsdp", "ctx"),
-        P("fsdp", None),
-        P("fsdp", "ctx", None),
-        P(None, "fsdp"),
-        P(None, "fsdp", "tp"),
-        P(None, "fsdp", "tp"),
-        P(None, "fsdp", "tp"),
-        P(None, "tp", "fsdp"),
-        P(None, "fsdp"),
-        P(None, "fsdp", "tp"),
-        P(None, "fsdp", "tp"),
-        P(None, "tp", "fsdp"),
+        P(FSDP, CTX, None),
+        P(FSDP, CTX),
+        P(FSDP, CTX),
+        P(FSDP, None),
+        P(FSDP, CTX, None),
+        P(None, FSDP),
+        P(None, FSDP, TP),
+        P(None, FSDP, TP),
+        P(None, FSDP, TP),
+        P(None, TP, FSDP),
+        P(None, FSDP),
+        P(None, FSDP, TP),
+        P(None, FSDP, TP),
+        P(None, TP, FSDP),
     )
     out_specs = (
-        P("fsdp", "ctx", None),
-        P("fsdp", "ctx", None),
-        P(None, "fsdp"),
-        P(None, "fsdp", "tp"),
-        P(None, "fsdp", "tp"),
-        P(None, "fsdp", "tp"),
-        P(None, "tp", "fsdp"),
-        P(None, "fsdp"),
-        P(None, "fsdp", "tp"),
-        P(None, "fsdp", "tp"),
-        P(None, "tp", "fsdp"),
+        P(FSDP, CTX, None),
+        P(FSDP, CTX, None),
+        P(None, FSDP),
+        P(None, FSDP, TP),
+        P(None, FSDP, TP),
+        P(None, FSDP, TP),
+        P(None, TP, FSDP),
+        P(None, FSDP),
+        P(None, FSDP, TP),
+        P(None, FSDP, TP),
+        P(None, TP, FSDP),
         P(),
     )
-    return jax.shard_map(local, mesh=mesh, in_specs=in_specs, out_specs=out_specs, check_vma=False)
+    return jax.shard_map(planned if fits(mesh) else general, mesh=mesh, in_specs=in_specs, out_specs=out_specs, check_vma=False)

time: 4280 us -> 753 us (0.18)
  waiting for transfers between devices: 3350 us -> 16.7 us
  Pallas kernels: 0 us -> 692 us
  matrix products: 362 us -> 0 us
  blocking collectives: 234 us -> 0 us
  other arithmetic: 153 us -> 5.8 us
  local copies, waits for them, and re-layouts: 153 us -> 17.4 us
    reduce_scatter x16 -> x3, waiting for transfers between devices: 2120 us -> 0.06 us  [reduced(): return lax.psum_scatter(g, FSDP, scatter_dimension=0, tiled=True)]
    all_gather x24 -> x4, waiting for transfers between devices: 1100 us -> 16 us  [whole(): lax.all_gather(w, (TP, FSDP), axis=0, tiled=True)]
    pallas_call x0 -> x10, Pallas kernels: none -> 692 us  [the longest x9 679 us: linked(): pl.pallas_call(body, out_shape=[*outs.values(), *late.values()], in_specs...]
    dot_general x54 -> x0, matrix products: 362 us -> none  [the longest x2 27.2 us: local(): jnp.einsum('sckgd,snkd->skgcn', grad_heads, value_heads, preferred_elemen...]
    all_gather x13 -> x0, blocking collectives: 145 us -> none  [the longest x2 25.4 us: local(): lax.all_gather(attn_gain[layer_no], 'fsdp', axis=0, tiled=True)]
    psum x7 -> x0, waiting for transfers between devices: 92.7 us -> none  [the longest x2 41 us: local(): lax.psum((jnp.einsum('rf,df->rd', grad_gate, w_g, preferred_element_type=...]
    unnamed x2 -> x0, blocking collectives: 89 us -> none
    convert_element_type x27 -> x2, other arithmetic: 55.8 us -> 0.96 us  [the longest x1 0.68 us: planned(): valid_f = seq_valid.astype(jnp.float32)[:, None]]
  transfers between devices with their start and end apart: 49 -> 7, of which waited for: 46 -> 1; matrix products, arithmetic and copies ran while one was open for 11% -> 1% of each run, Pallas kernels for 0% -> 72%
where the time goes in v4:
time: 753 us; the launch traced here: 747 us
  Pallas kernels  692 us (92%)
  local copies, waits for them, and re-layouts  17.4 us (2%)
  waiting for transfers between devices  16.7 us (2%)
  between operations  14.7 us (2%)
    pallas_call x9, Pallas kernels, linked(): pl.pallas_call(body, out_shape=[*outs.values(), *late.values()], in_specs...  679 us
    all_gather x4, waiting for transfers between devices, whole(): lax.all_gather(w, (TP, FSDP), axis=0, tiled=True)  16 us
  transfers between devices with their start and end apart: 7, of which 1 were waited for; matrix products, arithmetic and copies ran while one was open for 1% of the time, Pallas kernels for 72%

profile of v4, /device:TPU:0, one launch (start us, length us, event | category | flops | bytes accessed | tf_op | source)
XLA Modules:
  0.0 747.5 jit_solution(9233624554697786525)
XLA Ops:
  7.3 2.0 fusion.10
  9.2 1.8 fusion.9
  11.7 1.2 dynamic-slice_bitcast_fusion.4
  12.8 1.1 concatenate.18
  14.2 0.7 pad.12.refs_1_
  14.9 0.5 constant_dynamic-slice_fusion.2.refs_2_
  15.4 0.6 fusion.4.refs_0_
  16.0 47.1 %shard_map.229 = (f32[4,8,384]{2,1,0:T(8,128)}, s32[4,288,8]{2,1,0:T(8,128)}, bf16[4,288,1536]{2,1,0:T(8,128)(2,1)}, bf16[4,1152,576]{2,1,0:T(8,128)(2,1)}, bf16...) custom-call(f32[8,384]{1,0:T(8,128)} %fusion.4.refs_0_, s32[288,8]{1,0:T(8,128)} %pad.12.refs_1_, ...), custom_call_target="tpu_custom_call" | custom-call | bytes 136800000 | tf_op jit(solution)/shard_map/pallas_call | solution.py:1290
  63.3 0.7 convert_element_type.30.refs_1_
  64.4 2.1 fusion
  66.6 1.0 pad_maximum_fusion.refs_4_.refs_11_
  67.6 1.0 pad_maximum_fusion.1.refs_5_.refs_12_
  68.9 1.2 concatenate.21
  70.2 0.6 fusion.11
  70.8 65.3 %shard_map.230 = (f32[288,1536]{1,0:T(8,128)}, bf16[288,1536]{1,0:T(8,128)(2,1)}, f32[16,128]{1,0:T(8,128)}, bf16[4,288,1536]{2,1,0:T(8,128)(2,1)}, bf16[2,2,4,2...) custom-call(f32[1,1536]{1,0:T(1,128)} %bitcast.40, ...), custom_call_target="tpu_custom_call" | custom-call | bytes 270000000 | tf_op jit(solution)/shard_map/pallas_call | solution.py:1290
  136.1 0.5 all-gather.11.cloned.1.call-update
  136.7 15.9 %all-gather.7.cloned.1.call-done = bf16[3072,1536]{1,0:T(8,128)(2,1)} async-done(((bf16[384,1536]{1,0:T(8,128)(2,1)}), bf16[3072,1536]{1,0:T(8,128)(2,1)}) %all-gather.7.cloned.1.call-update) | async-done | bytes 9437200 | tf_op jit(solution)/shard_map/all_gather | solution.py:1526
  152.7 68.0 %shard_map.231 = (f32[288,1536]{1,0:T(8,128)}, bf16[288,1536]{1,0:T(8,128)(2,1)}, f32[16,128]{1,0:T(8,128)}, bf16[4,288,1536]{2,1,0:T(8,128)(2,1)}, bf16[2,4,288...) custom-call(f32[1,1536]{1,0:T(1,128)} %bitcast.44, ...), custom_call_target="tpu_custom_call" | custom-call | bytes 270000000 | tf_op jit(solution)/shard_map/pallas_call | solution.py:1290
  220.7 69.0 %shard_map.232 = (f32[288,1536]{1,0:T(8,128)}, bf16[288,1536]{1,0:T(8,128)(2,1)}, f32[16,128]{1,0:T(8,128)}, bf16[4,288,1536]{2,1,0:T(8,128)(2,1)}, bf16[2,2,4,2...) custom-call(f32[1,1536]{1,0:T(1,128)} %bitcast.42, ...), custom_call_target="tpu_custom_call" | custom-call | bytes 270000000 | tf_op jit(solution)/shard_map/pallas_call | solution.py:1290
  289.8 70.6 %shard_map.233 = (f32[288,1536]{1,0:T(8,128)}, bf16[288,1536]{1,0:T(8,128)(2,1)}, f32[16,1536]{1,0:T(8,128)}, bf16[1536,1536]{1,0:T(8,128)(2,1)}, bf16[4,288,1536]{2,1,0:T(8,128)(2,1)}) custom-call(f32[1,1536]{1,0:T(1,128)} %bitcast.43, bf16[288,1536]{1,0:T(8,128)(2,1)} %get-tuple-element.98.refs_1_, bf16[2,1536,1536]{2,1,0:T(8,128)(2,1)} %bitcast.37, ...), custom_call_target="tpu_custom_call" | custom-call | bytes 306000000 | tf_op jit(solution)/shard_map/pallas_call | solution.py:1290
  360.4 99.9 %shard_map.234 = (f32[16,1536]{1,0:T(8,128)}, f32[288,1536]{1,0:T(8,128)}, bf16[288,1536]{1,0:T(8,128)(2,1)}, f32[16,128]{1,0:T(8,128)}, bf16[1536,640]{1,0:T(8,128)(2,1)}, /*index=5*/bf16[2,288,1536]{2,1,0:T(8,128)(2,1)}) custom-call(f32[1,1536]{1,0:T(1,128)} %bitcast.45, f32[288,1]{1,0:T(8,128)} %convert_element_type.30.refs_1_, ...), custom_call_target="tpu_custom_call" | custom-call | bytes 360000000 | tf_op jit(solution)/shard_map/pallas_call | solution.py:1290
  460.3 0.4 reduce-scatter.8.cloned.1.call-start
  460.8 85.2 %shard_map.235 = (f32[288,1536]{1,0:T(8,128)}, bf16[288,1536]{1,0:T(8,128)(2,1)}, f32[16,1536]{1,0:T(8,128)}, bf16[1536,1536]{1,0:T(8,128)(2,1)}, bf16[4,192,1536]{2,1,0:T(8,128)(2,1)}) custom-call(f32[1,1536]{1,0:T(1,128)} %bitcast.41, bf16[288,1536]{1,0:T(8,128)(2,1)} %get-tuple-element.115.refs_1_, ...), custom_call_target="tpu_custom_call" | custom-call | bytes 306000000 | tf_op jit(solution)/shard_map/pallas_call | solution.py:1290
  546.0 103.0 %shard_map.236 = (f32[16,1536]{1,0:T(8,128)}, f32[2,288,1536]{2,1,0:T(8,128)}, bf16[1536,640]{1,0:T(8,128)(2,1)}, bf16[4,192,1536]{2,1,0:T(8,128)(2,1)}, bf16[4,384,640]{2,1,0:T(8,128)(2,1)}) custom-call(f32[1,1536]{1,0:T(1,128)} %bitcast.46, bf16[288,1536]{1,0:T(8,128)(2,1)} %get-tuple-element.122.refs_1_, ...), custom_call_target="tpu_custom_call" | custom-call | bytes 360000000 | tf_op jit(solution)/shard_map/pallas_call | solution.py:1290
  649.1 71.3 %shard_map.237 = (bf16[4,192,640]{2,1,0:T(8,128)(2,1)}, bf16[4,192,640]{2,1,0:T(8,128)(2,1)}, f32[8,128]{1,0:T(8,128)}, f32[8,384]{1,0:T(8,128)}, bf16[4,384,1536]{2,1,0:T(8,128)(2,1)}) custom-call(bf16[1536,640]{1,0:T(8,128)(2,1)} %get-tuple-element.131.refs_0_, f32[16,128]{1,0:T(8,128)} %get-tuple-element.132.refs_1_, ...), custom_call_target="tpu_custom_call" | custom-call | bytes 216000000 | tf_op jit(solution)/shard_map/pallas_call | solution.py:1290
  720.4 1.4 fusion.12
  721.8 0.7 slice_reduce_fusion
  722.5 0.6 reshape_squeeze.4
  723.1 12.8 %shard_map.238 = (f32[2,384,768]{2,1,0:T(8,128)}, f32[2,384,384]{2,1,0:T(8,128)}, f32[2,384,384]{2,1,0:T(8,128)}, f32[2,768,384]{2,1,0:T(8,128)}, f32[2,384,2048...) custom-call(bf16[4,192,1536]{2,1,0:T(8,128)(2,1)} %get-tuple-element.142.refs_0_, ...), custom_call_target="tpu_custom_call" | custom-call | tf_op jit(solution)/shard_map/pallas_call | solution.py:1685
  736.0 1.2 copy.39
  737.2 1.4 copy-done.2
  738.6 1.8 copy.40
  (57 shorter events, 2.0 us)
Async XLA Ops:
  7.2 7.7 %copy-start = (s32[2,2]{1,0:T(2,128)S(1)}, s32[2,2]{1,0:T(2,128)}, u32[]{:S(2)}) copy-start(s32[2,2]{1,0:T(2,128)} %param.17) | copy-start | bytes 52
  7.2 3.9 copy-start.4
  7.2 63.6 %all-gather.5.cloned.1.call-start = ((), (), s32[]{:S(2)}) async-start(), calls=%async_computation.3 | async-start | bytes 4423680 | tf_op jit(solution)/shard_map/all_gather | solution.py:1526
  7.3 3.9 copy-start.5
  11.2 2.8 copy-start.10
  11.2 2.8 copy-start.11
  11.3 4.1 copy-start.8
  11.3 4.0 copy-start.9
  13.9 138.7 %all-gather.7.cloned.1.call-start = ((), (), s32[]{:S(2)}) async-start(), calls=%async_computation.4 | async-start | bytes 10616832 | tf_op jit(solution)/shard_map/all_gather | solution.py:1526
  63.1 1.1 copy-start.6
  63.1 157.6 %all-gather.9.cloned.1.call-start = ((), (), s32[]{:S(2)}) async-start(), calls=%async_computation.5 | async-start | bytes 4423680 | tf_op jit(solution)/shard_map/all_gather | solution.py:1526
  66.6 3.6 copy-start.7
  136.1 153.7 %all-gather.11.cloned.1.call-start = ((), (), s32[]{:S(2)}) async-start(), calls=%async_computation.6 | async-start | bytes 10616832 | tf_op jit(solution)/shard_map/all_gather | solution.py:1526
  136.7 323.6 %reduce-scatter.4.cloned.1.call-start = ((), (), s32[]{:S(2)}) async-start(), calls=%async_computation.7 | async-start | bytes 5898240 | tf_op jit(solution)/shard_map/reduce_scatter | solution.py:1592
  360.4 185.7 %reduce-scatter.6.cloned.1.call-start = ((), (), s32[]{:S(2)}) async-start(), calls=%async_computation.8 | async-start | bytes 2457600 | tf_op jit(solution)/shard_map/reduce_scatter | solution.py:1592
  460.3 188.7 %reduce-scatter.8.cloned.1.call-start = ((), (), s32[]{:S(2)}) async-start(), calls=%async_computation.9 | async-start | bytes 5898240 | tf_op jit(solution)/shard_map/reduce_scatter | solution.py:1592
  723.1 12.9 %copy-start.3 = (bf16[2,288,1536]{2,1,0:T(8,128)(2,1)S(1)}, bf16[2,288,1536]{2,1,0:T(8,128)(2,1)}, u32[]{:S(2)}) copy-start(bf16[2,288,1536]{2,1,0:T(8,128)(2,1)} %get-tuple-element.191) | copy-start | bytes 5308420
  736.0 2.6 copy-start.2
  736.0 4.4 copy-start.1
Sparse Core Ops, SparseCore 0:
  14.0 47.3 all-gather.4
  63.2 89.3 all-gather.6
  154.8 43.2 all-gather.8
  199.5 89.5 all-gather.10
  360.5 82.7 reduce-scatter.3
  460.5 38.9 reduce-scatter.5
  546.1 82.7 reduce-scatter.7

commit v5 on v4

--- a/solution.py
+++ b/solution.py
@@ -472,7 +472,9 @@
         mine.start()
         for step, peer in enumerate(peers[n]):
             copies.append(send(src, dst.at[lax.axis_index(axis)], sems, step, {axis: peer}))
-        mine.wait()
+        copies.append(mine)
+    steps = gather_rows(full, (r.ag_send, r.ag_recv), place, r.x.at[lax.axis_index(TP)])
+    next(steps)
     packed = [getattr(r, f"packed_{layer}") for layer in range(r.gate.shape[0])]
     layers, units = len(packed), r.turned.shape[1]
     loads = []
@@ -486,8 +488,6 @@
             loads.append(pltpu.make_async_copy(src, dst, r.load.at[3 + 3 * layer + n]))
     for load in loads:
         load.start()
-    steps = gather_rows(full, (r.ag_send, r.ag_recv), place, r.x.at[lax.axis_index(TP)])
-    next(steps)
     own.wait()
     for copy in copies:
         copy.wait()
@@ -510,18 +510,18 @@
         block = 96
         query = lax.broadcasted_iota(jnp.int32, (1, length), 1)
         firsts = [r.starts[0:1, n : n + 1] for n in range(r.starts.shape[1])]
-        in_query = [jnp.where((query >= f) & (query < f + PIECE_LEN), 1, 0) for f in firsts]
+        in_query = [jnp.where((query >= f) & (query < f + PIECE_LEN), 1.0, 0.0) for f in firsts]
         for owner in range(r.all_places.shape[0]):
             @pl.loop(0, rows // block)
             def _(i):
                 here = pl.ds(pl.multiple_of(i * block, block), block)
                 key = owner * rows + i * block + lax.broadcasted_iota(jnp.int32, (block, 1), 0)
-                valid = r.all_places[owner, here, 1:2]
+                valid = r.all_places[owner, here, HEAD_DIM : HEAD_DIM + 1]
                 seen = 0
                 for f, row in zip(firsts, in_query):
-                    seen += jnp.where((key >= f) & (key < f + PIECE_LEN), 1, 0) * row
-                seen = jnp.where(key <= query, 1, seen) * valid
-                seen = jnp.where(key == query, 1, seen)
+                    seen += jnp.where((key >= f) & (key < f + PIECE_LEN), 1.0, 0.0) * row
+                seen = jnp.where(key <= query, 1.0, seen) * valid
+                seen = jnp.where(key == query, 1.0, seen)
                 added = jnp.where(seen > 0, 0.0, neg_big).astype(jnp.bfloat16)
                 keys = pl.ds(pl.multiple_of(owner * rows + i * block, block), block)
                 for n in range(r.all_places.shape[0]):
@@ -531,6 +531,13 @@
     norm(me, me)
     mask()
     r.keep("bias")
+    half_dim = HEAD_DIM // 2
+    for owner in range(r.all_places.shape[0]):
+        table = r.all_places[owner]
+        cos_b, sin_b = table[:, :half_dim], table[:, half_dim:HEAD_DIM]
+        r.cosine[owner] = jnp.concatenate([cos_b, cos_b], axis=1)
+        r.sine[owner] = jnp.concatenate([-sin_b, sin_b], axis=1)
+    r.keep("cosine", "sine")
     next(steps)
     norm(side_x, side_y)
     for load in loads:
@@ -602,6 +609,7 @@
     r.attn_stats = [r.attn_stats_0, r.attn_stats_1]
     r.mlp_stats = [r.mlp_stats_0, r.mlp_stats_1]
     counts = stat_steps(r, place)
+    next(counts)
     copies = []
     for part_no in range(2):
         copies.append([])
@@ -614,10 +622,6 @@
     next(first)
     next(counts)
     next(first)
-    next(counts)
-    next(counts)
-    next(counts)
-    run(counts)
     step = 48
     lasts = (r.last_0, r.last_1)
     steps = []
@@ -637,12 +641,16 @@
         steps.append(gather_rows(lasts[part_no], ((r.l0_send, r.l0_recv), (r.l1_send, r.l1_recv))[part_no], place, lasts[part_no].at[me]))
         next(steps[part_no])
         if part_no == 0:
-            next(steps[0])
+            next(counts)
+    next(steps[0])
+    next(counts)
+    next(steps[1])
     run(first)
     mine.wait()
     r.keep("gathered")
     run(steps[0])
     run(steps[1])
+    run(counts)
     for copy in copies[0] + copies[1]:
         copy.wait_send()
 
@@ -932,10 +940,6 @@
     gathered_work(r, place, scatter, both_rows if both else back_rows, r.rows_own, own, not both)
     if both:
         r.keep("part_out")
-        job = None
-    else:
-        job = gather_part(r.share, 0, r.gathered, r.load.at[1], r.ja_send, r.ja_recv, place)
-        next(job)
     normed, grad = (r.full, r.grad_all) if both else (r.normed, r.full)
     r.need("normed", "hidden")
     units = r.hidden.shape[-1]
@@ -947,10 +951,11 @@
     sums.theirs(0)
     sums.theirs(1)
     scatter.forward()
+    job = None if both else gather_part(r.share, 0, r.gathered, r.load.at[1], r.ja_send, r.ja_recv, place)
+    if job:
+        next(job)
     sums.theirs(2)
     sums.ours(0)
-    if job:
-        next(job)
     sums.ours(1)
     sums.ours(2)
     sums.add_up()
@@ -962,6 +967,8 @@
         r.grad_new[rows, :] = total
         r.grad_rows[rows, :] = total.astype(r.grad_rows.dtype)
 
+    if job:
+        next(job)
     norm_sum_back(scatter, r.middle, r.gain, r.grad, r.gain_rows, put)
     if job:
         run(job)
@@ -1164,6 +1171,9 @@
         r.part[owner] = total.astype(r.part.dtype)
 
     scatter = Scatter(r.part, (r.from_x, r.from_y, r.passed, r.last), (r.rs_send, r.rs_recv), place)
+    if not last:
+        for job in jobs:
+            next(job)
     branch(across)
     scatter.across()
     branch(side_x)
@@ -1178,15 +1188,20 @@
         r.summed, (r.tp_send, r.tp_recv),
     )
     sums.theirs(0)
-    for job in jobs:
-        next(job)
     scatter.forward()
+    if last:
+        for job in jobs:
+            next(job)
     sums.theirs(1)
     sums.ours(0)
     sums.ours(1)
     r.summed[:, base + cols_q :] = jnp.zeros((r.summed.shape[0], r.summed.shape[1] - base - cols_q), jnp.bfloat16)
     sums.add_up()
     r.keep("summed")
+    if not last:
+        for job in jobs:
+            run(job)
+        r.keep("out")
     scatter.finish()
     r.need("stream", "grad")
     side = lax.axis_index(TP)
@@ -1202,12 +1217,10 @@
     handed = []
     if last:
         handed.append(send(r.grad_new.at[side], r.grad_new.at[side], (r.tp_send, r.tp_recv), 2, sibling()))
-    for job in jobs:
-        run(job)
     if last:
+        for job in jobs:
+            run(job)
         r.keep("gathered_a", "gathered_b")
-    else:
-        r.keep("out")
     for copy in handed:
         copy.wait()
     sums.close()
@@ -1484,14 +1497,15 @@
         dict(gains=gains, places=places, starts=starts), dict(x=x, gate=gate, up=up, down=down), {},
         dict(
             all_gains=jax.ShapeDtypeStruct((depth, *gains.shape), gains.dtype),
-            all_places=jax.ShapeDtypeStruct((across, *places.shape), places.dtype),
             normed=shape16(across, *own),
         ),
         dict(
-            bias=shape16(across, length, 2 * own[0]),
+            bias=shape16(across, length, 2 * own[0]), cosine=shape32(across, own[0], HEAD_DIM),
+            sine=shape32(across, own[0], HEAD_DIM),
             **{f"packed_{layer}": shape16(rows, 3 * units) for layer in range(layers)},
         ),
         dict(
+            all_places=pltpu.VMEM((across, *places.shape), places.dtype),
             full=pltpu.VMEM((across, *own), jnp.bfloat16), turned=pltpu.VMEM((layers, units, rows), jnp.bfloat16),
             load=pltpu.SemaphoreType.DMA((3 + 3 * layers,)), **sems("gain", depth), **sems("place", across),
             **sems("ag", 6),
@@ -1530,7 +1544,7 @@
     def pack(*pieces):
         return with_layout_constraint(jnp.concatenate(pieces, axis=1), Layout(major_to_minor=(0, 1)))
 
-    def pack_attn(layer):
+    def pack_attn(layer, w_query, w_key, w_value, w_out):
         return pack(
             cut(w_query[layer], 1, cols_q),
             cut(w_key[layer], 1, cols_k),
@@ -1539,35 +1553,24 @@
             jnp.zeros((w_query.shape[1], 64), w_query.dtype),
         )
 
-    attn_w = [whole(pack_attn(0))]
-    packed_attn = [None] + [pack_attn(layer) for layer in range(1, layers)]
-    mlp_w = []
-    seq_pos, seq_valid = own(positions), own(valid)
-    starts = own(piece_starts)
+    attn_w = [whole(pack_attn(0, w_query, w_key, w_value, w_out))]
+    seq_pos, valid_f = own(positions), own(valid).astype(jnp.float32)[:, None]
+    half_dim = HEAD_DIM // 2
+    freqs = rope_base ** (-(jnp.arange(half_dim).astype(jnp.float32) * 2.0 / HEAD_DIM))
+    angles = seq_pos.astype(jnp.float32)[:, None] * freqs
     begun = start_step(
         jnp.pad(jnp.concatenate([attn_gain, mlp_gain], 0).astype(jnp.float32), ((0, 8 - 2 * layers), (0, 0))),
-        jnp.pad(jnp.stack([seq_pos, seq_valid], axis=1), ((0, 0), (0, 6))),
-        starts[None], tokens, w_gate, w_up, w_down,
+        jnp.concatenate([jnp.cos(angles), jnp.sin(angles), valid_f, jnp.zeros((rows, 127 - HEAD_DIM), jnp.float32)], axis=1),
+        own(piece_starts)[None], tokens, w_gate, w_up, w_down,
     )
     normed, bias = begun.normed, begun.bias
     packed_mlp = [getattr(begun, f"packed_{layer}") for layer in range(layers)]
     gains = begun.all_gains.swapaxes(0, 1).reshape(8, width)
-    places = begun.all_places
+    cosine, sine_t = begun.cosine, begun.sine
     gain_a = [gains[layer][None] for layer in range(layers)]
     gain_m = [gains[layers + layer][None] for layer in range(layers)]
-    pos_all = places[:, :, 0].reshape(length)
-    valid_f = seq_valid.astype(jnp.float32)[:, None]
     grad = (d_out,)
-    mlp_w.append(whole(packed_mlp[0]))
-    half_dim = HEAD_DIM // 2
-    freqs = rope_base ** (-(jnp.arange(half_dim).astype(jnp.float32) * 2.0 / HEAD_DIM))
-    angles = pos_all.astype(jnp.float32)[:, None] * freqs
-    cosine, sine_t = jnp.cos(angles), jnp.sin(angles)
-    cosine = jnp.concatenate([cosine, cosine], axis=1)
-    sine_t = jnp.concatenate([-sine_t, sine_t], axis=1)
-    cosine, sine_t = lax.optimization_barrier(
-        (cosine.reshape(ctx_count, rows, HEAD_DIM), sine_t.reshape(ctx_count, rows, HEAD_DIM))
-    )
+    mlp_w = [whole(packed_mlp[0])]
 
     streams, attends, mlps = [(tokens,)], [], []
     for layer in range(layers):
@@ -1579,10 +1582,10 @@
             grad_all, kept.full = kept.full, normed
         attends.append(kept)
         if layer + 1 < layers:
-            normed_m, packed_attn[layer + 1], packed_mlp[layer + 1] = lax.optimization_barrier(
-                (kept.normed_next, packed_attn[layer + 1], packed_mlp[layer + 1])
+            normed_m, w_query, w_key, w_value, w_out, packed_mlp[layer + 1] = lax.optimization_barrier(
+                (kept.normed_next, w_query, w_key, w_value, w_out, packed_mlp[layer + 1])
             )
-            attn_w.append(whole(packed_attn[layer + 1]))
+            attn_w.append(whole(pack_attn(layer + 1, w_query, w_key, w_value, w_out)))
             mlp_w.append(whole(packed_mlp[layer + 1]))
             mlps.append(mlp_step(normed_m, kept.middle, gain_a[layer + 1], valid_f, mlp_w[layer]))
             streams.append(mlps[layer].stream)
@@ -1627,24 +1630,30 @@
         attn_all, mlp_all,
         [(0, cols_q, False), (cols_q, cols_k, False), (cols_q + cols_k, cols_k, False), (base, cols_q, True)],
         [(0, units, False), (units, units, False), (2 * units, units, True)],
+        [output, input_grad],
     )
     gains = ended.gains
     return (
-        output, input_grad, gains[:layers], *placed[:4], gains[layers : 2 * layers], *placed[4:], rms_stats,
-    )
-
-
-def place_kernel(moves, count, *refs):
+        *placed[7:], gains[:layers], *placed[:4], gains[layers : 2 * layers], *placed[4:7], rms_stats,
+    )
+
+
+def place_kernel(moves, count, more, *refs):
     refs = list(refs)
     outs_count = 1 + max(out for _, _, pieces in moves for _, _, _, out in pieces)
-    ins, outs = refs[:count], refs[count : count + outs_count]
-    del refs[: count + outs_count]
-    held, laid = refs[:count], refs[count:-2]
+    ins, outs = refs[: count + more], refs[count + more : count + outs_count + 2 * more]
+    del refs[: count + outs_count + 2 * more]
+    held, laid = refs[: count + more], refs[count + more : -2]
     in_sems, out_sems = refs[-2:]
-    loads = [pltpu.make_async_copy(ins[n], held[n], in_sems.at[n]) for n in range(count)]
+    loads = [pltpu.make_async_copy(ins[n], held[n], in_sems.at[n]) for n in range(count + more)]
     for load in loads:
         load.start()
     stores = []
+    for n in range(more):
+        loads[count + n].wait()
+        store = pltpu.make_async_copy(held[count + n], outs[outs_count + n], out_sems.at[len(stores)])
+        store.start()
+        stores.append(store)
     for n, (layer, first, pieces) in enumerate(moves):
         loads[n].wait()
         rows = held[n].shape[1]
@@ -1664,7 +1673,7 @@
         store.wait()
 
 
-def place_outs(attn_all, mlp_all, attn_pieces, mlp_pieces):
+def place_outs(attn_all, mlp_all, attn_pieces, mlp_pieces, handed):
     layers = len(attn_all)
     shapes = []
     for came, pieces in ((attn_all, attn_pieces), (mlp_all, mlp_pieces)):
@@ -1683,15 +1692,17 @@
                 first += a.shape[1]
     hbm = pl.BlockSpec(memory_space=pl.ANY)
     return pl.pallas_call(
-        functools.partial(place_kernel, moves, len(ins)),
-        out_shape=[jax.ShapeDtypeStruct(s, jnp.float32) for s in shapes],
-        in_specs=[hbm] * len(ins),
-        out_specs=[hbm] * len(shapes),
-        scratch_shapes=[pltpu.VMEM(a.shape, a.dtype) for a in ins]
+        functools.partial(place_kernel, moves, len(ins), len(handed)),
+        out_shape=[jax.ShapeDtypeStruct(s, jnp.float32) for s in shapes]
+        + [jax.ShapeDtypeStruct(a.shape, a.dtype) for a in handed],
+        in_specs=[hbm] * (len(ins) + len(handed)),
+        out_specs=[hbm] * (len(shapes) + len(handed)),
+        scratch_shapes=[pltpu.VMEM(a.shape, a.dtype) for a in ins + handed]
         + [pltpu.VMEM(s, jnp.float32) for s in shapes]
-        + [pltpu.SemaphoreType.DMA((len(ins),)), pltpu.SemaphoreType.DMA((layers * len(shapes),))],
+        + [pltpu.SemaphoreType.DMA((len(ins) + len(handed),)),
+           pltpu.SemaphoreType.DMA((layers * len(shapes) + len(handed),))],
         compiler_params=pltpu.CompilerParams(vmem_limit_bytes=60 << 20),
-    )(*ins)
+    )(*ins, *handed)
 
 
 def fits(mesh):

time: 753 us -> 727 us (0.965)
  Pallas kernels: 692 us -> 675 us
    pallas_call x9, Pallas kernels: 679 us -> 658 us  [linked(): pl.pallas_call(body, out_shape=[*outs.values(), *late.values()], in_specs...]
  transfers between devices with their start and end apart: 7 -> 7, of which waited for: 1 -> 1; matrix products, arithmetic and copies ran while one was open for 1% -> 1% of each run, Pallas kernels for 72% -> 73%
where the time goes in v5:
time: 727 us; the launch traced here: 723 us
  Pallas kernels  675 us (93%)
  waiting for transfers between devices  19.6 us (3%)
  between operations  14.8 us (2%)
  local copies, waits for them, and re-layouts  11.3 us (2%)
    pallas_call x9, Pallas kernels, linked(): pl.pallas_call(body, out_shape=[*outs.values(), *late.values()], in_specs...  658 us
    all_gather x4, waiting for transfers between devices, whole(): lax.all_gather(w, (TP, FSDP), axis=0, tiled=True)  18.9 us
    pallas_call x1, Pallas kernels, place_outs(): pl.pallas_call(functools.partial(place_kernel, moves, len(ins), len(hande...  16.4 us
  transfers between devices with their start and end apart: 7, of which 1 were waited for; matrix products, arithmetic and copies ran while one was open for 1% of the time, Pallas kernels for 73%

profile of v5, /device:TPU:0, one launch (start us, length us, event | category | flops | bytes accessed | tf_op | source)
XLA Modules:
  0.0 723.1 jit_solution(8785641644396544522)
XLA Ops:
  7.3 1.1 slice.64
  8.4 1.0 slice.65
  9.6 0.1 dynamic-slice_bitcast_fusion.1
  9.8 0.1 copy.29
  10.0 1.1 concatenate.14
  11.2 0.1 copy.28.refs_1_
  11.4 0.5 constant_dynamic-slice_fusion.2.refs_2_
  12.0 0.6 fusion.3.refs_0_
  12.6 0.6 multiply_cosine_fusion
  13.2 0.8 maximum_maximum_fusion.refs_1_
  14.0 46.9 %shard_map.229 = (f32[4,8,384]{2,1,0:T(8,128)}, bf16[4,288,1536]{2,1,0:T(8,128)(2,1)}, bf16[4,1152,576]{2,1,0:T(8,128)(2,1)}, f32[4,288,96]{2,1,0:T(8,128)}, f32...) custom-call(f32[8,384]{1,0:T(8,128)} %fusion.3.refs_0_, ...), custom_call_target="tpu_custom_call" | custom-call | bytes 136800000 | tf_op jit(solution)/shard_map/pallas_call | solution.py:1303
  60.9 0.2 all-gather.9.cloned.1.call-start
  61.2 1.6 fusion.8
  62.7 65.1 %shard_map.230 = (f32[288,1536]{1,0:T(8,128)}, bf16[288,1536]{1,0:T(8,128)(2,1)}, f32[16,128]{1,0:T(8,128)}, bf16[4,288,1536]{2,1,0:T(8,128)(2,1)}, bf16[2,2,4,2...) custom-call(f32[1,1536]{1,0:T(1,128)} %bitcast.38, ...), custom_call_target="tpu_custom_call" | custom-call | bytes 270000000 | tf_op jit(solution)/shard_map/pallas_call | solution.py:1303
  127.9 1.0 slice-done.3
  128.9 0.1 copy.32
  129.1 0.1 dynamic-slice_bitcast_fusion
  129.4 1.1 concatenate.15
  130.5 0.5 all-gather.11.cloned.1.call-update
  131.1 18.9 %all-gather.7.cloned.1.call-done = bf16[3072,1536]{1,0:T(8,128)(2,1)} async-done(((bf16[384,1536]{1,0:T(8,128)(2,1)}), bf16[3072,1536]{1,0:T(8,128)(2,1)}) %all-gather.7.cloned.1.call-update) | async-done | bytes 9437200 | tf_op jit(solution)/shard_map/all_gather | solution.py:1540
  150.0 68.0 %shard_map.231 = (f32[288,1536]{1,0:T(8,128)}, bf16[288,1536]{1,0:T(8,128)(2,1)}, f32[16,128]{1,0:T(8,128)}, bf16[4,288,1536]{2,1,0:T(8,128)(2,1)}, bf16[2,4,288...) custom-call(f32[1,1536]{1,0:T(1,128)} %bitcast.42, f32[288,1]{1,0:T(8,128)} %copy-done.2, ...), custom_call_target="tpu_custom_call" | custom-call | bytes 270000000 | tf_op jit(solution)/shard_map/pallas_call | solution.py:1303
  218.0 68.8 %shard_map.232 = (f32[288,1536]{1,0:T(8,128)}, bf16[288,1536]{1,0:T(8,128)(2,1)}, f32[16,128]{1,0:T(8,128)}, bf16[4,288,1536]{2,1,0:T(8,128)(2,1)}, bf16[2,2,4,2...) custom-call(f32[1,1536]{1,0:T(1,128)} %bitcast.40, ...), custom_call_target="tpu_custom_call" | custom-call | bytes 270000000 | tf_op jit(solution)/shard_map/pallas_call | solution.py:1303
  286.8 70.8 %shard_map.233 = (f32[288,1536]{1,0:T(8,128)}, bf16[288,1536]{1,0:T(8,128)(2,1)}, f32[16,1536]{1,0:T(8,128)}, bf16[1536,1536]{1,0:T(8,128)(2,1)}, bf16[4,288,1536]{2,1,0:T(8,128)(2,1)}) custom-call(f32[1,1536]{1,0:T(1,128)} %bitcast.41, bf16[288,1536]{1,0:T(8,128)(2,1)} %get-tuple-element.104.refs_1_, bf16[2,1536,1536]{2,1,0:T(8,128)(2,1)} %bitcast.35, ...), custom_call_target="tpu_custom_call" | custom-call | bytes 306000000 | tf_op jit(solution)/shard_map/pallas_call | solution.py:1303
  357.6 93.2 %shard_map.234 = (f32[16,1536]{1,0:T(8,128)}, f32[288,1536]{1,0:T(8,128)}, bf16[288,1536]{1,0:T(8,128)(2,1)}, f32[16,128]{1,0:T(8,128)}, bf16[1536,640]{1,0:T(8,128)(2,1)}, /*index=5*/bf16[2,288,1536]{2,1,0:T(8,128)(2,1)}) custom-call(f32[1,1536]{1,0:T(1,128)} %bitcast.43, f32[288,1]{1,0:T(8,128)} %copy-done.2, ...), custom_call_target="tpu_custom_call" | custom-call | bytes 360000000 | tf_op jit(solution)/shard_map/pallas_call | solution.py:1303
  450.9 0.4 reduce-scatter.8.cloned.1.call-start
  451.4 83.2 %shard_map.235 = (f32[288,1536]{1,0:T(8,128)}, bf16[288,1536]{1,0:T(8,128)(2,1)}, f32[16,1536]{1,0:T(8,128)}, bf16[1536,1536]{1,0:T(8,128)(2,1)}, bf16[4,192,1536]{2,1,0:T(8,128)(2,1)}) custom-call(f32[1,1536]{1,0:T(1,128)} %bitcast.39, bf16[288,1536]{1,0:T(8,128)(2,1)} %get-tuple-element.120.refs_1_, ...), custom_call_target="tpu_custom_call" | custom-call | bytes 306000000 | tf_op jit(solution)/shard_map/pallas_call | solution.py:1303
  534.6 100.8 %shard_map.236 = (f32[16,1536]{1,0:T(8,128)}, f32[2,288,1536]{2,1,0:T(8,128)}, bf16[1536,640]{1,0:T(8,128)(2,1)}, bf16[4,192,1536]{2,1,0:T(8,128)(2,1)}, bf16[4,384,640]{2,1,0:T(8,128)(2,1)}) custom-call(f32[1,1536]{1,0:T(1,128)} %bitcast.44, bf16[288,1536]{1,0:T(8,128)(2,1)} %get-tuple-element.128.refs_1_, ...), custom_call_target="tpu_custom_call" | custom-call | bytes 360000000 | tf_op jit(solution)/shard_map/pallas_call | solution.py:1303
  635.5 61.5 %shard_map.237 = (bf16[4,192,640]{2,1,0:T(8,128)(2,1)}, bf16[4,192,640]{2,1,0:T(8,128)(2,1)}, f32[8,128]{1,0:T(8,128)}, f32[8,384]{1,0:T(8,128)}, bf16[4,384,1536]{2,1,0:T(8,128)(2,1)}) custom-call(bf16[1536,640]{1,0:T(8,128)(2,1)} %get-tuple-element.138.refs_0_, f32[16,128]{1,0:T(8,128)} %get-tuple-element.139.refs_1_, ...), custom_call_target="tpu_custom_call" | custom-call | bytes 216000000 | tf_op jit(solution)/shard_map/pallas_call | solution.py:1303
  697.0 0.7 slice_reduce_fusion
  697.7 0.6 reshape_squeeze.3
  698.3 1.4 fusion.9
  699.7 16.4 %shard_map.238 = (f32[2,384,768]{2,1,0:T(8,128)}, f32[2,384,384]{2,1,0:T(8,128)}, f32[2,384,384]{2,1,0:T(8,128)}, f32[2,768,384]{2,1,0:T(8,128)}, f32[2,384,2048...) custom-call(bf16[4,192,1536]{2,1,0:T(8,128)(2,1)} %get-tuple-element, ...), custom_call_target="tpu_custom_call" | custom-call | tf_op jit(solution)/shard_map/pallas_call | solution.py:1694
  (53 shorter events, 1.0 us)
Async XLA Ops:
  7.2 4.3 copy-start
  7.2 2.4 slice-start
  7.2 2.6 slice-start.2
  7.2 55.5 %all-gather.5.cloned.1.call-start = ((), (), s32[]{:S(2)}) async-start(), calls=%async_computation.3 | async-start | bytes 4423680 | tf_op jit(solution)/shard_map/all_gather | solution.py:1540
  9.6 1.6 copy-start.5
  9.6 1.8 copy-start.6
  9.6 2.4 copy-start.3
  9.6 2.4 copy-start.4
  11.1 138.9 %all-gather.7.cloned.1.call-start = ((), (), s32[]{:S(2)}) async-start(), calls=%async_computation.4 | async-start | bytes 10616832 | tf_op jit(solution)/shard_map/all_gather | solution.py:1540
  11.3 49.6 %copy-start.2 = (f32[288,1]{1,0:T(8,128)}, f32[288,1]{1,0:T(8,128)S(1)}, u32[]{:S(2)}) copy-start(f32[288,1]{1,0:T(8,128)S(1)} %copy.28.refs_1_) | copy-start | bytes 3460
  60.9 157.0 %all-gather.9.cloned.1.call-start = ((), (), s32[]{:S(2)}) async-start(), calls=%async_computation.5 | async-start | bytes 4423680 | tf_op jit(solution)/shard_map/all_gather | solution.py:1540
  127.9 1.1 slice-start.3
  127.9 1.2 slice-start.1
  127.9 1.4 slice-start.4
  127.9 1.4 slice-start.5
  130.5 156.3 %all-gather.11.cloned.1.call-start = ((), (), s32[]{:S(2)}) async-start(), calls=%async_computation.6 | async-start | bytes 10616832 | tf_op jit(solution)/shard_map/all_gather | solution.py:1540
  131.1 319.8 %reduce-scatter.4.cloned.1.call-start = ((), (), s32[]{:S(2)}) async-start(), calls=%async_computation.7 | async-start | bytes 5898240 | tf_op jit(solution)/shard_map/reduce_scatter | solution.py:1595
  357.6 177.0 %reduce-scatter.6.cloned.1.call-start = ((), (), s32[]{:S(2)}) async-start(), calls=%async_computation.8 | async-start | bytes 2457600 | tf_op jit(solution)/shard_map/reduce_scatter | solution.py:1595
  450.9 184.6 %reduce-scatter.8.cloned.1.call-start = ((), (), s32[]{:S(2)}) async-start(), calls=%async_computation.9 | async-start | bytes 5898240 | tf_op jit(solution)/shard_map/reduce_scatter | solution.py:1595
  699.7 16.4 %copy-start.1 = (s32[2,2]{1,0:T(2,128)S(1)}, s32[2,2]{1,0:T(2,128)}, u32[]{:S(2)}) copy-start(s32[2,2]{1,0:T(2,128)} %param.17) | copy-start | bytes 52
Sparse Core Ops, SparseCore 0:
  11.2 47.5 all-gather.4
  61.1 88.8 all-gather.6
  152.1 43.2 all-gather.8
  196.8 89.5 all-gather.10
  357.7 82.7 reduce-scatter.3
  451.0 38.9 reduce-scatter.5
  534.7 83.4 reduce-scatter.7

commit v6 on v5

--- a/solution.py
+++ b/solution.py
@@ -462,6 +462,10 @@
     for axis, _, _, _ in groups:
         count = lax.axis_size(axis)
         peers.append([lax.rem(lax.axis_index(axis) + step, count) for step in range(1, count)])
+    layers = r.attn_gain.shape[0]
+    r.gains[...] = jnp.zeros_like(r.gains)
+    r.gains[0:layers, :] = r.attn_gain[...].astype(jnp.float32)
+    r.gains[layers : 2 * layers, :] = r.mlp_gain[...].astype(jnp.float32)
     full = r.full
     own = pltpu.make_async_copy(r.x.at[lax.axis_index(TP)], full.at[me], r.load.at[0])
     own.start()
@@ -509,7 +513,8 @@
         length = r.bias.shape[1]
         block = 96
         query = lax.broadcasted_iota(jnp.int32, (1, length), 1)
-        firsts = [r.starts[0:1, n : n + 1] for n in range(r.starts.shape[1])]
+        here = r.starts[pl.ds(lax.axis_index(TP), 1), :]
+        firsts = [here[:, n : n + 1] for n in range(r.starts.shape[1])]
         in_query = [jnp.where((query >= f) & (query < f + PIECE_LEN), 1.0, 0.0) for f in firsts]
         for owner in range(r.all_places.shape[0]):
             @pl.loop(0, rows // block)
@@ -687,44 +692,51 @@
         first = self.half // 48 * 16
         return (2, pl.ds(0, first)) if some == 0 else (6, pl.ds(first, self.half - first))
 
-    def add_to(self, slot, owner, start, came):
+    def pieces(self):
+        first = self.half // 32 * 16
+        return (0, first), (first, self.half - first)
+
+    def pass_on(self, side, owner, came, axis_peer):
+        self.copies[side].wait_recv()
         step = 16
-
-        @pl.loop(0, self.half // step)
-        def _(i):
-            rows = pl.ds(pl.multiple_of(i * step, step), step)
-            mine = self.part[owner, pl.ds(pl.multiple_of(start + i * step, step), step), :]
-            total = mine.astype(jnp.float32) + came[1, rows, :].astype(jnp.float32)
-            self.passed[slot, rows, :] = total.astype(self.passed.dtype)
+        for n, (first, count) in enumerate(self.pieces()):
+            @pl.loop(0, count // step)
+            def _(i):
+                rows = pl.ds(pl.multiple_of(first + i * step, step), step)
+                mine = self.part[owner, pl.ds(pl.multiple_of(side * self.half + first + i * step, step), step), :]
+                total = mine.astype(jnp.float32) + came[1, rows, :].astype(jnp.float32)
+                self.passed[side, rows, :] = total.astype(self.passed.dtype)
+
+            piece = pl.ds(first, count)
+            self.send(4 + side + 4 * n, self.passed.at[side, piece], self.last.at[side, piece], axis_peer)
 
     def forward(self):
         _, side_x, side_y, _ = self.place
-        self.copies[0].wait_recv()
-        self.add_to(0, side_y, 0, self.from_x)
-        self.send(4, self.passed.at[0], self.last.at[0], side_y)
-        self.copies[1].wait_recv()
-        self.add_to(1, side_x, self.half, self.from_y)
-        self.send(5, self.passed.at[1], self.last.at[1], side_x)
+        self.pass_on(0, side_y, self.from_x, side_y)
+        self.pass_on(1, side_x, self.from_y, side_x)
 
     def finish(self):
         for slot in self.copies:
-            if slot > 1:
+            if 1 < slot < 8:
                 self.copies[slot].wait_recv()
-        for slot in self.copies:
-            self.copies[slot].wait_send()
 
     def each_row(self, work, step=16):
         me = self.place[0]
-        for side in range(2):
-            came = self.from_x if side == 0 else self.from_y
-
-            @pl.loop(0, self.half // step)
-            def _(i):
-                rows = pl.ds(pl.multiple_of(i * step, step), step)
-                whole = pl.ds(pl.multiple_of(side * self.half + i * step, step), step)
-                total = self.part[me, whole, :].astype(jnp.float32)
-                total += came[0, rows, :].astype(jnp.float32)
-                work(whole, total + self.last[side, rows, :].astype(jnp.float32))
+        for n, (first, count) in enumerate(self.pieces()):
+            for side in range(2):
+                if n == 1:
+                    self.copies[8 + side].wait_recv()
+                came = self.from_x if side == 0 else self.from_y
+
+                @pl.loop(0, count // step)
+                def _(i):
+                    rows = pl.ds(pl.multiple_of(first + i * step, step), step)
+                    whole = pl.ds(pl.multiple_of(side * self.half + first + i * step, step), step)
+                    total = self.part[me, whole, :].astype(jnp.float32)
+                    total += came[0, rows, :].astype(jnp.float32)
+                    work(whole, total + self.last[side, rows, :].astype(jnp.float32))
+        for copy in self.copies.values():
+            copy.wait_send()
 
 
 def scatter_steps(scatter):
@@ -745,7 +757,7 @@
         self.copies = []
 
     def product(self, p, t, put):
-        block = 256
+        block = 768
         left, right = self.lefts[p], self.rights[p]
         width = left.shape[-1]
 
@@ -1352,7 +1364,7 @@
         dict(full=shape16(4, rows, width), hidden=kept, gate=kept, up=kept),
         dict(
             part=pltpu.VMEM((4, rows, width), jnp.bfloat16), load=pltpu.SemaphoreType.DMA((1,)),
-            **sum_room(rows, width), **sems("ag", 6), **sems("rs", 8),
+            **sum_room(rows, width), **sems("ag", 6), **sems("rs", 10),
         ),
     )
 
@@ -1368,7 +1380,7 @@
     scratch = dict(
         full=room(whole), part=room(whole), load=pltpu.SemaphoreType.DMA((2,)),
         **{f"came_{p}": pltpu.VMEM((width, units), jnp.bfloat16) for p in range(3)},
-        **sum_room(rows, width), **sems("ag", 6), **sems("rs", 8), **sems(TP, 3),
+        **sum_room(rows, width), **sems("ag", 6), **sems("rs", 10), **sems(TP, 3),
     )
     if both:
         lazy["grad_all"] = grad_all
@@ -1410,7 +1422,7 @@
         ),
         dict(
             part=pltpu.VMEM((4, rows, width), jnp.bfloat16), load=pltpu.SemaphoreType.DMA((1,)),
-            **sum_room(rows, width), **sems("ag", 6), **sems("rs", 8),
+            **sum_room(rows, width), **sems("ag", 6), **sems("rs", 10),
         ),
     )
 
@@ -1441,7 +1453,7 @@
         bias=pltpu.VMEM((2, length, 2 * rows), jnp.bfloat16), bias_load=pltpu.SemaphoreType.DMA((4,)),
         came_0=pltpu.VMEM((width, sizes[0]), jnp.bfloat16), came_1=pltpu.VMEM((width, 256), jnp.bfloat16),
         load=pltpu.SemaphoreType.DMA((3,)),
-        **sum_room(rows, width), **sems("ag", 6), **sems("rs", 8), **sems(TP, 4),
+        **sum_room(rows, width), **sems("ag", 6), **sems("rs", 10), **sems(TP, 4),
     )
     if last:
         far.update(share_a=shares[0], share_b=shares[1])
@@ -1456,7 +1468,7 @@
         near["valid"] = end[2]
         outs.update(grad_new=shape32(rows, width), grad_rows=shape16(rows, width), stats=shape32(16, 128))
         late["out"] = shape16(2, rows, width)
-        scratch.update(**sum_room(rows, width, "end_"), **sems("end", 6), **sems("out", 1))
+        scratch.update(**sum_room(rows, width, "end_"), **sems("end", 10), **sems("out", 1))
     return linked(
         functools.partial(attend_back_kernel, last), 7 if last else 6, 100, near, far, lazy, outs, late, scratch,
     )
@@ -1486,7 +1498,7 @@
     )
 
 
-def start_step(gains, places, starts, x, gate, up, down):
+def start_step(attn_gain, mlp_gain, places, starts, x, gate, up, down):
     depth, across = lax.axis_size(FSDP), lax.axis_size(CTX)
     layers, rows = gate.shape[:2]
     units = gate.shape[2] // across
@@ -1494,9 +1506,9 @@
     length = across * own[0]
     return linked(
         start_kernel, 8, 38,
-        dict(gains=gains, places=places, starts=starts), dict(x=x, gate=gate, up=up, down=down), {},
+        dict(attn_gain=attn_gain, mlp_gain=mlp_gain, places=places, starts=starts), dict(x=x, gate=gate, up=up, down=down), {},
         dict(
-            all_gains=jax.ShapeDtypeStruct((depth, *gains.shape), gains.dtype),
+            all_gains=shape32(depth, 8, attn_gain.shape[1]),
             normed=shape16(across, *own),
         ),
         dict(
@@ -1505,6 +1517,7 @@
             **{f"packed_{layer}": shape16(rows, 3 * units) for layer in range(layers)},
         ),
         dict(
+            gains=pltpu.VMEM((8, attn_gain.shape[1]), jnp.float32),
             all_places=pltpu.VMEM((across, *places.shape), places.dtype),
             full=pltpu.VMEM((across, *own), jnp.bfloat16), turned=pltpu.VMEM((layers, units, rows), jnp.bfloat16),
             load=pltpu.SemaphoreType.DMA((3 + 3 * layers,)), **sems("gain", depth), **sems("place", across),
@@ -1559,9 +1572,9 @@
     freqs = rope_base ** (-(jnp.arange(half_dim).astype(jnp.float32) * 2.0 / HEAD_DIM))
     angles = seq_pos.astype(jnp.float32)[:, None] * freqs
     begun = start_step(
-        jnp.pad(jnp.concatenate([attn_gain, mlp_gain], 0).astype(jnp.float32), ((0, 8 - 2 * layers), (0, 0))),
+        attn_gain, mlp_gain,
         jnp.concatenate([jnp.cos(angles), jnp.sin(angles), valid_f, jnp.zeros((rows, 127 - HEAD_DIM), jnp.float32)], axis=1),
-        own(piece_starts)[None], tokens, w_gate, w_up, w_down,
+        piece_starts, tokens, w_gate, w_up, w_down,
     )
     normed, bias = begun.normed, begun.bias
     packed_mlp = [getattr(begun, f"packed_{layer}") for layer in range(layers)]
@@ -1624,38 +1637,40 @@
     input_grad = back.grad_new
     mlp_all = [[ended.gathered], [came.gathered, back.gathered_a]]
     attn_all = [[ended.last_0, ended.last_1], [back.gathered_b]]
-    rms_stats = ended.all_stats[0, : 3 * layers].reshape(layers, 3)
     base = cols_q + 2 * cols_k
     placed = place_outs(
         attn_all, mlp_all,
         [(0, cols_q, False), (cols_q, cols_k, False), (cols_q + cols_k, cols_k, False), (base, cols_q, True)],
         [(0, units, False), (units, units, False), (2 * units, units, True)],
-        [output, input_grad],
-    )
-    gains = ended.gains
-    return (
-        *placed[7:], gains[:layers], *placed[:4], gains[layers : 2 * layers], *placed[4:7], rms_stats,
-    )
+        [output, input_grad], [ended.gains, ended.all_stats],
+    )
+    return (*placed[7:9], placed[9], *placed[:4], placed[10], *placed[4:7], placed[11])
 
 
 def place_kernel(moves, count, more, *refs):
     refs = list(refs)
+    gains, stats = refs[:2]
+    del refs[:2]
     outs_count = 1 + max(out for _, _, pieces in moves for _, _, _, out in pieces)
     ins, outs = refs[: count + more], refs[count + more : count + outs_count + 2 * more]
     del refs[: count + outs_count + 2 * more]
+    attn_gain, mlp_gain, roots = refs[:3]
+    del refs[:3]
+    layers = attn_gain.shape[0]
+    attn_gain[...] = gains[0:layers, :]
+    mlp_gain[...] = gains[layers : 2 * layers, :]
+    for layer in range(layers):
+        roots[layer : layer + 1, :] = stats[0:1, 3 * layer : 3 * layer + 3]
     held, laid = refs[: count + more], refs[count + more : -2]
     in_sems, out_sems = refs[-2:]
     loads = [pltpu.make_async_copy(ins[n], held[n], in_sems.at[n]) for n in range(count + more)]
-    for load in loads:
+    for load in loads[:2]:
         load.start()
     stores = []
-    for n in range(more):
-        loads[count + n].wait()
-        store = pltpu.make_async_copy(held[count + n], outs[outs_count + n], out_sems.at[len(stores)])
-        store.start()
-        stores.append(store)
     for n, (layer, first, pieces) in enumerate(moves):
         loads[n].wait()
+        if n + 2 < len(loads):
+            loads[n + 2].start()
         rows = held[n].shape[1]
         for start, size, flip, out in pieces:
             for c in range(held[n].shape[0]):
@@ -1669,11 +1684,18 @@
             store = pltpu.make_async_copy(laid[out].at[layer], outs[out].at[layer], out_sems.at[len(stores)])
             store.start()
             stores.append(store)
+    for n in range(more):
+        if len(moves) + 2 <= count + n:
+            loads[count + n].start()
+        loads[count + n].wait()
+        store = pltpu.make_async_copy(held[count + n], outs[outs_count + n], out_sems.at[len(stores)])
+        store.start()
+        stores.append(store)
     for store in stores:
         store.wait()
 
 
-def place_outs(attn_all, mlp_all, attn_pieces, mlp_pieces, handed):
+def place_outs(attn_all, mlp_all, attn_pieces, mlp_pieces, handed, small):
     layers = len(attn_all)
     shapes = []
     for came, pieces in ((attn_all, attn_pieces), (mlp_all, mlp_pieces)):
@@ -1690,19 +1712,20 @@
                 ins.append(a)
                 moves.append((layer, first, [(*piece, base + n) for n, piece in enumerate(pieces)]))
                 first += a.shape[1]
-    hbm = pl.BlockSpec(memory_space=pl.ANY)
+    hbm, vmem = pl.BlockSpec(memory_space=pl.ANY), pl.BlockSpec(memory_space=pltpu.VMEM)
     return pl.pallas_call(
         functools.partial(place_kernel, moves, len(ins), len(handed)),
         out_shape=[jax.ShapeDtypeStruct(s, jnp.float32) for s in shapes]
-        + [jax.ShapeDtypeStruct(a.shape, a.dtype) for a in handed],
-        in_specs=[hbm] * (len(ins) + len(handed)),
-        out_specs=[hbm] * (len(shapes) + len(handed)),
+        + [jax.ShapeDtypeStruct(a.shape, a.dtype) for a in handed]
+        + [shape32(layers, small[0].shape[1])] * 2 + [shape32(layers, 3)],
+        in_specs=[vmem] * 2 + [hbm] * (len(ins) + len(handed)),
+        out_specs=[hbm] * (len(shapes) + len(handed)) + [vmem] * 3,
         scratch_shapes=[pltpu.VMEM(a.shape, a.dtype) for a in ins + handed]
         + [pltpu.VMEM(s, jnp.float32) for s in shapes]
         + [pltpu.SemaphoreType.DMA((len(ins) + len(handed),)),
            pltpu.SemaphoreType.DMA((layers * len(shapes) + len(handed),))],
         compiler_params=pltpu.CompilerParams(vmem_limit_bytes=60 << 20),
-    )(*ins, *handed)
+    )(*small, *ins, *handed)
 
 
 def fits(mesh):

time: 727 us -> 721 us (level)
    pallas_call x9, Pallas kernels: 658 us -> 650 us  [linked(): pl.pallas_call(body, out_shape=[*outs.values(), *late.values()], in_specs...]
  transfers between devices with their start and end apart: 7 -> 7, of which waited for: 1 -> 2; matrix products, arithmetic and copies ran while one was open for 1% -> 1% of each run, Pallas kernels for 73% -> 73%
where the time goes in v6:
time: 721 us; the launch traced here: 717 us
  Pallas kernels  668 us (93%)
  waiting for transfers between devices  24.6 us (3%)
  between operations  14.7 us (2%)
  local copies, waits for them, and re-layouts  8.01 us (1%)
    pallas_call x9, Pallas kernels, linked(): pl.pallas_call(body, out_shape=[*outs.values(), *late.values()], in_specs...  650 us
    all_gather x4, waiting for transfers between devices, whole(): lax.all_gather(w, (TP, FSDP), axis=0, tiled=True)  24 us
    pallas_call x1, Pallas kernels, place_outs(): pl.pallas_call(functools.partial(place_kernel, moves, len(ins), len(hande...  17.6 us
  transfers between devices with their start and end apart: 7, of which 2 were waited for; matrix products, arithmetic and copies ran while one was open for 1% of the time, Pallas kernels for 73%

profile of v6, /device:TPU:0, one launch (start us, length us, event | category | flops | bytes accessed | tf_op | source)
XLA Modules:
  0.0 717.2 jit_solution(13934697450735891232)
XLA Ops:
  7.3 1.1 slice.57
  8.3 1.0 slice.58
  9.3 0.1 dynamic-slice_bitcast_fusion.5
  9.4 0.1 dynamic-slice_bitcast_fusion.4
  9.6 0.1 dynamic-slice_bitcast_fusion.1
  9.8 0.1 copy.29
  10.0 1.1 concatenate.10
  11.1 0.1 copy.28.refs_1_
  11.3 0.1 pad.3.clone
  11.4 0.6 multiply_cosine_fusion
  12.0 0.8 maximum_maximum_fusion.refs_2_
  12.8 47.0 %shard_map.229 = (f32[4,8,384]{2,1,0:T(8,128)}, bf16[4,288,1536]{2,1,0:T(8,128)(2,1)}, bf16[4,1152,576]{2,1,0:T(8,128)(2,1)}, f32[4,288,96]{2,1,0:T(8,128)}, f32...) custom-call(bf16[2,384]{1,0:T(2,128)(2,1)} %refs_0_.1, bf16[2,384]{1,0:T(2,128)(2,1)} %refs_1_.1, ...), custom_call_target="tpu_custom_call" | custom-call | bytes 136800000 | tf_op jit(solution)/shard_map/pallas_call | solution.py:1315
  59.8 0.2 all-gather.9.cloned.1.call-start
  60.0 1.6 fusion.4
  61.6 63.7 %shard_map.230 = (f32[288,1536]{1,0:T(8,128)}, bf16[288,1536]{1,0:T(8,128)(2,1)}, f32[16,128]{1,0:T(8,128)}, bf16[4,288,1536]{2,1,0:T(8,128)(2,1)}, bf16[2,2,4,2...) custom-call(f32[1,1536]{1,0:T(1,128)} %bitcast.38, ...), custom_call_target="tpu_custom_call" | custom-call | bytes 270000000 | tf_op jit(solution)/shard_map/pallas_call | solution.py:1315
  125.3 1.0 slice-done.3
  126.4 0.1 copy.32
  126.5 0.1 dynamic-slice_bitcast_fusion
  126.7 0.1 dynamic-slice_bitcast_fusion.2
  126.8 1.1 concatenate.11
  127.9 0.5 all-gather.11.cloned.1.call-update
  128.5 21.3 %all-gather.7.cloned.1.call-done = bf16[3072,1536]{1,0:T(8,128)(2,1)} async-done(((bf16[384,1536]{1,0:T(8,128)(2,1)}), bf16[3072,1536]{1,0:T(8,128)(2,1)}) %all-gather.7.cloned.1.call-update) | async-done | bytes 9437200 | tf_op jit(solution)/shard_map/all_gather | solution.py:1553
  149.8 66.5 %shard_map.231 = (f32[288,1536]{1,0:T(8,128)}, bf16[288,1536]{1,0:T(8,128)(2,1)}, f32[16,128]{1,0:T(8,128)}, bf16[4,288,1536]{2,1,0:T(8,128)(2,1)}, bf16[2,4,288...) custom-call(f32[1,1536]{1,0:T(1,128)} %bitcast.42, f32[288,1]{1,0:T(8,128)} %copy-done, ...), custom_call_target="tpu_custom_call" | custom-call | bytes 270000000 | tf_op jit(solution)/shard_map/pallas_call | solution.py:1315
  216.4 67.3 %shard_map.232 = (f32[288,1536]{1,0:T(8,128)}, bf16[288,1536]{1,0:T(8,128)(2,1)}, f32[16,128]{1,0:T(8,128)}, bf16[4,288,1536]{2,1,0:T(8,128)(2,1)}, bf16[2,2,4,2...) custom-call(f32[1,1536]{1,0:T(1,128)} %bitcast.40, ...), custom_call_target="tpu_custom_call" | custom-call | bytes 270000000 | tf_op jit(solution)/shard_map/pallas_call | solution.py:1315
  283.7 2.6 all-gather.11.cloned.1.call-done
  286.3 68.0 %shard_map.233 = (f32[288,1536]{1,0:T(8,128)}, bf16[288,1536]{1,0:T(8,128)(2,1)}, f32[16,1536]{1,0:T(8,128)}, bf16[1536,1536]{1,0:T(8,128)(2,1)}, bf16[4,288,1536]{2,1,0:T(8,128)(2,1)}) custom-call(f32[1,1536]{1,0:T(1,128)} %bitcast.41, bf16[288,1536]{1,0:T(8,128)(2,1)} %get-tuple-element.107.refs_1_, bf16[2,1536,1536]{2,1,0:T(8,128)(2,1)} %bitcast.35, ...), custom_call_target="tpu_custom_call" | custom-call | bytes 306000000 | tf_op jit(solution)/shard_map/pallas_call | solution.py:1315
  354.4 92.3 %shard_map.234 = (f32[16,1536]{1,0:T(8,128)}, f32[288,1536]{1,0:T(8,128)}, bf16[288,1536]{1,0:T(8,128)(2,1)}, f32[16,128]{1,0:T(8,128)}, bf16[1536,640]{1,0:T(8,128)(2,1)}, /*index=5*/bf16[2,288,1536]{2,1,0:T(8,128)(2,1)}) custom-call(f32[1,1536]{1,0:T(1,128)} %bitcast.43, f32[288,1]{1,0:T(8,128)} %copy-done, bf16[288,1536]{1,0:T(8,128)(2,1)} %get-tuple-element.111.refs_2_, ...), custom_call_target="tpu_custom_call" | custom-call | bytes 360000000 | tf_op jit(solution)/shard_map/pallas_call | solution.py:1315
  446.7 0.2 reduce-scatter.8.cloned.1.call-start
  447.0 83.2 %shard_map.235 = (f32[288,1536]{1,0:T(8,128)}, bf16[288,1536]{1,0:T(8,128)(2,1)}, f32[16,1536]{1,0:T(8,128)}, bf16[1536,1536]{1,0:T(8,128)(2,1)}, bf16[4,192,1536]{2,1,0:T(8,128)(2,1)}) custom-call(f32[1,1536]{1,0:T(1,128)} %bitcast.39, bf16[288,1536]{1,0:T(8,128)(2,1)} %get-tuple-element.123.refs_1_, ...), custom_call_target="tpu_custom_call" | custom-call | bytes 306000000 | tf_op jit(solution)/shard_map/pallas_call | solution.py:1315
  530.3 100.8 %shard_map.236 = (f32[16,1536]{1,0:T(8,128)}, f32[2,288,1536]{2,1,0:T(8,128)}, bf16[1536,640]{1,0:T(8,128)(2,1)}, bf16[4,192,1536]{2,1,0:T(8,128)(2,1)}, bf16[4,384,640]{2,1,0:T(8,128)(2,1)}) custom-call(f32[1,1536]{1,0:T(1,128)} %bitcast.44, bf16[288,1536]{1,0:T(8,128)(2,1)} %get-tuple-element.130.refs_1_, ...), custom_call_target="tpu_custom_call" | custom-call | bytes 360000000 | tf_op jit(solution)/shard_map/pallas_call | solution.py:1315
  631.1 61.5 %shard_map.237 = (bf16[4,192,640]{2,1,0:T(8,128)(2,1)}, bf16[4,192,640]{2,1,0:T(8,128)(2,1)}, f32[8,128]{1,0:T(8,128)}, f32[8,384]{1,0:T(8,128)}, bf16[4,384,1536]{2,1,0:T(8,128)(2,1)}) custom-call(bf16[1536,640]{1,0:T(8,128)(2,1)} %get-tuple-element.138.refs_0_, f32[16,128]{1,0:T(8,128)} %get-tuple-element.139.refs_1_, ...), custom_call_target="tpu_custom_call" | custom-call | bytes 216000000 | tf_op jit(solution)/shard_map/pallas_call | solution.py:1315
  692.6 17.6 %shard_map.238 = (f32[2,384,768]{2,1,0:T(8,128)}, f32[2,384,384]{2,1,0:T(8,128)}, f32[2,384,384]{2,1,0:T(8,128)}, f32[2,768,384]{2,1,0:T(8,128)}, f32[2,384,2048...) custom-call(f32[8,384]{1,0:T(8,128)} %get-tuple-element.148.refs_0_,, ...), custom_call_target="tpu_custom_call" | custom-call | tf_op jit(solution)/shard_map/pallas_call | solution.py:1716
  (40 shorter events, 0.6 us)
Async XLA Ops:
  7.2 2.4 slice-start
  7.2 2.5 slice-start.2
  7.2 54.4 %all-gather.5.cloned.1.call-start = ((), (), s32[]{:S(2)}) async-start(), calls=%async_computation.3 | async-start | bytes 4423680 | tf_op jit(solution)/shard_map/all_gather | solution.py:1553
  9.6 1.5 copy-start.1
  9.6 1.8 copy-start.2
  11.0 138.8 %all-gather.7.cloned.1.call-start = ((), (), s32[]{:S(2)}) async-start(), calls=%async_computation.4 | async-start | bytes 10616832 | tf_op jit(solution)/shard_map/all_gather | solution.py:1553
  11.3 48.5 %copy-start = (f32[288,1]{1,0:T(8,128)}, f32[288,1]{1,0:T(8,128)S(1)}, u32[]{:S(2)}) copy-start(f32[288,1]{1,0:T(8,128)S(1)} %copy.28.refs_1_) | copy-start | bytes 3460
  59.8 156.6 %all-gather.9.cloned.1.call-start = ((), (), s32[]{:S(2)}) async-start(), calls=%async_computation.5 | async-start | bytes 4423680 | tf_op jit(solution)/shard_map/all_gather | solution.py:1553
  125.3 1.1 slice-start.3
  125.3 1.2 slice-start.1
  125.3 1.4 slice-start.4
  125.3 1.4 slice-start.5
  127.9 158.4 %all-gather.11.cloned.1.call-start = ((), (), s32[]{:S(2)}) async-start(), calls=%async_computation.6 | async-start | bytes 10616832 | tf_op jit(solution)/shard_map/all_gather | solution.py:1553
  128.5 318.2 %reduce-scatter.4.cloned.1.call-start = ((), (), s32[]{:S(2)}) async-start(), calls=%async_computation.7 | async-start | bytes 5898240 | tf_op jit(solution)/shard_map/reduce_scatter | solution.py:1608
  354.3 175.9 %reduce-scatter.6.cloned.1.call-start = ((), (), s32[]{:S(2)}) async-start(), calls=%async_computation.8 | async-start | bytes 2457600 | tf_op jit(solution)/shard_map/reduce_scatter | solution.py:1608
  446.7 184.3 %reduce-scatter.8.cloned.1.call-start = ((), (), s32[]{:S(2)}) async-start(), calls=%async_computation.9 | async-start | bytes 5898240 | tf_op jit(solution)/shard_map/reduce_scatter | solution.py:1608
Sparse Core Ops, SparseCore 0:
  11.2 47.5 all-gather.4
  60.3 89.4 all-gather.6
  152.0 43.2 all-gather.8
  196.7 89.5 all-gather.10
  354.4 82.7 reduce-scatter.3
  446.9 38.9 reduce-scatter.5
  530.4 83.3 reduce-scatter.7

commit v7 on v6

--- a/solution.py
+++ b/solution.py
@@ -607,14 +607,14 @@
     peers = [lax.rem(level + step, depth) for step in range(1, depth)]
     mine = pltpu.make_async_copy(r.share, r.gathered.at[me], r.load.at[0])
     mine.start()
-    greet_near(place, sibling(), *[{FSDP: peer} for peer in peers])
     rows = r.share.shape[0]
     half = rows // 2
+    own = pltpu.make_async_copy(r.summed.at[pl.ds(pl.multiple_of(level * rows, rows), rows)], r.own, r.load.at[1])
+    own.start()
+    greet_near(place, sibling(), *[{FSDP: peer} for peer in peers])
     r.gain_rows = [r.gain_rows_0, r.gain_rows_1, r.gain_rows_2, r.gain_rows_3]
     r.attn_stats = [r.attn_stats_0, r.attn_stats_1]
     r.mlp_stats = [r.mlp_stats_0, r.mlp_stats_1]
-    counts = stat_steps(r, place)
-    next(counts)
     copies = []
     for part_no in range(2):
         copies.append([])
@@ -625,8 +625,12 @@
             )
     first = gather_rows(r.gathered, (r.ag_send, r.ag_recv), place, r.share)
     next(first)
+    counts = stat_steps(r, place)
+    r.need(*list(r.loads))
+    next(counts)
     next(counts)
     next(first)
+    own.wait()
     step = 48
     lasts = (r.last_0, r.last_1)
     steps = []
@@ -637,8 +641,8 @@
         @pl.loop(0, half // step)
         def _(i):
             here = pl.ds(pl.multiple_of(i * step, step), step)
-            start = pl.multiple_of(level * rows + part_no * half + i * step, step)
-            total = r.summed[pl.ds(start, step), :].astype(jnp.float32)
+            start = pl.multiple_of(part_no * half + i * step, step)
+            total = r.own[pl.ds(start, step), :].astype(jnp.float32)
             for peer in peers:
                 total += r.z_came[part_no, peer, here, :].astype(jnp.float32)
             lasts[part_no][me, here, :] = total.astype(jnp.bfloat16)
@@ -1481,18 +1485,18 @@
     wide = summed.shape[0] + 128
     return linked(
         functools.partial(tail_kernel, summed.shape[0]), 10, 60,
+        {}, dict(share=share, summed=summed),
         dict(
-            summed=summed,
             **{f"attn_stats_{layer}": a for layer, a in enumerate(attn_stats)},
             **{f"mlp_stats_{layer}": a for layer, a in enumerate(mlp_stats)},
             **{f"gain_rows_{n}": a for n, a in enumerate(gain_rows)},
         ),
-        dict(share=share), {},
         dict(last_0=last, last_1=last, all_stats=shape32(8, 128), gains=shape32(8, summed.shape[0] // depth)), dict(gathered=shape16(4, *share.shape)),
         dict(
             z_came=pltpu.VMEM((2, depth, half, cols), jnp.bfloat16), stat_sent=pltpu.VMEM((4, 8, wide), jnp.float32),
             stat_came=pltpu.VMEM((3, 8, wide), jnp.float32), stat_z=pltpu.VMEM((depth, 8, wide), jnp.float32),
-            load=pltpu.SemaphoreType.DMA((1,)), **sems("z", 2 * depth), **sems("ag", 6), **sems("stat", 3 + depth),
+            own=pltpu.VMEM((share.shape[0], cols), jnp.bfloat16),
+            load=pltpu.SemaphoreType.DMA((2,)), **sems("z", 2 * depth), **sems("ag", 6), **sems("stat", 3 + depth),
             **sems("l0", 6), **sems("l1", 6),
         ),
     )

time: 721 us -> 720 us (level)
  no operation moved by 1% of the time
where the time goes in v7:
time: 720 us; the launch traced here: 715 us
  Pallas kernels  666 us (92%)
  waiting for transfers between devices  24.6 us (3%)
  between operations  14.7 us (2%)
  local copies, waits for them, and re-layouts  8.01 us (1%)
    pallas_call x9, Pallas kernels, linked(): pl.pallas_call(body, out_shape=[*outs.values(), *late.values()], in_specs...  648 us
    all_gather x4, waiting for transfers between devices, whole(): lax.all_gather(w, (TP, FSDP), axis=0, tiled=True)  24 us
    pallas_call x1, Pallas kernels, place_outs(): pl.pallas_call(functools.partial(place_kernel, moves, len(ins), len(hande...  17.6 us
  transfers between devices with their start and end apart: 7, of which 2 were waited for; matrix products, arithmetic and copies ran while one was open for 1% of the time, Pallas kernels for 73%

profile of v7, /device:TPU:0, one launch (start us, length us, event | category | flops | bytes accessed | tf_op | source)
XLA Modules:
  0.0 715.5 jit_solution(479579507922399609)
XLA Ops:
  7.3 1.1 slice.55
  8.3 1.0 slice.56
  9.3 0.1 dynamic-slice_bitcast_fusion.5
  9.4 0.1 dynamic-slice_bitcast_fusion.4
  9.6 0.1 dynamic-slice_bitcast_fusion.1
  9.8 0.1 copy.29
  10.0 1.1 concatenate.10
  11.1 0.1 copy.28.refs_1_
  11.3 0.1 pad.3.clone
  11.4 0.6 multiply_cosine_fusion
  12.0 0.8 maximum_maximum_fusion.refs_2_
  12.8 47.0 %shard_map.229 = (f32[4,8,384]{2,1,0:T(8,128)}, bf16[4,288,1536]{2,1,0:T(8,128)(2,1)}, bf16[4,1152,576]{2,1,0:T(8,128)(2,1)}, f32[4,288,96]{2,1,0:T(8,128)}, f32...) custom-call(bf16[2,384]{1,0:T(2,128)(2,1)} %refs_0_.1, bf16[2,384]{1,0:T(2,128)(2,1)} %refs_1_.1, ...), custom_call_target="tpu_custom_call" | custom-call | bytes 136800000 | tf_op jit(solution)/shard_map/pallas_call | solution.py:1319
  59.8 0.2 all-gather.9.cloned.1.call-start
  60.0 1.6 fusion.4
  61.6 63.7 %shard_map.230 = (f32[288,1536]{1,0:T(8,128)}, bf16[288,1536]{1,0:T(8,128)(2,1)}, f32[16,128]{1,0:T(8,128)}, bf16[4,288,1536]{2,1,0:T(8,128)(2,1)}, bf16[2,2,4,2...) custom-call(f32[1,1536]{1,0:T(1,128)} %bitcast.38, ...), custom_call_target="tpu_custom_call" | custom-call | bytes 270000000 | tf_op jit(solution)/shard_map/pallas_call | solution.py:1319
  125.3 1.0 slice-done.3
  126.4 0.1 copy.32
  126.5 0.1 dynamic-slice_bitcast_fusion
  126.7 0.1 dynamic-slice_bitcast_fusion.2
  126.8 1.1 concatenate.11
  127.9 0.5 all-gather.11.cloned.1.call-update
  128.5 21.3 %all-gather.7.cloned.1.call-done = bf16[3072,1536]{1,0:T(8,128)(2,1)} async-done(((bf16[384,1536]{1,0:T(8,128)(2,1)}), bf16[3072,1536]{1,0:T(8,128)(2,1)}) %all-gather.7.cloned.1.call-update) | async-done | bytes 9437200 | tf_op jit(solution)/shard_map/all_gather | solution.py:1557
  149.8 66.5 %shard_map.231 = (f32[288,1536]{1,0:T(8,128)}, bf16[288,1536]{1,0:T(8,128)(2,1)}, f32[16,128]{1,0:T(8,128)}, bf16[4,288,1536]{2,1,0:T(8,128)(2,1)}, bf16[2,4,288...) custom-call(f32[1,1536]{1,0:T(1,128)} %bitcast.42, f32[288,1]{1,0:T(8,128)} %copy-done, ...), custom_call_target="tpu_custom_call" | custom-call | bytes 270000000 | tf_op jit(solution)/shard_map/pallas_call | solution.py:1319
  216.4 67.3 %shard_map.232 = (f32[288,1536]{1,0:T(8,128)}, bf16[288,1536]{1,0:T(8,128)(2,1)}, f32[16,128]{1,0:T(8,128)}, bf16[4,288,1536]{2,1,0:T(8,128)(2,1)}, bf16[2,2,4,2...) custom-call(f32[1,1536]{1,0:T(1,128)} %bitcast.40, ...), custom_call_target="tpu_custom_call" | custom-call | bytes 270000000 | tf_op jit(solution)/shard_map/pallas_call | solution.py:1319
  283.7 2.6 all-gather.11.cloned.1.call-done
  286.3 68.0 %shard_map.233 = (f32[288,1536]{1,0:T(8,128)}, bf16[288,1536]{1,0:T(8,128)(2,1)}, f32[16,1536]{1,0:T(8,128)}, bf16[1536,1536]{1,0:T(8,128)(2,1)}, bf16[4,288,1536]{2,1,0:T(8,128)(2,1)}) custom-call(f32[1,1536]{1,0:T(1,128)} %bitcast.41, bf16[288,1536]{1,0:T(8,128)(2,1)} %get-tuple-element.107.refs_1_, bf16[2,1536,1536]{2,1,0:T(8,128)(2,1)} %bitcast.35, ...), custom_call_target="tpu_custom_call" | custom-call | bytes 306000000 | tf_op jit(solution)/shard_map/pallas_call | solution.py:1319
  354.4 92.3 %shard_map.234 = (f32[16,1536]{1,0:T(8,128)}, f32[288,1536]{1,0:T(8,128)}, bf16[288,1536]{1,0:T(8,128)(2,1)}, f32[16,128]{1,0:T(8,128)}, bf16[1536,640]{1,0:T(8,128)(2,1)}, /*index=5*/bf16[2,288,1536]{2,1,0:T(8,128)(2,1)}) custom-call(f32[1,1536]{1,0:T(1,128)} %bitcast.43, f32[288,1]{1,0:T(8,128)} %copy-done, bf16[288,1536]{1,0:T(8,128)(2,1)} %get-tuple-element.111.refs_2_, ...), custom_call_target="tpu_custom_call" | custom-call | bytes 360000000 | tf_op jit(solution)/shard_map/pallas_call | solution.py:1319
  446.7 0.2 reduce-scatter.6.cloned.1.call-start
  447.0 83.2 %shard_map.235 = (f32[288,1536]{1,0:T(8,128)}, bf16[288,1536]{1,0:T(8,128)(2,1)}, f32[16,1536]{1,0:T(8,128)}, bf16[1536,1536]{1,0:T(8,128)(2,1)}, bf16[4,192,1536]{2,1,0:T(8,128)(2,1)}) custom-call(f32[1,1536]{1,0:T(1,128)} %bitcast.39, bf16[288,1536]{1,0:T(8,128)(2,1)} %get-tuple-element.123.refs_1_, ...), custom_call_target="tpu_custom_call" | custom-call | bytes 306000000 | tf_op jit(solution)/shard_map/pallas_call | solution.py:1319
  530.3 100.8 %shard_map.236 = (f32[16,1536]{1,0:T(8,128)}, f32[2,288,1536]{2,1,0:T(8,128)}, bf16[1536,640]{1,0:T(8,128)(2,1)}, bf16[4,192,1536]{2,1,0:T(8,128)(2,1)}, bf16[4,384,640]{2,1,0:T(8,128)(2,1)}) custom-call(f32[1,1536]{1,0:T(1,128)} %bitcast.44, bf16[288,1536]{1,0:T(8,128)(2,1)} %get-tuple-element.131.refs_1_, ...), custom_call_target="tpu_custom_call" | custom-call | bytes 360000000 | tf_op jit(solution)/shard_map/pallas_call | solution.py:1319
  631.1 59.7 %shard_map.237 = (bf16[4,192,640]{2,1,0:T(8,128)(2,1)}, bf16[4,192,640]{2,1,0:T(8,128)(2,1)}, f32[8,128]{1,0:T(8,128)}, f32[8,384]{1,0:T(8,128)}, bf16[4,384,1536]{2,1,0:T(8,128)(2,1)}) custom-call(bf16[384,1536]{1,0:T(8,128)(2,1)} %reduce-scatter.6.cloned.1.call-done.refs_0_, bf16[1536,640]{1,0:T(8,128)(2,1)} %get-tuple-element.139.refs_1_, ...), custom_call_target="tpu_custom_call" | custom-call | bytes 216000000 | tf_op jit(solution)/shard_map/pallas_call | solution.py:1319
  690.8 17.6 %shard_map.238 = (f32[2,384,768]{2,1,0:T(8,128)}, f32[2,384,384]{2,1,0:T(8,128)}, f32[2,384,384]{2,1,0:T(8,128)}, f32[2,768,384]{2,1,0:T(8,128)}, f32[2,384,2048...) custom-call(f32[8,384]{1,0:T(8,128)} %get-tuple-element.148.refs_0_,, ...), custom_call_target="tpu_custom_call" | custom-call | tf_op jit(solution)/shard_map/pallas_call | solution.py:1720
  (40 shorter events, 0.6 us)
Async XLA Ops:
  7.2 2.4 slice-start
  7.2 2.5 slice-start.2
  7.2 54.4 %all-gather.5.cloned.1.call-start = ((), (), s32[]{:S(2)}) async-start(), calls=%async_computation.3 | async-start | bytes 4423680 | tf_op jit(solution)/shard_map/all_gather | solution.py:1557
  9.6 1.5 copy-start.1
  9.6 1.8 copy-start.2
  11.0 138.8 %all-gather.7.cloned.1.call-start = ((), (), s32[]{:S(2)}) async-start(), calls=%async_computation.4 | async-start | bytes 10616832 | tf_op jit(solution)/shard_map/all_gather | solution.py:1557
  11.3 48.5 %copy-start = (f32[288,1]{1,0:T(8,128)}, f32[288,1]{1,0:T(8,128)S(1)}, u32[]{:S(2)}) copy-start(f32[288,1]{1,0:T(8,128)S(1)} %copy.28.refs_1_) | copy-start | bytes 3460
  59.8 156.6 %all-gather.9.cloned.1.call-start = ((), (), s32[]{:S(2)}) async-start(), calls=%async_computation.5 | async-start | bytes 4423680 | tf_op jit(solution)/shard_map/all_gather | solution.py:1557
  125.3 1.1 slice-start.3
  125.3 1.2 slice-start.1
  125.3 1.4 slice-start.4
  125.3 1.4 slice-start.5
  127.9 158.4 %all-gather.11.cloned.1.call-start = ((), (), s32[]{:S(2)}) async-start(), calls=%async_computation.6 | async-start | bytes 10616832 | tf_op jit(solution)/shard_map/all_gather | solution.py:1557
  128.5 318.2 %reduce-scatter.4.cloned.1.call-start = ((), (), s32[]{:S(2)}) async-start(), calls=%async_computation.7 | async-start | bytes 5898240 | tf_op jit(solution)/shard_map/reduce_scatter | solution.py:1612
  354.3 175.9 %reduce-scatter.8.cloned.1.call-start = ((), (), s32[]{:S(2)}) async-start(), calls=%async_computation.9 | async-start | bytes 2457600 | tf_op jit(solution)/shard_map/reduce_scatter | solution.py:1612
  446.7 184.3 %reduce-scatter.6.cloned.1.call-start = ((), (), s32[]{:S(2)}) async-start(), calls=%async_computation.8 | async-start | bytes 5898240 | tf_op jit(solution)/shard_map/reduce_scatter | solution.py:1612
Sparse Core Ops, SparseCore 0:
  11.2 47.5 all-gather.4
  60.3 89.4 all-gather.6
  152.0 43.2 all-gather.8
  196.7 89.5 all-gather.10
  354.4 82.7 reduce-scatter.3
  446.9 38.9 reduce-scatter.7
  530.4 83.3 reduce-scatter.5
